TPU v7x, 256 devices: a whole 4x4x8 slice. The times are simulated.
256 devices in a mesh: tm: 32 (over y, x, core), slab: 8 (over z).
Axes of the slice: x: 4, y: 4, z: 8, core: 2. Of those that a mesh axis runs over, the one named last changes fastest.
Arguments:
- precision_blocks: bfloat16 [64, 1024, 1024], P('tm', None, 'slab'), may hold values from -0.2 to 0.2, as said below
- coupling: bfloat16 [64, 1024, 1024], P('tm'), may hold values from -0.03125 to 1.03125
Outputs:
- variance_blocks: bfloat16 [64, 1024, 1024], P('tm', None, 'slab')
Inputs may be any that keep to these rules, and one draw needn't show every extreme that they name: `precision_blocks`: each block is symmetric positive definite.
All inputs are finite; a program needn't handle non-finite values.
Results may differ from a plain program's by a relative error of at most 0.0065.
The roundings to bfloat16 on the way count: a program that leaves them out, or rounds other values in their place, can miss the bound.
Values may be sent and summed in bfloat16 or wider, within the bound.
No kernel may reach another device: no remote copies, remote signals or barrier semaphores. Data moves between devices by JAX's collectives and lax.ppermute only.
A program may use at most 64 MiB of HBM per device.

v0:
```python
import jax
import jax.numpy as jnp
from jax import lax
from jax.sharding import PartitionSpec as P


def passed_along(block, axis, distance):
    devices = range(lax.axis_size(axis))
    route = [(i - distance, i) for i in devices if i - distance in devices]
    return lax.ppermute(block, axis, route)


def left_transposed(left, right):
    return lax.dot_general(
        left, right, (((0,), (0,)), ((), ())), preferred_element_type=jnp.float32
    )


def fold_with(right_cols, piece):
    return jnp.dot(piece, right_cols, preferred_element_type=jnp.float32)


def shards(precision_blocks, coupling):
    part_cols = precision_blocks.shape[2]
    first_col = lax.axis_index("slab") * part_cols
    first_p = precision_blocks[0]
    second_p = precision_blocks[1]
    first_k = coupling[0]
    second_k = coupling[1]

    def own_cols(full):
        return lax.dynamic_slice_in_dim(full, first_col, part_cols, 1)

    mixed = fold_with(
        own_cols(first_k), lax.all_gather(second_p, "slab", axis=1, tiled=True)
    ).astype(jnp.bfloat16)
    reduced = (first_p.astype(jnp.float32) + left_transposed(first_k, mixed)).astype(jnp.bfloat16)
    carried = jnp.dot(second_k, first_k, preferred_element_type=jnp.float32).astype(jnp.bfloat16)
    level_count = lax.axis_size("tm").bit_length() - 1
    for depth_index in range(level_count):
        distance = 1 << depth_index
        sent = carried
        if depth_index + 1 < level_count:
            far_reduced, far_sent = passed_along((reduced, sent), "tm", -distance)
        else:
            far_reduced = passed_along(reduced, "tm", -distance)
        carried_cols = own_cols(carried)
        bridge = fold_with(
            carried_cols, lax.all_gather(far_reduced, "slab", axis=1, tiled=True)
        ).astype(jnp.bfloat16)
        new_reduced = (reduced.astype(jnp.float32) + left_transposed(carried, bridge)).astype(
            jnp.bfloat16
        )
        if depth_index + 1 < level_count:
            slab_piece = jnp.dot(far_sent, carried_cols, preferred_element_type=jnp.float32).astype(
                jnp.bfloat16
            )
            carried = lax.all_gather(slab_piece, "slab", axis=1, tiled=True)
        reduced = new_reduced
    next_reduced = passed_along(reduced, "tm", -1)
    weighed = fold_with(
        own_cols(second_k), lax.all_gather(next_reduced, "slab", axis=1, tiled=True)
    ).astype(jnp.bfloat16)
    second_sigma = (second_p.astype(jnp.float32) + left_transposed(second_k, weighed)).astype(
        jnp.bfloat16
    )
    return jnp.stack([reduced, second_sigma], axis=0)


def solution(mesh):
    return jax.shard_map(
        shards,
        mesh=mesh,
        in_specs=(P("tm", None, "slab"), P("tm", None, None)),
        out_specs=P("tm", None, "slab"),
        check_vma=False,
    )
```

profile of v0, /device:TPU:1, one launch (start us, length us, event | category | flops | bytes accessed | tf_op | source)
XLA Modules:
  0.0 537.5 jit_solution(4612044563072169827)
XLA Ops:
  6.5 1.1 fusion.88
  7.6 0.9 copy.17
  8.7 4.0 fusion.87
  12.7 37.7 %all-gather.33.cloned.1.call-done = bf16[1,1024,1024]{1,2,0:T(8,128)(2,1)} async-done(((bf16[1,1024,128]{1,2,0:T(8,128)(2,1)}), bf16[1,1024,1024]{1,2,0:T(8,128)(2,1)}) %all-gather.33.cloned.1.call-update) | async-done | bytes 2097168 | tf_op jit(solution)/shard_map/all_gather | solution.py:35
  50.4 3.1 fusion.34
  53.5 6.3 %collective-permute-start = (bf16[1024,128]{0,1:T(8,128)(2,1)S(1)}, bf16[1024,128]{0,1:T(8,128)(2,1)S(1)}, u32[]{:S(2)}, u32[]{:S(2)}) collective-permute-start(bf16[1024,128]{0,1:T(8,128)(2,1)S(1)} %fusion.34), channel_id=1, source_target_pairs={{8,0},{16,8},{24,16},{32,24},{40,32},{48,40},{56,48},{64,56},{72,6... | collective-permute-start | bytes 786440 | tf_op jit(solution)/shard_map/ppermute | solution.py:10
  59.8 5.1 collective-permute-done
  64.9 0.7 copy-done.4
  65.7 4.6 fusion.9
  70.3 1.9 collective-permute-start.1
  72.2 25.8 %collective-permute-done.1 = bf16[1024,1024]{1,0:T(8,128)(2,1)S(1)} collective-permute-done((bf16[1024,1024]{1,0:T(8,128)(2,1)S(1)}, bf16[1024,1024]{1,0:T(8,128)(2,1)S(1)}, u32[]{:S(2)}, u32[]{:S(2)}) %collective-permute-start.1) | collective-permute-done | bytes 2097184 | tf_op jit(solution)/shard_map/ppermute | solution.py:10
  98.0 1.4 convolution_convert_fusion.8
  99.5 1.4 all-gather.13.cloned.1.call-done
  101.0 3.7 fusion.29
  104.7 1.3 collective-permute-start.2
  106.0 5.8 %collective-permute-done.2 = bf16[1024,128]{0,1:T(8,128)(2,1)S(1)} collective-permute-done((bf16[1024,128]{0,1:T(8,128)(2,1)S(1)}, bf16[1024,128]{0,1:T(8,128)(2,1)S(1)}, u32[]{:S(2)}, u32[]{:S(2)}) %collective-permute-start.2) | collective-permute-done | bytes 262176 | tf_op jit(solution)/shard_map/ppermute | solution.py:10
  111.8 0.7 copy-done.1
  112.6 35.9 %all-gather.15.cloned.1.call-done = bf16[1024,1024]{1,0:T(8,128)(2,1)} async-done(((bf16[1024,128]{1,0:T(8,128)(2,1)}), bf16[1024,1024]{1,0:T(8,128)(2,1)}) %all-gather.15.cloned.1.call-update) | async-done | bytes 2097168 | tf_op jit(solution)/shard_map/all_gather | solution.py:58
  148.5 1.3 collective-permute-start.3
  149.8 43.1 %collective-permute-done.3 = bf16[1024,1024]{1,0:T(8,128)(2,1)S(1)} collective-permute-done((bf16[1024,1024]{1,0:T(8,128)(2,1)}, bf16[1024,1024]{1,0:T(8,128)(2,1)S(1)}, u32[]{:S(2)}, u32[]{:S(2)}) %collective-permute-start.3) | collective-permute-done | bytes 2097184 | tf_op jit(solution)/shard_map/ppermute | solution.py:10
  192.9 2.4 convolution_convert_fusion.6
  195.3 3.7 fusion.30
  199.0 1.3 collective-permute-start.4
  200.3 7.7 %collective-permute-done.4 = bf16[1024,128]{0,1:T(8,128)(2,1)S(1)} collective-permute-done((bf16[1024,128]{0,1:T(8,128)(2,1)S(1)}, bf16[1024,128]{0,1:T(8,128)(2,1)S(1)}, u32[]{:S(2)}, u32[]{:S(2)}) %collective-permute-start.4) | collective-permute-done | bytes 262176 | tf_op jit(solution)/shard_map/ppermute | solution.py:10
  208.1 0.7 copy-done.2
  208.8 35.2 %all-gather.19.cloned.1.call-done = bf16[1024,1024]{1,0:T(8,128)(2,1)} async-done(((bf16[1024,128]{1,0:T(8,128)(2,1)}), bf16[1024,1024]{1,0:T(8,128)(2,1)}) %all-gather.19.cloned.1.call-update) | async-done | bytes 2097168 | tf_op jit(solution)/shard_map/all_gather | solution.py:58
  244.0 1.3 collective-permute-start.5
  245.3 44.5 %collective-permute-done.5 = bf16[1024,1024]{1,0:T(8,128)(2,1)S(1)} collective-permute-done((bf16[1024,1024]{1,0:T(8,128)(2,1)}, bf16[1024,1024]{1,0:T(8,128)(2,1)S(1)}, u32[]{:S(2)}, u32[]{:S(2)}) %collective-permute-start.5) | collective-permute-done | bytes 2097184 | tf_op jit(solution)/shard_map/ppermute | solution.py:10
  289.8 2.4 convolution_convert_fusion.4
  292.2 3.7 fusion.31
  295.9 1.3 collective-permute-start.6
  297.2 6.2 %collective-permute-done.6 = bf16[1024,128]{0,1:T(8,128)(2,1)S(1)} collective-permute-done((bf16[1024,128]{0,1:T(8,128)(2,1)S(1)}, bf16[1024,128]{0,1:T(8,128)(2,1)S(1)}, u32[]{:S(2)}, u32[]{:S(2)}) %collective-permute-start.6) | collective-permute-done | bytes 262176 | tf_op jit(solution)/shard_map/ppermute | solution.py:10
  304.2 35.8 %all-gather.23.cloned.1.call-done = bf16[1024,1024]{1,0:T(8,128)(2,1)} async-done(((bf16[1024,128]{1,0:T(8,128)(2,1)}), bf16[1024,1024]{1,0:T(8,128)(2,1)}) %all-gather.23.cloned.1.call-update) | async-done | bytes 2097168 | tf_op jit(solution)/shard_map/all_gather | solution.py:58
  340.1 1.3 collective-permute-start.7
  341.3 43.1 %collective-permute-done.7 = bf16[1024,1024]{1,0:T(8,128)(2,1)S(1)} collective-permute-done((bf16[1024,1024]{1,0:T(8,128)(2,1)}, bf16[1024,1024]{1,0:T(8,128)(2,1)S(1)}, u32[]{:S(2)}, u32[]{:S(2)}) %collective-permute-start.7) | collective-permute-done | bytes 2097184 | tf_op jit(solution)/shard_map/ppermute | solution.py:10
  384.4 2.4 convolution_convert_fusion.2
  387.1 3.7 fusion.32
  390.8 1.3 collective-permute-start.8
  392.1 7.3 %collective-permute-done.8 = bf16[1024,128]{0,1:T(8,128)(2,1)S(1)} collective-permute-done((bf16[1024,128]{0,1:T(8,128)(2,1)S(1)}, bf16[1024,128]{0,1:T(8,128)(2,1)S(1)}, u32[]{:S(2)}, u32[]{:S(2)}) %collective-permute-start.8) | collective-permute-done | bytes 262176 | tf_op jit(solution)/shard_map/ppermute | solution.py:10
  399.4 0.7 copy-done.5
  400.2 33.5 %all-gather.27.cloned.1.call-done = bf16[1024,1024]{1,0:T(8,128)(2,1)} async-done(((bf16[1024,128]{1,0:T(8,128)(2,1)}), bf16[1024,1024]{1,0:T(8,128)(2,1)}) %all-gather.27.cloned.1.call-update) | async-done | bytes 2097168 | tf_op jit(solution)/shard_map/all_gather | solution.py:58
  433.7 42.0 %all-gather.29.cloned.1.call-done = bf16[1024,1024]{0,1:T(8,128)(2,1)} async-done(((bf16[1024,128]{0,1:T(8,128)(2,1)}), bf16[1024,1024]{0,1:T(8,128)(2,1)}) %all-gather.29.cloned.1.call-update) | async-done | bytes 2097168 | tf_op jit(solution)/shard_map/all_gather | solution.py:49
  475.7 3.7 fusion.33
  479.4 6.3 %collective-permute-start.9 = (bf16[1024,128]{0,1:T(8,128)(2,1)S(1)}, bf16[1024,128]{0,1:T(8,128)(2,1)S(1)}, u32[]{:S(2)}, u32[]{:S(2)}) collective-permute-start(bf16[1024,128]{0,1:T(8,128)(2,1)S(1)} %fusion.33), channel_id=1, source_target_pairs={{8,0},{16,8},{24,16},{32,24},{40,32},{48,40},{56,48},{64,56},{72,6... | collective-permute-start | bytes 786440 | tf_op jit(solution)/shard_map/ppermute | solution.py:10
  485.7 5.1 collective-permute-done.9
  491.6 35.3 %all-gather.31.cloned.1.call-done = bf16[1024,1024]{0,1:T(8,128)(2,1)} async-done(((bf16[1024,128]{0,1:T(8,128)(2,1)}), bf16[1024,1024]{0,1:T(8,128)(2,1)}) %all-gather.31.cloned.1.call-update) | async-done | bytes 2097168 | tf_op jit(solution)/shard_map/all_gather | solution.py:62
  526.8 3.1 fusion.40
  530.0 1.0 copy.10
  (39 shorter events, 2.4 us)
Async XLA Ops:
  6.5 43.8 %all-gather.33.cloned.1.call-start = ((), (), s32[]{:S(2)}) async-start(), calls=%async_computation.10 | async-start | bytes 2359296 | tf_op jit(solution)/shard_map/all_gather | solution.py:35
  8.5 92.5 %all-gather.13.cloned.1.call-start = ((), (), s32[]{:S(2)}) async-start(), calls=%async_computation | async-start | bytes 2359296 | tf_op jit(solution)/shard_map/all_gather | solution.py:49
  53.5 11.4 %collective-permute-start = (bf16[1024,128]{0,1:T(8,128)(2,1)S(1)}, bf16[1024,128]{0,1:T(8,128)(2,1)S(1)}, u32[]{:S(2)}, u32[]{:S(2)}) collective-permute-start(bf16[1024,128]{0,1:T(8,128)(2,1)S(1)} %fusion.34), channel_id=1, source_target_pairs={{8,0},{16,8},{24,16},{32,24},{40,32},{48,40},{56,48},{64,56},{72,6... | collective-permute-start | bytes 786440 | tf_op jit(solution)/shard_map/ppermute | solution.py:10
  64.9 0.7 copy-start.4
  65.7 82.8 %all-gather.15.cloned.1.call-start = ((), (), s32[]{:S(2)}) async-start(), calls=%async_computation.1 | async-start | bytes 2359296 | tf_op jit(solution)/shard_map/all_gather | solution.py:58
  70.3 27.8 %copy-start.7 = (bf16[1024,1024]{1,0:T(8,128)(2,1)}, bf16[1024,1024]{1,0:T(8,128)(2,1)S(1)}, u32[]{:S(2)}) copy-start(bf16[1024,1024]{1,0:T(8,128)(2,1)S(1)} %fusion.9) | copy-start | bytes 6291460
  70.3 27.8 %collective-permute-start.1 = (bf16[1024,1024]{1,0:T(8,128)(2,1)S(1)}, bf16[1024,1024]{1,0:T(8,128)(2,1)S(1)}, u32[]{:S(2)}, u32[]{:S(2)}) collective-permute-start(bf16[1024,1024]{1,0:T(8,128)(2,1)S(1)} %fusion.9), channel_id=1, source_target_pairs={{8,0},{16,8},{24,16},{32,24},{40,32},{48,40},{56,48},{64,56},{72,6... | collective-permute-start | bytes 6291464 | tf_op jit(solution)/shard_map/ppermute | solution.py:10
  99.5 95.8 %all-gather.17.cloned.1.call-start = ((), (), s32[]{:S(2)}) async-start(), calls=%async_computation.2 | async-start | bytes 2359296 | tf_op jit(solution)/shard_map/all_gather | solution.py:49
  104.7 7.1 %collective-permute-start.2 = (bf16[1024,128]{0,1:T(8,128)(2,1)S(1)}, bf16[1024,128]{0,1:T(8,128)(2,1)S(1)}, u32[]{:S(2)}, u32[]{:S(2)}) collective-permute-start(bf16[1024,128]{0,1:T(8,128)(2,1)S(1)} %fusion.29), channel_id=1, source_target_pairs={{16,0},{24,8},{32,16},{40,24},{48,32},{56,40},{64,48},{72,56},{80,... | collective-permute-start | bytes 786440 | tf_op jit(solution)/shard_map/ppermute | solution.py:10
  111.8 0.7 copy-start.1
  112.5 131.5 %all-gather.19.cloned.1.call-start = ((), (), s32[]{:S(2)}) async-start(), calls=%async_computation.3 | async-start | bytes 2359296 | tf_op jit(solution)/shard_map/all_gather | solution.py:58
  148.5 44.4 %collective-permute-start.3 = (bf16[1024,1024]{1,0:T(8,128)(2,1)}, bf16[1024,1024]{1,0:T(8,128)(2,1)S(1)}, u32[]{:S(2)}, u32[]{:S(2)}) collective-permute-start(bf16[1024,1024]{1,0:T(8,128)(2,1)} %all-gather.15.cloned.1.call-done), channel_id=1, source_target_pairs={{16,0},{24,8},{32,16},{40,24},{48,32},{56,40},{64,48},{72,56},{80,... | collective-permute-start | bytes 6291464 | tf_op jit(solution)/shard_map/ppermute | solution.py:10
  195.3 97.0 %all-gather.21.cloned.1.call-start = ((), (), s32[]{:S(2)}) async-start(), calls=%async_computation.4 | async-start | bytes 2359296 | tf_op jit(solution)/shard_map/all_gather | solution.py:49
  199.0 9.0 %collective-permute-start.4 = (bf16[1024,128]{0,1:T(8,128)(2,1)S(1)}, bf16[1024,128]{0,1:T(8,128)(2,1)S(1)}, u32[]{:S(2)}, u32[]{:S(2)}) collective-permute-start(bf16[1024,128]{0,1:T(8,128)(2,1)S(1)} %fusion.30), channel_id=1, source_target_pairs={{32,0},{40,8},{48,16},{56,24},{64,32},{72,40},{80,48},{88,56},{96,... | collective-permute-start | bytes 786440 | tf_op jit(solution)/shard_map/ppermute | solution.py:10
  208.1 0.7 copy-start.2
  208.8 131.3 %all-gather.23.cloned.1.call-start = ((), (), s32[]{:S(2)}) async-start(), calls=%async_computation.5 | async-start | bytes 2359296 | tf_op jit(solution)/shard_map/all_gather | solution.py:58
  244.0 45.8 %collective-permute-start.5 = (bf16[1024,1024]{1,0:T(8,128)(2,1)}, bf16[1024,1024]{1,0:T(8,128)(2,1)S(1)}, u32[]{:S(2)}, u32[]{:S(2)}) collective-permute-start(bf16[1024,1024]{1,0:T(8,128)(2,1)} %all-gather.19.cloned.1.call-done), channel_id=1, source_target_pairs={{32,0},{40,8},{48,16},{56,24},{64,32},{72,40},{80,48},{88,56},{96,... | collective-permute-start | bytes 6291464 | tf_op jit(solution)/shard_map/ppermute | solution.py:10
  292.1 94.9 %all-gather.25.cloned.1.call-start = ((), (), s32[]{:S(2)}) async-start(), calls=%async_computation.6 | async-start | bytes 2359296 | tf_op jit(solution)/shard_map/all_gather | solution.py:49
  295.9 7.5 %collective-permute-start.6 = (bf16[1024,128]{0,1:T(8,128)(2,1)S(1)}, bf16[1024,128]{0,1:T(8,128)(2,1)S(1)}, u32[]{:S(2)}, u32[]{:S(2)}) collective-permute-start(bf16[1024,128]{0,1:T(8,128)(2,1)S(1)} %fusion.31), channel_id=1, source_target_pairs={{64,0},{72,8},{80,16},{88,24},{96,32},{104,40},{112,48},{120,56},{... | collective-permute-start | bytes 786440 | tf_op jit(solution)/shard_map/ppermute | solution.py:10
  303.4 0.7 copy-start.3
  304.2 129.5 %all-gather.27.cloned.1.call-start = ((), (), s32[]{:S(2)}) async-start(), calls=%async_computation.7 | async-start | bytes 2359296 | tf_op jit(solution)/shard_map/all_gather | solution.py:58
  340.1 44.4 %collective-permute-start.7 = (bf16[1024,1024]{1,0:T(8,128)(2,1)}, bf16[1024,1024]{1,0:T(8,128)(2,1)S(1)}, u32[]{:S(2)}, u32[]{:S(2)}) collective-permute-start(bf16[1024,1024]{1,0:T(8,128)(2,1)} %all-gather.23.cloned.1.call-done), channel_id=1, source_target_pairs={{64,0},{72,8},{80,16},{88,24},{96,32},{104,40},{112,48},{120,56},{... | collective-permute-start | bytes 6291464 | tf_op jit(solution)/shard_map/ppermute | solution.py:10
  386.8 88.9 %all-gather.29.cloned.1.call-start = ((), (), s32[]{:S(2)}) async-start(), calls=%async_computation.8 | async-start | bytes 2359296 | tf_op jit(solution)/shard_map/all_gather | solution.py:49
  390.8 8.6 %collective-permute-start.8 = (bf16[1024,128]{0,1:T(8,128)(2,1)S(1)}, bf16[1024,128]{0,1:T(8,128)(2,1)S(1)}, u32[]{:S(2)}, u32[]{:S(2)}) collective-permute-start(bf16[1024,128]{0,1:T(8,128)(2,1)S(1)} %fusion.32), channel_id=1, source_target_pairs={{128,0},{136,8},{144,16},{152,24},{160,32},{168,40},{176,48},{184,... | collective-permute-start | bytes 786440 | tf_op jit(solution)/shard_map/ppermute | solution.py:10
  399.4 0.7 copy-start.5
  400.1 126.7 %copy-start = (bf16[1,1024,128]{1,2,0:T(8,128)(2,1)S(1)}, bf16[1,1024,128]{1,2,0:T(8,128)(2,1)}, u32[]{:S(2)}) copy-start(bf16[1,1024,128]{1,2,0:T(8,128)(2,1)} %copy.17) | copy-start | bytes 786436
  400.2 126.7 %all-gather.31.cloned.1.call-start = ((), (), s32[]{:S(2)}) async-start(), calls=%async_computation.9 | async-start | bytes 2359296 | tf_op jit(solution)/shard_map/all_gather | solution.py:62
  479.4 11.4 %collective-permute-start.9 = (bf16[1024,128]{0,1:T(8,128)(2,1)S(1)}, bf16[1024,128]{0,1:T(8,128)(2,1)S(1)}, u32[]{:S(2)}, u32[]{:S(2)}) collective-permute-start(bf16[1024,128]{0,1:T(8,128)(2,1)S(1)} %fusion.33), channel_id=1, source_target_pairs={{8,0},{16,8},{24,16},{32,24},{40,32},{48,40},{56,48},{64,56},{72,6... | collective-permute-start | bytes 786440 | tf_op jit(solution)/shard_map/ppermute | solution.py:10
  490.8 0.7 copy-start.6
Sparse Core Ops, SparseCore 0:
  9.1 41.1 all-gather.32
  65.8 35.1 all-gather.12
  102.7 45.7 all-gather.14
  150.2 40.2 all-gather.16
  195.4 48.5 all-gather.18
  245.6 40.2 all-gather.20
  292.3 47.7 all-gather.22
  341.8 40.2 all-gather.24
  386.9 46.7 all-gather.26
  435.4 40.2 all-gather.28
  491.7 35.1 all-gather.30
where the time goes:
time: 541 us; the launch traced here: 538 us
  waiting for transfers between devices  451 us (83%)
  matrix products  37.8 us (7%)
  starting transfers between devices  24.1 us (4%)
  between operations  13.4 us (2%)
  local copies, waits for them, and re-layouts  11.3 us (2%)
    ppermute x10, waiting for transfers between devices, passed_along(): return lax.ppermute(block, axis, route)  194 us
    all_gather x4, waiting for transfers between devices, shards(): carried = lax.all_gather(slab_piece, 'slab', axis=1, tiled=True)  140 us
    all_gather x5, waiting for transfers between devices, shards(): lax.all_gather(far_reduced, 'slab', axis=1, tiled=True)  43.5 us
    all_gather x1, waiting for transfers between devices, shards(): lax.all_gather(second_p, 'slab', axis=1, tiled=True)  37.7 us
    all_gather x1, waiting for transfers between devices, shards(): lax.all_gather(next_reduced, 'slab', axis=1, tiled=True)  35.3 us
    dot_general x7, matrix products, left_transposed(): lax.dot_general(left, right, (((0,), (0,)), ((), ())), preferred_element_...  24.8 us
    ppermute x10, starting transfers between devices, passed_along(): return lax.ppermute(block, axis, route)  23.5 us
  transfers between devices with their start and end apart: 21, of which 18 were waited for; matrix products, arithmetic and copies ran while one was open for 6% of the time, Pallas kernels for 0%

commit v1 on v0

v1 whole, which is shorter than its diff:
```python
import jax
import jax.numpy as jnp
from jax import lax
from jax.sharding import Mesh, PartitionSpec as P

BF16 = jnp.bfloat16
F32 = jnp.float32
CHIPS = ("y", "x")


def dot(left, right):
    return jnp.dot(left, right, preferred_element_type=F32)


def from_later(block, distance):
    chips = lax.axis_size(CHIPS)
    return lax.ppermute(block, CHIPS, [(i + distance, i) for i in range(chips - distance)])


def from_other_core(block):
    return lax.ppermute(block, "core", [(0, 1), (1, 0)])


def turned(rows):
    slabs = lax.axis_size("z")
    m, n = rows.shape
    width = n // slabs
    pieces = rows.reshape(m, slabs, width).swapaxes(0, 1)
    return lax.all_to_all(pieces, "z", 0, 0, tiled=True)


def shards(precision_blocks, coupling):
    core = lax.axis_index("core")
    slab = lax.axis_index("z")
    width = precision_blocks.shape[2]
    half = width // 2
    order = precision_blocks.shape[1]
    first_k, second_k = coupling[0], coupling[1]
    rows = precision_blocks.swapaxes(1, 2)
    first_p, second_p = rows[0], rows[1]

    def side(a, b):
        return jnp.where(core == 0, a, b)

    own = dot(second_k, first_k).astype(BF16)
    other = from_other_core(own)
    c_low, c_high = side(own, other), side(other, own)
    whole = dot(c_high, c_low).astype(BF16)
    phi_last = side(dot(c_high, second_k).astype(BF16), second_k)

    def own_rows(full):
        return lax.dynamic_slice_in_dim(full, slab * width + core * half, half, 0)

    pieces = {1: own_rows(whole)}
    spans = {1: whole}
    levels = lax.axis_size(CHIPS).bit_length() - 1
    piece = pieces[1]
    for count in range(2, (1 << (levels - 1)) + 1):
        piece = dot(from_later(piece, 1), whole).astype(BF16)
        if count & (count - 1) == 0:
            spans[count] = lax.all_gather(piece, ("z", "core"), axis=0, tiled=True)

    z = dot(second_p, first_k).astype(BF16)
    cols = turned(z).reshape(order, width)
    part = (first_p.astype(F32) + dot(cols.T, first_k)).astype(BF16)

    def half_rows(block, which):
        return lax.dynamic_slice_in_dim(block, which * half, half, 0)

    def folded(base, x, c):
        z = dot(x, c).astype(BF16)
        got = turned(z)
        far = from_other_core(got)
        full = jnp.stack([side(got, far), side(far, got)], axis=1).reshape(order, width)
        y = half_rows(full.T, core)
        return (base.astype(F32) + dot(y, c)).astype(BF16)

    sent = half_rows(part, 1 - core)
    came = from_other_core(sent)
    kept = half_rows(part, core)
    reduced = folded(side(kept, came), side(came, kept), c_low)
    for level in range(levels):
        distance = 1 << level
        reduced = folded(reduced, from_later(reduced, distance), spans[distance])

    far = from_other_core(reduced)
    start = jnp.concatenate([side(reduced, far), side(far, reduced)], axis=0)
    after = from_later(reduced, 1)
    far_after = from_other_core(after)
    after = jnp.concatenate([side(after, far_after), side(far_after, after)], axis=0)
    part_high = from_other_core(part)
    left_a = side(part_high, after)
    right_a = side(second_k, own)
    z = jnp.concatenate([dot(left_a, right_a), dot(after, phi_last)], axis=0).astype(BF16)
    got = turned(z).reshape(8, 2, width, width)
    ya = got[:, 0].reshape(order, width).T
    yb = got[:, 1].reshape(order, width).T
    ta, tb = dot(ya, right_a), dot(yb, phi_last)
    out_a = side(start, (part.astype(F32) + ta).astype(BF16))
    out_b = (second_p.astype(F32) + side(ta + tb, tb)).astype(BF16)
    return jnp.stack([out_a, out_b], axis=0).swapaxes(1, 2)


def solution(mesh):
    grid = Mesh(mesh.devices.reshape(4, 4, 2, 8), ("y", "x", "core", "z"))
    return jax.shard_map(
        shards,
        mesh=grid,
        in_specs=(P(("y", "x", "core"), None, "z"), P(("y", "x", "core"), None, None)),
        out_specs=P(("y", "x", "core"), None, "z"),
        check_vma=False,
    )
```

time: 541 us -> 261 us (0.48)
  waiting for transfers between devices: 451 us -> 105 us
  blocking collectives: 0 us -> 43.9 us
  starting transfers between devices: 24.1 us -> 47.8 us
  local copies, waits for them, and re-layouts: 11.3 us -> 3.48 us
    all_gather x11 -> x3, waiting for transfers between devices: 257 us -> 0.04 us  [shards(): spans[count] = lax.all_gather(piece, ('z', 'core'), axis=0, tiled=True)]
    ppermute x10 -> x22, waiting for transfers between devices: 194 us -> 73.1 us  [the longest x12 64.2 us: from_later(): lax.ppermute(block, CHIPS, [(i + distance, i) for i in range(chips - dist...]
    all_to_all x0 -> x4, blocking collectives: none -> 43.9 us  [turned(): return lax.all_to_all(pieces, 'z', 0, 0, tiled=True)]
    all_to_all x0 -> x3, waiting for transfers between devices: none -> 32.2 us  [turned(): return lax.all_to_all(pieces, 'z', 0, 0, tiled=True)]
    all_to_all x0 -> x3, starting transfers between devices: none -> 13.4 us  [turned(): return lax.all_to_all(pieces, 'z', 0, 0, tiled=True)]
    ppermute x10 -> x22, starting transfers between devices: 23.5 us -> 34.4 us  [the longest x10 18.3 us: from_other_core(): return lax.ppermute(block, 'core', [(0, 1), (1, 0)])]
    dot_general x12 -> x26, matrix products: 37.8 us -> 39.7 us  [dot(): return jnp.dot(left, right, preferred_element_type=F32)]
  transfers between devices with their start and end apart: 21 -> 28, of which waited for: 18 -> 21; matrix products, arithmetic and copies ran while one was open for 6% -> 10% of each run, Pallas kernels for 0% -> 0%
where the time goes in v1:
time: 261 us; the launch traced here: 258 us
  waiting for transfers between devices  105 us (40%)
  starting transfers between devices  47.8 us (18%)
  blocking collectives  43.9 us (17%)
  matrix products  39.7 us (15%)
  between operations  13.8 us (5%)
  other arithmetic  3.83 us (1%)
  local copies, waits for them, and re-layouts  3.48 us (1%)
    ppermute x12, waiting for transfers between devices, from_later(): lax.ppermute(block, CHIPS, [(i + distance, i) for i in range(chips - dist...  64.2 us
    all_to_all x4, blocking collectives, turned(): return lax.all_to_all(pieces, 'z', 0, 0, tiled=True)  43.9 us
    dot_general x26, matrix products, dot(): return jnp.dot(left, right, preferred_element_type=F32)  39.7 us
    all_to_all x3, waiting for transfers between devices, turned(): return lax.all_to_all(pieces, 'z', 0, 0, tiled=True)  32.2 us
    ppermute x10, starting transfers between devices, from_other_core(): return lax.ppermute(block, 'core', [(0, 1), (1, 0)])  18.3 us
    ppermute x12, starting transfers between devices, from_later(): lax.ppermute(block, CHIPS, [(i + distance, i) for i in range(chips - dist...  16 us
    all_to_all x3, starting transfers between devices, turned(): return lax.all_to_all(pieces, 'z', 0, 0, tiled=True)  13.4 us
    ppermute x10, waiting for transfers between devices, from_other_core(): return lax.ppermute(block, 'core', [(0, 1), (1, 0)])  8.86 us
  transfers between devices with their start and end apart: 28, of which 21 were waited for; matrix products, arithmetic and copies ran while one was open for 10% of the time, Pallas kernels for 0%

profile of v1, /device:TPU:1, one launch (start us, length us, event | category | flops | bytes accessed | tf_op | source)
XLA Modules:
  0.0 257.9 jit_solution(12046178700905583063)
XLA Ops:
  6.5 4.6 %fusion.9 = bf16[1024,1024]{1,0:T(8,128)(2,1)S(1)} fusion(bf16[2,1024,1024]{2,1,0:T(8,128)(2,1)} %param.3), kind=kOutput, calls=%fused_computation.13 | convolution fusion | flops 2148532224 | bytes 6291456 | tf_op jit(solution)/shard_map/dot_general | solution.py:12
  11.1 3.3 %collective-permute-start.1 = (bf16[1024,1024]{1,0:T(8,128)(2,1)S(1)}, bf16[1024,1024]{1,0:T(8,128)(2,1)}, u32[]{:S(2)}, u32[]{:S(2)}) collective-permute-start(bf16[1024,1024]{1,0:T(8,128)(2,1)S(1)} %fusion.9), channel_id=1, source_target_pairs={{0,8},{8,0},{1,9},{9,1},{2,10},{10,2},{3,11},{11,3},{4,12},{12,4},... | collective-permute-start | bytes 6291464 | tf_op jit(solution)/shard_map/ppermute | solution.py:21
  14.4 3.9 %collective-permute-done.1 = bf16[1024,1024]{1,0:T(8,128)(2,1)} collective-permute-done((bf16[1024,1024]{1,0:T(8,128)(2,1)S(1)}, bf16[1024,1024]{1,0:T(8,128)(2,1)}, u32[]{:S(2)}, u32[]{:S(2)}) %collective-permute-start.1) | collective-permute-done | bytes 2097184 | tf_op jit(solution)/shard_map/ppermute | solution.py:21
  18.4 1.8 broadcast_select_fusion.1
  20.2 4.7 %convolution_convert_fusion = bf16[1024,1024]{1,0:T(8,128)(2,1)S(1)} fusion(bf16[1024,1024]{1,0:T(8,128)(2,1)S(1)} %broadcast_select_fusion.1, bf16[1024,1024]{1,0:T(8,128)(2,1)} %collective-permute-done.1, bf16[1024,1024]{1,0:T(8,128)(2,1)} %copy-done.5, pred[]{:T(512)S(6)} %eq.2), kind=kOutput, calls=%fused_computation.14 | convolution fusion | flops 2149580800 | bytes 8388609 | tf_op jit(solution)/shard_map/dot_general | solution.py:12
  24.9 1.3 collective-permute-start.6
  26.2 5.1 %collective-permute-done.6 = bf16[64,1024]{1,0:T(8,128)(2,1)S(1)} collective-permute-done((bf16[64,1024]{1,0:T(8,128)(2,1)S(1)}, bf16[64,1024]{1,0:T(8,128)(2,1)S(1)}, u32[]{:S(2)}, u32[]{:S(2)}) %collective-permute-start.6) | collective-permute-done | bytes 131104 | tf_op jit(solution)/shard_map/ppermute | solution.py:17
  32.5 1.4 collective-permute-start.9
  33.9 6.0 %collective-permute-done.9 = bf16[64,1024]{1,0:T(8,128)(2,1)S(1)} collective-permute-done((bf16[64,1024]{1,0:T(8,128)(2,1)}, bf16[64,1024]{1,0:T(8,128)(2,1)S(1)}, u32[]{:S(2)}, u32[]{:S(2)}) %collective-permute-start.9) | collective-permute-done | bytes 131104 | tf_op jit(solution)/shard_map/ppermute | solution.py:17
  40.4 1.3 collective-permute-start.10
  41.7 4.9 %collective-permute-done.10 = bf16[64,1024]{1,0:T(8,128)(2,1)S(1)} collective-permute-done((bf16[64,1024]{1,0:T(8,128)(2,1)S(1)}, bf16[64,1024]{1,0:T(8,128)(2,1)S(1)}, u32[]{:S(2)}, u32[]{:S(2)}) %collective-permute-start.10) | collective-permute-done | bytes 131104 | tf_op jit(solution)/shard_map/ppermute | solution.py:17
  47.9 2.0 fusion.32
  50.7 6.5 %all-to-all-start = ((bf16[8,128,128]{2,1,0:T(8,128)(2,1)}), bf16[8,128,128]{2,1,0:T(8,128)(2,1)S(1)}, u32[]{:S(2)}, u32[]{:S(2)}) async-start(bf16[8,128,128]{2,1,0:T(8,128)(2,1)} %bitcast.161), calls=%async_computation | async-start | bytes 524288 | tf_op jit(solution)/shard_map/all_to_all | solution.py:29
  57.2 11.7 %all-to-all-done = bf16[8,128,128]{2,1,0:T(8,128)(2,1)S(1)} async-done(((bf16[8,128,128]{2,1,0:T(8,128)(2,1)}), bf16[8,128,128]{2,1,0:T(8,128)(2,1)S(1)}, u32[]{:S(2)}, u32[]{:S(2)}) %all-to-all-start) | async-done | bytes 262176 | tf_op jit(solution)/shard_map/all_to_all | solution.py:29
  68.9 2.1 fusion.27
  71.0 2.7 %collective-permute-start = (bf16[64,1024]{1,0:T(8,128)(2,1)S(1)}, bf16[64,1024]{1,0:T(8,128)(2,1)S(1)}, u32[]{:S(2)}, u32[]{:S(2)}) collective-permute-start(bf16[64,1024]{1,0:T(8,128)(2,1)S(1)} %constant_dynamic-slice_fusion.1), channel_id=1, source_target_pairs={{0,8},{8,0},{1,9},{9,1},{2,10},{10,2},{3,11},{11,3},{4,12},{12,4},... | collective-permute-start | bytes 393224 | tf_op jit(solution)/shard_map/ppermute | solution.py:21
  75.0 2.1 fusion.38
  77.8 3.4 %all-to-all-start.1 = ((bf16[8,64,128]{2,1,0:T(8,128)(2,1)}), bf16[8,64,128]{2,1,0:T(8,128)(2,1)S(1)}, u32[]{:S(2)}, u32[]{:S(2)}) async-start(bf16[8,64,128]{2,1,0:T(8,128)(2,1)} %bitcast.171), calls=%async_computation.1 | async-start | bytes 262144 | tf_op jit(solution)/shard_map/all_to_all | solution.py:29
  81.2 1.7 collective-permute-done.13
  83.4 1.3 collective-permute-start.14
  84.7 5.1 %all-to-all-done.1 = bf16[8,64,128]{2,1,0:T(8,128)(2,1)S(1)} async-done(((bf16[8,64,128]{2,1,0:T(8,128)(2,1)}), bf16[8,64,128]{2,1,0:T(8,128)(2,1)S(1)}, u32[]{:S(2)}, u32[]{:S(2)}) %all-to-all-start.1) | async-done | bytes 131104 | tf_op jit(solution)/shard_map/all_to_all | solution.py:29
  89.8 1.4 collective-permute-start.2
  92.0 1.4 collective-permute-start.15
  93.5 8.2 %collective-permute-done.15 = bf16[64,1024]{1,0:T(8,128)(2,1)S(1)} collective-permute-done((bf16[64,1024]{1,0:T(8,128)(2,1)S(1)}, bf16[64,1024]{1,0:T(8,128)(2,1)S(1)}, u32[]{:S(2)}, u32[]{:S(2)}) %collective-permute-start.15) | collective-permute-done | bytes 131104 | tf_op jit(solution)/shard_map/ppermute | solution.py:17
  102.2 1.3 collective-permute-start.16
  104.1 1.3 collective-permute-start.3
  105.4 4.7 %collective-permute-done.16 = bf16[64,1024]{1,0:T(8,128)(2,1)S(1)} collective-permute-done((bf16[64,1024]{1,0:T(8,128)(2,1)S(1)}, bf16[64,1024]{1,0:T(8,128)(2,1)S(1)}, u32[]{:S(2)}, u32[]{:S(2)}) %collective-permute-start.16) | collective-permute-done | bytes 131104 | tf_op jit(solution)/shard_map/ppermute | solution.py:17
  111.3 2.0 collective-permute-done.3
  113.8 11.5 %all_to_all.35 = bf16[8,64,128]{2,1,0:T(8,128)(2,1)S(1)} all-to-all(bf16[8,64,128]{2,1,0:T(8,128)(2,1)S(1)} %bitcast.184), channel_id=1, replica_groups=mesh['y'=4,'x'=4,'core'=2,'z'=8] {'z'}, dimensions={0} | all-to-all | bytes 262144 | tf_op jit(solution)/shard_map/all_to_all | solution.py:29
  125.3 2.9 %collective-permute-start.4 = (bf16[8,64,128]{2,1,0:T(8,128)(2,1)S(1)}, bf16[8,64,128]{2,1,0:T(8,128)(2,1)S(1)}, u32[]{:S(2)}, u32[]{:S(2)}) collective-permute-start(bf16[8,64,128]{2,1,0:T(8,128)(2,1)S(1)} %all_to_all.35), channel_id=1, source_target_pairs={{0,8},{8,0},{1,9},{9,1},{2,10},{10,2},{3,11},{11,3},{4,12},{12,4},... | collective-permute-start | bytes 393224 | tf_op jit(solution)/shard_map/ppermute | solution.py:21
  130.0 1.3 collective-permute-start.5
  131.3 11.5 %collective-permute-done.5 = bf16[64,1024]{1,0:T(8,128)(2,1)S(1)} collective-permute-done((bf16[64,1024]{1,0:T(8,128)(2,1)S(1)}, bf16[64,1024]{1,0:T(8,128)(2,1)S(1)}, u32[]{:S(2)}, u32[]{:S(2)}) %collective-permute-start.5) | collective-permute-done | bytes 131104 | tf_op jit(solution)/shard_map/ppermute | solution.py:17
  142.8 2.2 fusion.40
  145.0 12.0 %all_to_all.36 = bf16[8,64,128]{2,1,0:T(8,128)(2,1)S(1)} all-to-all(bf16[8,64,128]{2,1,0:T(8,128)(2,1)S(1)} %bitcast.185), channel_id=1, replica_groups=mesh['y'=4,'x'=4,'core'=2,'z'=8] {'z'}, dimensions={0} | all-to-all | bytes 262144 | tf_op jit(solution)/shard_map/all_to_all | solution.py:29
  161.1 8.3 %collective-permute-done.8 = bf16[64,1024]{1,0:T(8,128)(2,1)S(1)} collective-permute-done((bf16[64,1024]{1,0:T(8,128)(2,1)S(1)}, bf16[64,1024]{1,0:T(8,128)(2,1)S(1)}, u32[]{:S(2)}, u32[]{:S(2)}) %collective-permute-start.8) | collective-permute-done | bytes 131104 | tf_op jit(solution)/shard_map/ppermute | solution.py:17
  169.4 2.1 fusion.41
  171.5 10.1 %all_to_all.37 = bf16[8,64,128]{2,1,0:T(8,128)(2,1)S(1)} all-to-all(bf16[8,64,128]{2,1,0:T(8,128)(2,1)S(1)} %bitcast.186), channel_id=1, replica_groups=mesh['y'=4,'x'=4,'core'=2,'z'=8] {'z'}, dimensions={0} | all-to-all | bytes 262144 | tf_op jit(solution)/shard_map/all_to_all | solution.py:29
  181.7 2.3 collective-permute-start.11
  187.0 6.8 %collective-permute-done.12 = bf16[64,1024]{1,0:T(8,128)(2,1)S(1)} collective-permute-done((bf16[64,1024]{1,0:T(8,128)(2,1)S(1)}, bf16[64,1024]{1,0:T(8,128)(2,1)S(1)}, u32[]{:S(2)}, u32[]{:S(2)}) %collective-permute-start.12) | collective-permute-done | bytes 131104 | tf_op jit(solution)/shard_map/ppermute | solution.py:17
  193.8 2.1 fusion.42
  195.9 10.3 %all_to_all.38 = bf16[8,64,128]{2,1,0:T(8,128)(2,1)S(1)} all-to-all(bf16[8,64,128]{2,1,0:T(8,128)(2,1)S(1)} %bitcast.187), channel_id=1, replica_groups=mesh['y'=4,'x'=4,'core'=2,'z'=8] {'z'}, dimensions={0} | all-to-all | bytes 262144 | tf_op jit(solution)/shard_map/all_to_all | solution.py:29
  206.2 2.3 collective-permute-start.17
  210.3 1.6 collective-permute-start.20
  212.3 4.9 %collective-permute-done.20 = bf16[64,1024]{1,0:T(8,128)(2,1)S(1)} collective-permute-done((bf16[64,1024]{1,0:T(8,128)(2,1)S(1)}, bf16[64,1024]{1,0:T(8,128)(2,1)S(1)}, u32[]{:S(2)}, u32[]{:S(2)}) %collective-permute-start.20) | collective-permute-done | bytes 131104 | tf_op jit(solution)/shard_map/ppermute | solution.py:17
  218.3 4.6 %bitcast_select_fusion = bf16[1024,1024]{1,0:T(8,128)(2,1)S(1)} fusion(pred[]{:T(512)S(6)} %eq.2, bf16[2,1024,1024]{2,1,0:T(8,128)(2,1)} %param.3, bf16[1024,1024]{1,0:T(8,128)(2,1)} %collective-permute-done.1, bf16[1024,1024]{1,0:T(8,128)(2,1)S(1)} %copy-done.6), kind=kOutput, calls=%fused_computation | convolution fusion | flops 2150629376 | bytes 10486784 | tf_op jit(solution)/shard_map/dot_general | solution.py:12
  225.0 3.5 %all-to-all-start.6 = ((bf16[8,256,128]{2,1,0:T(8,128)(2,1)}), bf16[8,256,128]{2,1,0:T(8,128)(2,1)S(1)}, u32[]{:S(2)}, u32[]{:S(2)}) async-start(bf16[8,256,128]{2,1,0:T(8,128)(2,1)} %maximum_bitcast_fusion), calls=%async_computation.6 | async-start | bytes 1048576 | tf_op jit(solution)/shard_map/all_to_all | solution.py:29
  230.9 15.4 %all-to-all-done.6 = bf16[8,256,128]{2,1,0:T(8,128)(2,1)S(1)} async-done(((bf16[8,256,128]{2,1,0:T(8,128)(2,1)}), bf16[8,256,128]{2,1,0:T(8,128)(2,1)S(1)}, u32[]{:S(2)}, u32[]{:S(2)}) %all-to-all-start.6) | async-done | bytes 524320 | tf_op jit(solution)/shard_map/all_to_all | solution.py:29
  246.4 2.8 %fusion.43 = f32[128,1024]{1,0:T(8,128)S(1)} fusion(bf16[1024,128]{1,0:T(8,128)(2,1)S(1)} %bitcast.189, bf16[1024,1024]{1,0:T(8,128)(2,1)} %copy-done.5, pred[]{:T(512)S(6)} %eq.2, bf16[2,1024,1024]{2,1,0:T(8,128)(2,1)} %param.3), kind=kOutput, calls=%fused_computation.52 | convolution fusion | flops 269484032 | bytes 4980737 | tf_op jit(solution)/shard_map/dot_general | solution.py:12
  (98 shorter events, 28.6 us)
Async XLA Ops:
  6.5 136.2 %all-gather.4.cloned.1.call-start = ((), (), s32[]{:S(2)}) async-start(), calls=%async_computation.7 | async-start | bytes 2228224 | tf_op jit(solution)/shard_map/all_gather | solution.py:61
  11.1 7.3 %copy-start.5 = (bf16[1024,1024]{1,0:T(8,128)(2,1)}, bf16[1024,1024]{1,0:T(8,128)(2,1)S(1)}, u32[]{:S(2)}) copy-start(bf16[1024,1024]{1,0:T(8,128)(2,1)S(1)} %fusion.9) | copy-start | bytes 6291460
  11.1 7.2 %collective-permute-start.1 = (bf16[1024,1024]{1,0:T(8,128)(2,1)S(1)}, bf16[1024,1024]{1,0:T(8,128)(2,1)}, u32[]{:S(2)}, u32[]{:S(2)}) collective-permute-start(bf16[1024,1024]{1,0:T(8,128)(2,1)S(1)} %fusion.9), channel_id=1, source_target_pairs={{0,8},{8,0},{1,9},{9,1},{2,10},{10,2},{3,11},{11,3},{4,12},{12,4},... | collective-permute-start | bytes 6291464 | tf_op jit(solution)/shard_map/ppermute | solution.py:21
  20.2 4.7 %copy-start = (bf16[1024,1024]{1,0:T(8,128)(2,1)}, bf16[1024,1024]{1,0:T(8,128)(2,1)S(1)}, u32[]{:S(2)}) copy-start(bf16[1024,1024]{1,0:T(8,128)(2,1)S(1)} %broadcast_select_fusion.1) | copy-start | bytes 6291460
  24.9 6.4 %collective-permute-start.6 = (bf16[64,1024]{1,0:T(8,128)(2,1)S(1)}, bf16[64,1024]{1,0:T(8,128)(2,1)S(1)}, u32[]{:S(2)}, u32[]{:S(2)}) collective-permute-start(bf16[64,1024]{1,0:T(8,128)(2,1)S(1)} %constant_dynamic-slice_fusion), channel_id=1, source_target_pairs={{16,0},{32,16},{48,32},{64,48},{80,64},{96,80},{112,96},{128,112},... | collective-permute-start | bytes 393224 | tf_op jit(solution)/shard_map/ppermute | solution.py:17
  32.4 15.3 %copy-start.10 = (bf16[2,1024,128]{2,1,0:T(8,128)(2,1)S(1)}, bf16[2,1024,128]{2,1,0:T(8,128)(2,1)}, u32[]{:S(2)}) copy-start(bf16[2,1024,128]{2,1,0:T(8,128)(2,1)} %param.2) | copy-start | bytes 1572868
  32.4 128.6 %all-gather.6.cloned.1.call-start = ((), (), s32[]{:S(2)}) async-start(), calls=%async_computation.8 | async-start | bytes 2228224 | tf_op jit(solution)/shard_map/all_gather | solution.py:61
  32.5 7.4 %collective-permute-start.9 = (bf16[64,1024]{1,0:T(8,128)(2,1)}, bf16[64,1024]{1,0:T(8,128)(2,1)S(1)}, u32[]{:S(2)}, u32[]{:S(2)}) collective-permute-start(bf16[64,1024]{1,0:T(8,128)(2,1)} %convolution_convert_fusion.12), channel_id=1, source_target_pairs={{16,0},{32,16},{48,32},{64,48},{80,64},{96,80},{112,96},{128,112},... | collective-permute-start | bytes 393224 | tf_op jit(solution)/shard_map/ppermute | solution.py:17
  40.4 6.2 %collective-permute-start.10 = (bf16[64,1024]{1,0:T(8,128)(2,1)S(1)}, bf16[64,1024]{1,0:T(8,128)(2,1)S(1)}, u32[]{:S(2)}, u32[]{:S(2)}) collective-permute-start(bf16[64,1024]{1,0:T(8,128)(2,1)S(1)} %convolution_convert_fusion.10), channel_id=1, source_target_pairs={{16,0},{32,16},{48,32},{64,48},{80,64},{96,80},{112,96},{128,112},... | collective-permute-start | bytes 393224 | tf_op jit(solution)/shard_map/ppermute | solution.py:17
  50.0 23.7 %copy-start.9 = (bf16[64,1024]{1,0:T(8,128)(2,1)S(1)}, bf16[64,1024]{1,0:T(8,128)(2,1)}, u32[]{:S(2)}) copy-start(bf16[64,1024]{1,0:T(8,128)(2,1)} %convolution_convert_fusion.9) | copy-start | bytes 393220
  50.7 18.2 %all-to-all-start = ((bf16[8,128,128]{2,1,0:T(8,128)(2,1)}), bf16[8,128,128]{2,1,0:T(8,128)(2,1)S(1)}, u32[]{:S(2)}, u32[]{:S(2)}) async-start(bf16[8,128,128]{2,1,0:T(8,128)(2,1)} %bitcast.161), calls=%async_computation | async-start | bytes 524288 | tf_op jit(solution)/shard_map/all_to_all | solution.py:29
  71.0 4.0 %collective-permute-start = (bf16[64,1024]{1,0:T(8,128)(2,1)S(1)}, bf16[64,1024]{1,0:T(8,128)(2,1)S(1)}, u32[]{:S(2)}, u32[]{:S(2)}) collective-permute-start(bf16[64,1024]{1,0:T(8,128)(2,1)S(1)} %constant_dynamic-slice_fusion.1), channel_id=1, source_target_pairs={{0,8},{8,0},{1,9},{9,1},{2,10},{10,2},{3,11},{11,3},{4,12},{12,4},... | collective-permute-start | bytes 393224 | tf_op jit(solution)/shard_map/ppermute | solution.py:21
  73.7 9.2 %collective-permute-start.13 = (bf16[64,1024]{1,0:T(8,128)(2,1)S(1)}, bf16[64,1024]{1,0:T(8,128)(2,1)S(1)}, u32[]{:S(2)}, u32[]{:S(2)}) collective-permute-start(bf16[64,1024]{1,0:T(8,128)(2,1)S(1)} %copy-done.9), channel_id=1, source_target_pairs={{16,0},{32,16},{48,32},{64,48},{80,64},{96,80},{112,96},{128,112},... | collective-permute-start | bytes 393224 | tf_op jit(solution)/shard_map/ppermute | solution.py:17
  77.8 12.0 %all-to-all-start.1 = ((bf16[8,64,128]{2,1,0:T(8,128)(2,1)}), bf16[8,64,128]{2,1,0:T(8,128)(2,1)S(1)}, u32[]{:S(2)}, u32[]{:S(2)}) async-start(bf16[8,64,128]{2,1,0:T(8,128)(2,1)} %bitcast.171), calls=%async_computation.1 | async-start | bytes 262144 | tf_op jit(solution)/shard_map/all_to_all | solution.py:29
  81.2 105.8 %all-gather.8.cloned.1.call-start = ((), (), s32[]{:S(2)}) async-start(), calls=%async_computation.9 | async-start | bytes 2228224 | tf_op jit(solution)/shard_map/all_gather | solution.py:61
  83.4 8.1 %collective-permute-start.14 = (bf16[64,1024]{1,0:T(8,128)(2,1)S(1)}, bf16[64,1024]{1,0:T(8,128)(2,1)S(1)}, u32[]{:S(2)}, u32[]{:S(2)}) collective-permute-start(bf16[64,1024]{1,0:T(8,128)(2,1)S(1)} %convolution_convert_fusion.7), channel_id=1, source_target_pairs={{16,0},{32,16},{48,32},{64,48},{80,64},{96,80},{112,96},{128,112},... | collective-permute-start | bytes 393224 | tf_op jit(solution)/shard_map/ppermute | solution.py:17
  89.8 3.6 %collective-permute-start.2 = (bf16[8,64,128]{2,1,0:T(8,128)(2,1)S(1)}, bf16[8,64,128]{2,1,0:T(8,128)(2,1)S(1)}, u32[]{:S(2)}, u32[]{:S(2)}) collective-permute-start(bf16[8,64,128]{2,1,0:T(8,128)(2,1)S(1)} %all-to-all-done.1), channel_id=1, source_target_pairs={{0,8},{8,0},{1,9},{9,1},{2,10},{10,2},{3,11},{11,3},{4,12},{12,4},... | collective-permute-start | bytes 393224 | tf_op jit(solution)/shard_map/ppermute | solution.py:21
  91.9 11.5 %copy-start.1 = (bf16[1024,1024]{1,0:T(8,128)(2,1)S(1)}, bf16[1024,1024]{1,0:T(8,128)(2,1)}, u32[]{:S(2)}) copy-start(bf16[1024,1024]{1,0:T(8,128)(2,1)} %copy-done) | copy-start | bytes 6291460
  92.0 9.7 %collective-permute-start.15 = (bf16[64,1024]{1,0:T(8,128)(2,1)S(1)}, bf16[64,1024]{1,0:T(8,128)(2,1)S(1)}, u32[]{:S(2)}, u32[]{:S(2)}) collective-permute-start(bf16[64,1024]{1,0:T(8,128)(2,1)S(1)} %convolution_convert_fusion.6), channel_id=1, source_target_pairs={{16,0},{32,16},{48,32},{64,48},{80,64},{96,80},{112,96},{128,112},... | collective-permute-start | bytes 393224 | tf_op jit(solution)/shard_map/ppermute | solution.py:17
  102.2 8.0 %collective-permute-start.16 = (bf16[64,1024]{1,0:T(8,128)(2,1)S(1)}, bf16[64,1024]{1,0:T(8,128)(2,1)S(1)}, u32[]{:S(2)}, u32[]{:S(2)}) collective-permute-start(bf16[64,1024]{1,0:T(8,128)(2,1)S(1)} %convolution_convert_fusion.5), channel_id=1, source_target_pairs={{16,0},{32,16},{48,32},{64,48},{80,64},{96,80},{112,96},{128,112},... | collective-permute-start | bytes 393224 | tf_op jit(solution)/shard_map/ppermute | solution.py:17
  104.1 9.2 %collective-permute-start.3 = (bf16[64,1024]{1,0:T(8,128)(2,1)S(1)}, bf16[64,1024]{1,0:T(8,128)(2,1)S(1)}, u32[]{:S(2)}, u32[]{:S(2)}) collective-permute-start(bf16[64,1024]{1,0:T(8,128)(2,1)S(1)} %add_convert_fusion.2), channel_id=1, source_target_pairs={{16,0},{32,16},{48,32},{64,48},{80,64},{96,80},{112,96},{128,112},... | collective-permute-start | bytes 393224 | tf_op jit(solution)/shard_map/ppermute | solution.py:17
  125.3 3.9 %collective-permute-start.4 = (bf16[8,64,128]{2,1,0:T(8,128)(2,1)S(1)}, bf16[8,64,128]{2,1,0:T(8,128)(2,1)S(1)}, u32[]{:S(2)}, u32[]{:S(2)}) collective-permute-start(bf16[8,64,128]{2,1,0:T(8,128)(2,1)S(1)} %all_to_all.35), channel_id=1, source_target_pairs={{0,8},{8,0},{1,9},{9,1},{2,10},{10,2},{3,11},{11,3},{4,12},{12,4},... | collective-permute-start | bytes 393224 | tf_op jit(solution)/shard_map/ppermute | solution.py:21
  130.0 12.8 %collective-permute-start.5 = (bf16[64,1024]{1,0:T(8,128)(2,1)S(1)}, bf16[64,1024]{1,0:T(8,128)(2,1)S(1)}, u32[]{:S(2)}, u32[]{:S(2)}) collective-permute-start(bf16[64,1024]{1,0:T(8,128)(2,1)S(1)} %add_convert_fusion.1), channel_id=1, source_target_pairs={{32,0},{48,16},{64,32},{80,48},{96,64},{112,80},{128,96},{144,112}... | collective-permute-start | bytes 393224 | tf_op jit(solution)/shard_map/ppermute | solution.py:17
  142.8 16.4 %copy-start.3 = (bf16[1024,1024]{1,0:T(8,128)(2,1)S(1)}, bf16[1024,1024]{1,0:T(8,128)(2,1)}, u32[]{:S(2)}) copy-start(bf16[1024,1024]{1,0:T(8,128)(2,1)} %all-gather.4.cloned.1.call-done) | copy-start | bytes 6291460
  157.0 2.0 collective-permute-start.7
  159.7 9.7 %collective-permute-start.8 = (bf16[64,1024]{1,0:T(8,128)(2,1)S(1)}, bf16[64,1024]{1,0:T(8,128)(2,1)S(1)}, u32[]{:S(2)}, u32[]{:S(2)}) collective-permute-start(bf16[64,1024]{1,0:T(8,128)(2,1)S(1)} %fusion.35), channel_id=1, source_target_pairs={{64,0},{80,16},{96,32},{112,48},{128,64},{144,80},{160,96},{176,11... | collective-permute-start | bytes 393224 | tf_op jit(solution)/shard_map/ppermute | solution.py:17
  161.1 23.9 %copy-start.2 = (bf16[1024,1024]{1,0:T(8,128)(2,1)S(1)}, bf16[1024,1024]{1,0:T(8,128)(2,1)}, u32[]{:S(2)}) copy-start(bf16[1024,1024]{1,0:T(8,128)(2,1)} %all-gather.6.cloned.1.call-done) | copy-start | bytes 6291460
  181.7 3.2 %collective-permute-start.11 = (bf16[8,64,128]{2,1,0:T(8,128)(2,1)S(1)}, bf16[8,64,128]{2,1,0:T(8,128)(2,1)S(1)}, u32[]{:S(2)}, u32[]{:S(2)}) collective-permute-start(bf16[8,64,128]{2,1,0:T(8,128)(2,1)S(1)} %all_to_all.37), channel_id=1, source_target_pairs={{0,8},{8,0},{1,9},{9,1},{2,10},{10,2},{3,11},{11,3},{4,12},{12,4},... | collective-permute-start | bytes 393224 | tf_op jit(solution)/shard_map/ppermute | solution.py:21
  185.7 8.1 %collective-permute-start.12 = (bf16[64,1024]{1,0:T(8,128)(2,1)S(1)}, bf16[64,1024]{1,0:T(8,128)(2,1)S(1)}, u32[]{:S(2)}, u32[]{:S(2)}) collective-permute-start(bf16[64,1024]{1,0:T(8,128)(2,1)S(1)} %fusion.36), channel_id=1, source_target_pairs={{128,0},{144,16},{160,32},{176,48},{192,64},{208,80},{224,96},{240... | collective-permute-start | bytes 393224 | tf_op jit(solution)/shard_map/ppermute | solution.py:17
  187.0 22.6 %copy-start.4 = (bf16[1024,1024]{1,0:T(8,128)(2,1)S(1)}, bf16[1024,1024]{1,0:T(8,128)(2,1)}, u32[]{:S(2)}) copy-start(bf16[1024,1024]{1,0:T(8,128)(2,1)} %all-gather.8.cloned.1.call-done) | copy-start | bytes 6291460
  206.2 12.1 %copy-start.6 = (bf16[1024,1024]{1,0:T(8,128)(2,1)S(1)}, bf16[1024,1024]{1,0:T(8,128)(2,1)}, u32[]{:S(2)}) copy-start(bf16[1024,1024]{1,0:T(8,128)(2,1)} %copy-done.5) | copy-start | bytes 6291460
  206.2 3.3 %collective-permute-start.17 = (bf16[8,64,128]{2,1,0:T(8,128)(2,1)S(1)}, bf16[8,64,128]{2,1,0:T(8,128)(2,1)S(1)}, u32[]{:S(2)}, u32[]{:S(2)}) collective-permute-start(bf16[8,64,128]{2,1,0:T(8,128)(2,1)S(1)} %all_to_all.38), channel_id=1, source_target_pairs={{0,8},{8,0},{1,9},{9,1},{2,10},{10,2},{3,11},{11,3},{4,12},{12,4},... | collective-permute-start | bytes 393224 | tf_op jit(solution)/shard_map/ppermute | solution.py:21
  210.3 12.7 %copy-start.11 = (bf16[2,1024,1024]{2,1,0:T(8,128)(2,1)S(1)}, bf16[2,1024,1024]{2,1,0:T(8,128)(2,1)}, u32[]{:S(2)}) copy-start(bf16[2,1024,1024]{2,1,0:T(8,128)(2,1)} %param.3) | copy-start | bytes 12582916
  210.3 6.9 %collective-permute-start.20 = (bf16[64,1024]{1,0:T(8,128)(2,1)S(1)}, bf16[64,1024]{1,0:T(8,128)(2,1)S(1)}, u32[]{:S(2)}, u32[]{:S(2)}) collective-permute-start(bf16[64,1024]{1,0:T(8,128)(2,1)S(1)} %fusion.37), channel_id=1, source_target_pairs={{16,0},{32,16},{48,32},{64,48},{80,64},{96,80},{112,96},{128,112},... | collective-permute-start | bytes 393224 | tf_op jit(solution)/shard_map/ppermute | solution.py:17
  211.8 11.1 %collective-permute-start.19 = (bf16[128,1024]{1,0:T(8,128)(2,1)S(1)}, bf16[128,1024]{1,0:T(8,128)(2,1)S(1)}, u32[]{:S(2)}, u32[]{:S(2)}) collective-permute-start(bf16[128,1024]{1,0:T(8,128)(2,1)S(1)} %fusion.27), channel_id=1, source_target_pairs={{0,8},{8,0},{1,9},{9,1},{2,10},{10,2},{3,11},{11,3},{4,12},{12,4},... | collective-permute-start | bytes 786440 | tf_op jit(solution)/shard_map/ppermute | solution.py:21
  217.2 5.8 %collective-permute-start.21 = (bf16[64,1024]{1,0:T(8,128)(2,1)S(1)}, bf16[64,1024]{1,0:T(8,128)(2,1)S(1)}, u32[]{:S(2)}, u32[]{:S(2)}) collective-permute-start(bf16[64,1024]{1,0:T(8,128)(2,1)S(1)} %collective-permute-done.20), channel_id=1, source_target_pairs={{0,8},{8,0},{1,9},{9,1},{2,10},{10,2},{3,11},{11,3},{4,12},{12,4},... | collective-permute-start | bytes 393224 | tf_op jit(solution)/shard_map/ppermute | solution.py:21
  225.0 21.4 %all-to-all-start.6 = ((bf16[8,256,128]{2,1,0:T(8,128)(2,1)}), bf16[8,256,128]{2,1,0:T(8,128)(2,1)S(1)}, u32[]{:S(2)}, u32[]{:S(2)}) async-start(bf16[8,256,128]{2,1,0:T(8,128)(2,1)} %maximum_bitcast_fusion), calls=%async_computation.6 | async-start | bytes 1048576 | tf_op jit(solution)/shard_map/all_to_all | solution.py:29
  228.5 1.7 collective-permute-start.18
  249.2 0.9 copy-start.7
  249.2 1.0 copy-start.8
Sparse Core Ops, SparseCore 0:
  32.5 44.0 all-gather.3
  78.5 38.8 all-gather.5
  119.2 40.7 all-gather.7

commit v2 on v1

v2 whole, which is shorter than its diff:
```python
import jax
import jax.numpy as jnp
from jax import lax
from jax.sharding import Mesh, PartitionSpec as P

BF16 = jnp.bfloat16
F32 = jnp.float32
CHIPS = ("y", "x")


def dot(left, right):
    return jnp.dot(left, right, preferred_element_type=F32)


def tie(value, *others):
    return lax.optimization_barrier((value, *others))[0]


def moved(block, pairs):
    return lax.ppermute(block, CHIPS, pairs)


def from_other_core(block):
    return lax.ppermute(block, "core", [(0, 1), (1, 0)])


def turned(rows):
    slabs = lax.axis_size("z")
    m, n = rows.shape
    rows = lax.optimization_barrier(rows)
    pieces = rows.reshape(m, slabs, n // slabs).swapaxes(0, 1)
    return lax.all_to_all(pieces, "z", 0, 0, tiled=True)


def shards(precision_blocks, coupling):
    core = lax.axis_index("core")
    slab = lax.axis_index("z")
    chip = lax.axis_index(CHIPS)
    chips = lax.axis_size(CHIPS)
    order, width = precision_blocks.shape[1:]
    half = width // 2

    def side(a, b):
        return jnp.where(core == 0, a, b)

    def half_rows(block, which):
        return lax.dynamic_slice_in_dim(block, which * half, half, 0)

    def both_halves(block):
        far = from_other_core(block)
        return side(jnp.concatenate([block, far], axis=0), jnp.concatenate([far, block], axis=0))

    def later(distance):
        return [(i + distance, i) for i in range(chips - distance)]

    first_k, second_k = coupling[0], coupling[1]
    p_high = lax.ppermute(precision_blocks[0], "core", [(1, 0)])
    own = dot(second_k, first_k).astype(BF16)
    other = from_other_core(own)
    z_a = lax.dot_general(
        precision_blocks[1], first_k, (((0,), (0,)), ((), ())), preferred_element_type=F32
    ).astype(BF16)
    z_b = side(dot(p_high.T, own), dot(z_a, other)).astype(BF16)

    whole = dot(side(other, own), side(own, other)).astype(BF16)
    piece = lax.dynamic_slice_in_dim(whole, slab * width + core * half, half, 0)
    z_b, piece = lax.optimization_barrier((z_b, piece))
    got = turned(jnp.concatenate([z_a, z_b], axis=0))
    hop = moved(piece, later(1))
    mine = lax.dynamic_slice_in_dim(whole, core * (order // 2), order // 2, 1)
    near = moved(mine, [(i, i + 1) for i in range(chips - 1)])
    piece = dot(hop, whole).astype(BF16)
    piece = dot(moved(piece, later(1)), whole).astype(BF16)

    got, piece = lax.optimization_barrier((got, piece))
    hop = moved(piece, later(1))
    rows = precision_blocks.swapaxes(1, 2)
    first_p, second_p = rows[0].astype(F32), rows[1].astype(F32)
    got = got.reshape(8, 2, width, width)
    y_a = got[:, 0].reshape(order, width).T
    y_b = got[:, 1].reshape(order, width).T
    base = first_p + dot(y_a, first_k)
    part = base.astype(BF16)
    left = side(y_b, dot(y_b, first_k).astype(BF16))
    total = side(base + dot(left, own), dot(left, other))
    came = from_other_core(half_rows(total, 1 - core))
    reduced = (half_rows(total, core) + came).astype(BF16)

    def closed(base, got, times):
        far = from_other_core(got)
        full = jnp.stack([side(got, far), side(far, got)], axis=1).reshape(order, width)
        y = half_rows(full.T, core)
        return (base.astype(F32) + times(y)).astype(BF16)

    times = lambda x: dot(x, whole)
    x = moved(reduced, later(1))
    piece = dot(hop, whole).astype(BF16)
    near_piece = moved(piece, [(e, (e - 1) % chips) for e in range(chips)])
    far_piece = moved(piece, [(e + 4, (e - 1) % chips) for e in range(chips - 4)])
    near_piece, far_piece, near, x = lax.optimization_barrier((near_piece, far_piece, near, x))
    z = times(x).astype(BF16)
    both = lax.all_gather(
        jnp.stack([near_piece, far_piece], axis=0), ("z", "core"), axis=1, tiled=True
    )
    phi2_mine = dot(whole, near).astype(BF16)
    phi2_other = from_other_core(phi2_mine)
    got, phi2_mine = lax.optimization_barrier((turned(z), phi2_mine))
    reduced = closed(reduced, got, times)

    def times(x):
        mine, far = dot(x, phi2_mine), dot(x, phi2_other)
        return side(jnp.concatenate([mine, far], axis=1), jnp.concatenate([far, mine], axis=1))

    x = moved(reduced, [(c + 1, c) for c in range(1, chips - 1)])
    base = moved(reduced, [(c, (c + 1) % chips) for c in range(chips)])
    x, base = lax.optimization_barrier((x, base))
    reduced = closed(base, turned(times(x).astype(BF16)), times)

    x = moved(reduced, [((e + 5) % chips, (e - 1) % chips) for e in range(chips - 4)])
    base = moved(reduced, [((e + 1) % chips, (e - 1) % chips) for e in range(chips)])
    phi4, phi4_far = lax.optimization_barrier((both[0], both[1]))
    times = lambda x: dot(x, phi4)
    z = times(x).astype(BF16)
    phi8 = dot(tie(phi4_far, z), phi4).astype(BF16)
    got, base, phi8 = lax.optimization_barrier((turned(z), base, phi8))
    reduced = closed(base, got, times)
    times = lambda x: dot(x, phi8)
    x = moved(reduced, [((e + 7) % chips, (e - 1) % chips) for e in range(chips - 8)])
    reduced = closed(reduced, turned(times(x).astype(BF16)), times)

    start = moved(reduced, [(c, (c + 1) % chips) for c in range(chips)])
    after = jnp.where(chip == chips - 1, jnp.zeros_like(reduced), reduced)
    after = both_halves(after)
    part_high = lax.ppermute(part, "core", [(1, 0)])
    through = side(dot(after, other), dot(after, own)).astype(BF16)
    v = dot(side(part_high, after), second_k).astype(BF16)
    w = dot(through, second_k).astype(BF16)
    got = turned(jnp.concatenate([side(v, through), side(w, v)], axis=0))
    got = got.reshape(8, 2, width, width)
    y_a = got[:, 0].reshape(order, width).T
    y_b = got[:, 1].reshape(order, width).T
    w = side(dot(y_b, other), dot(y_a, own))
    q = side((y_a.astype(F32) + w).astype(BF16), y_b)
    out_b = (second_p + dot(q, second_k)).astype(BF16)
    out_a = side(both_halves(start), (part.astype(F32) + w).astype(BF16))
    return jnp.stack([out_a, out_b], axis=0).swapaxes(1, 2)


def solution(mesh):
    grid = Mesh(mesh.devices.reshape(4, 4, 2, 8), ("y", "x", "core", "z"))
    return jax.shard_map(
        shards,
        mesh=grid,
        in_specs=(P(("y", "x", "core"), None, "z"), P(("y", "x", "core"), None, None)),
        out_specs=P(("y", "x", "core"), None, "z"),
        check_vma=False,
    )
```

time: 261 us -> 223 us (0.85)
  waiting for transfers between devices: 105 us -> 59.2 us
  blocking collectives: 43.9 us -> 22.4 us
  starting transfers between devices: 47.8 us -> 66.8 us
  local copies, waits for them, and re-layouts: 3.48 us -> 12.5 us
  matrix products: 39.7 us -> 44.6 us
    ppermute x12 -> x15, waiting for transfers between devices: 64.2 us -> 35.3 us  [the longest x13 35.3 us: moved(): return lax.ppermute(block, CHIPS, pairs)]
    all_to_all x4 -> x2, blocking collectives: 43.9 us -> 22.4 us  [turned(): return lax.all_to_all(pieces, 'z', 0, 0, tiled=True)]
    ppermute x12 -> x15, starting transfers between devices: 16 us -> 33.8 us  [the longest x13 29.8 us: moved(): return lax.ppermute(block, CHIPS, pairs)]
    all_to_all x3 -> x4, waiting for transfers between devices: 32.2 us -> 19.9 us  [turned(): return lax.all_to_all(pieces, 'z', 0, 0, tiled=True)]
    all_to_all x3 -> x4, starting transfers between devices: 13.4 us -> 18.9 us  [turned(): return lax.all_to_all(pieces, 'z', 0, 0, tiled=True)]
    ppermute x10 -> x9, waiting for transfers between devices: 8.86 us -> 3.95 us  [from_other_core(): return lax.ppermute(block, 'core', [(0, 1), (1, 0)])]
    ppermute x10 -> x9, starting transfers between devices: 18.3 us -> 14.1 us  [from_other_core(): return lax.ppermute(block, 'core', [(0, 1), (1, 0)])]
    squeeze x0 -> x2, local copies, waits for them, and re-layouts: none -> 4 us  [the longest x1 3.98 us: shards(): phi4, phi4_far = lax.optimization_barrier((both[0], both[1]))]
  transfers between devices with their start and end apart: 28 -> 29, of which waited for: 21 -> 15; matrix products, arithmetic and copies ran while one was open for 10% -> 21% of each run, Pallas kernels for 0% -> 0%
where the time goes in v2:
time: 223 us; the launch traced here: 222 us
  starting transfers between devices  66.8 us (30%)
  waiting for transfers between devices  59.2 us (27%)
  matrix products  44.6 us (20%)
  blocking collectives  22.4 us (10%)
  between operations  14.2 us (6%)
  local copies, waits for them, and re-layouts  12.5 us (6%)
  other arithmetic  2.27 us (1%)
    dot_general x30, matrix products, dot(): return jnp.dot(left, right, preferred_element_type=F32)  42.6 us
    ppermute x13, waiting for transfers between devices, moved(): return lax.ppermute(block, CHIPS, pairs)  35.3 us
    ppermute x13, starting transfers between devices, moved(): return lax.ppermute(block, CHIPS, pairs)  29.8 us
    all_to_all x2, blocking collectives, turned(): return lax.all_to_all(pieces, 'z', 0, 0, tiled=True)  22.4 us
    all_to_all x4, waiting for transfers between devices, turned(): return lax.all_to_all(pieces, 'z', 0, 0, tiled=True)  19.9 us
    all_to_all x4, starting transfers between devices, turned(): return lax.all_to_all(pieces, 'z', 0, 0, tiled=True)  18.9 us
    ppermute x9, starting transfers between devices, from_other_core(): return lax.ppermute(block, 'core', [(0, 1), (1, 0)])  14.1 us
  transfers between devices with their start and end apart: 29, of which 15 were waited for; matrix products, arithmetic and copies ran while one was open for 21% of the time, Pallas kernels for 0%

profile of v2, /device:TPU:1, one launch (start us, length us, event | category | flops | bytes accessed | tf_op | source)
XLA Modules:
  0.0 221.8 jit_solution(16945548519997946665)
XLA Ops:
  6.5 4.6 %fusion.24 = bf16[1024,1024]{1,0:T(8,128)(2,1)S(1)} fusion(bf16[2,1024,1024]{2,1,0:T(8,128)(2,1)} %param.3), kind=kOutput, calls=%fused_computation.22 | convolution fusion | flops 2148532224 | bytes 6291456 | tf_op jit(solution)/shard_map/dot_general | solution.py:12
  11.2 3.3 %collective-permute-start.1 = (bf16[1024,1024]{1,0:T(8,128)(2,1)S(1)}, bf16[1024,1024]{1,0:T(8,128)(2,1)}, u32[]{:S(2)}, u32[]{:S(2)}) collective-permute-start(bf16[1024,1024]{1,0:T(8,128)(2,1)S(1)} %fusion.24), channel_id=1, source_target_pairs={{0,8},{8,0},{1,9},{9,1},{2,10},{10,2},{3,11},{11,3},{4,12},{12,4},... | collective-permute-start | bytes 6291464 | tf_op jit(solution)/shard_map/ppermute | solution.py:24
  14.5 1.9 collective-permute-start
  16.5 2.1 fusion.44
  18.6 4.6 %fusion.19 = bf16[1024,1024]{1,0:T(8,128)(2,1)S(1)} fusion(bf16[1024,1024]{1,0:T(8,128)(2,1)} %copy-done.2, bf16[1024,1024]{1,0:T(8,128)(2,1)} %collective-permute-done.1, pred[]{:T(512)S(6)} %eq.4), kind=kOutput, calls=%fused_computation.21 | convolution fusion | flops 2150629376 | bytes 6291457 | tf_op jit(solution)/shard_map/dot_general | solution.py:12
  23.2 2.2 fusion.107
  26.8 6.4 %all-to-all-start = ((bf16[8,256,128]{2,1,0:T(8,128)(2,1)}), bf16[8,256,128]{2,1,0:T(8,128)(2,1)S(1)}, u32[]{:S(2)}, u32[]{:S(2)}) async-start(bf16[8,256,128]{2,1,0:T(8,128)(2,1)} %bitcast_bitcast_fusion.1), calls=%async_computation | async-start | bytes 1048576 | tf_op jit(solution)/shard_map/all_to_all | solution.py:32
  33.3 1.3 collective-permute-start.2
  35.6 4.2 %collective-permute-done.2 = bf16[64,1024]{1,0:T(8,128)(2,1)S(1)} collective-permute-done((bf16[64,1024]{1,0:T(8,128)(2,1)S(1)}, bf16[64,1024]{1,0:T(8,128)(2,1)S(1)}, u32[]{:S(2)}, u32[]{:S(2)}) %collective-permute-start.2) | collective-permute-done | bytes 131104 | tf_op jit(solution)/shard_map/ppermute | solution.py:20
  40.3 1.3 collective-permute-start.3
  41.6 1.1 constant_dynamic-slice_fusion
  42.7 4.9 %collective-permute-start.8 = (bf16[1024,512]{1,0:T(8,128)(2,1)}, bf16[1024,512]{1,0:T(8,128)(2,1)}, u32[]{:S(2)}, u32[]{:S(2)}) collective-permute-start(bf16[1024,512]{1,0:T(8,128)(2,1)} %constant_dynamic-slice_fusion), channel_id=1, source_target_pairs={{0,16},{16,32},{32,48},{48,64},{64,80},{80,96},{96,112},{112,128},... | collective-permute-start | bytes 3145736 | tf_op jit(solution)/shard_map/ppermute | solution.py:20
  48.1 3.1 %all-to-all-done = bf16[8,256,128]{2,1,0:T(8,128)(2,1)S(1)} async-done(((bf16[8,256,128]{2,1,0:T(8,128)(2,1)}), bf16[8,256,128]{2,1,0:T(8,128)(2,1)S(1)}, u32[]{:S(2)}, u32[]{:S(2)}) %all-to-all-start) | async-done | bytes 524320 | tf_op jit(solution)/shard_map/all_to_all | solution.py:32
  51.2 1.3 collective-permute-start.5
  54.1 2.1 fusion.67
  56.2 2.2 fusion.106
  58.9 2.0 convolution_select_fusion.2
  61.6 1.4 convolution_convert_fusion.5
  63.0 7.1 %collective-permute-start.6 = (bf16[64,1024]{1,0:T(8,128)(2,1)S(1)}, bf16[64,1024]{1,0:T(8,128)(2,1)S(1)}, u32[]{:S(2)}, u32[]{:S(2)}) collective-permute-start(bf16[64,1024]{1,0:T(8,128)(2,1)S(1)} %convolution_convert_fusion.5), channel_id=1, source_target_pairs={{0,240},{16,0},{32,16},{48,32},{64,48},{80,64},{96,80},{112,96},{1... | collective-permute-start | bytes 393224 | tf_op jit(solution)/shard_map/ppermute | solution.py:20
  70.1 1.3 collective-permute-start.7
  71.4 1.3 collective-permute-start.9
  73.0 4.7 %collective-permute-done.7 = bf16[64,1024]{1,0:T(8,128)(2,1)S(1)} collective-permute-done((bf16[64,1024]{1,0:T(8,128)(2,1)S(1)}, bf16[64,1024]{1,0:T(8,128)(2,1)S(1)}, u32[]{:S(2)}, u32[]{:S(2)}) %collective-permute-start.7) | collective-permute-done | bytes 131104 | tf_op jit(solution)/shard_map/ppermute | solution.py:20
  80.0 5.3 %all-to-all-start.1 = ((bf16[8,64,128]{2,1,0:T(8,128)(2,1)}), bf16[8,64,128]{2,1,0:T(8,128)(2,1)S(1)}, u32[]{:S(2)}, u32[]{:S(2)}) async-start(bf16[8,64,128]{2,1,0:T(8,128)(2,1)} %bitcast_bitcast_fusion.5), calls=%async_computation.1 | async-start | bytes 262144 | tf_op jit(solution)/shard_map/all_to_all | solution.py:32
  85.4 2.5 %convolution_convert_fusion.1 = bf16[1024,512]{1,0:T(8,128)(2,1)S(1)} fusion(bf16[1024,1024]{1,0:T(8,128)(2,1)S(1)} %fusion.19, bf16[1024,512]{1,0:T(8,128)(2,1)} %collective-permute-done.8), kind=kOutput, calls=%fused_computation.24 | convolution fusion | flops 1074266112 | bytes 4194304 | tf_op jit(solution)/shard_map/dot_general | solution.py:12
  87.8 5.6 %all-to-all-done.1 = bf16[8,64,128]{2,1,0:T(8,128)(2,1)S(1)} async-done(((bf16[8,64,128]{2,1,0:T(8,128)(2,1)}), bf16[8,64,128]{2,1,0:T(8,128)(2,1)S(1)}, u32[]{:S(2)}, u32[]{:S(2)}) %all-to-all-start.1) | async-done | bytes 131104 | tf_op jit(solution)/shard_map/all_to_all | solution.py:32
  93.4 2.5 %collective-permute-start.10 = (bf16[8,64,128]{2,1,0:T(8,128)(2,1)S(1)}, bf16[8,64,128]{2,1,0:T(8,128)(2,1)S(1)}, u32[]{:S(2)}, u32[]{:S(2)}) collective-permute-start(bf16[8,64,128]{2,1,0:T(8,128)(2,1)S(1)} %all-to-all-done.1), channel_id=1, source_target_pairs={{0,8},{8,0},{1,9},{9,1},{2,10},{10,2},{3,11},{11,3},{4,12},{12,4},... | collective-permute-start | bytes 393224 | tf_op jit(solution)/shard_map/ppermute | solution.py:24
  97.0 1.5 add_convert_fusion.2
  99.3 10.4 %collective-permute-done.12 = bf16[64,1024]{1,0:T(8,128)(2,1)S(1)} collective-permute-done((bf16[64,1024]{1,0:T(8,128)(2,1)S(1)}, bf16[64,1024]{1,0:T(8,128)(2,1)S(1)}, u32[]{:S(2)}, u32[]{:S(2)}) %collective-permute-start.12) | collective-permute-done | bytes 131104 | tf_op jit(solution)/shard_map/ppermute | solution.py:20
  110.4 11.4 %all_to_all.30 = bf16[8,64,128]{2,1,0:T(8,128)(2,1)S(1)} all-to-all(bf16[8,64,128]{2,1,0:T(8,128)(2,1)S(1)} %bitcast_bitcast_fusion.4), channel_id=1, replica_groups=mesh['y'=4,'x'=4,'core'=2,'z'=8] {'z'}, dimensions={0} | all-to-all | bytes 262144 | tf_op jit(solution)/shard_map/all_to_all | solution.py:32
  121.7 2.0 collective-permute-start.14
  125.8 4.9 %collective-permute-start.15 = (bf16[64,1024]{1,0:T(8,128)(2,1)S(1)}, bf16[64,1024]{1,0:T(8,128)(2,1)S(1)}, u32[]{:S(2)}, u32[]{:S(2)}) collective-permute-start(bf16[64,1024]{1,0:T(8,128)(2,1)S(1)} %fusion.78), channel_id=1, source_target_pairs={{80,240},{96,0},{112,16},{128,32},{144,48},{160,64},{176,80},{192,... | collective-permute-start | bytes 393224 | tf_op jit(solution)/shard_map/ppermute | solution.py:20
  130.7 4.1 %collective-permute-start.16 = (bf16[64,1024]{1,0:T(8,128)(2,1)S(1)}, bf16[64,1024]{1,0:T(8,128)(2,1)S(1)}, u32[]{:S(2)}, u32[]{:S(2)}) collective-permute-start(bf16[64,1024]{1,0:T(8,128)(2,1)S(1)} %fusion.78), channel_id=1, source_target_pairs={{16,240},{32,0},{48,16},{64,32},{80,48},{96,64},{112,80},{128,96},... | collective-permute-start | bytes 393224 | tf_op jit(solution)/shard_map/ppermute | solution.py:20
  134.8 4.0 %slice_bitcast_fusion = (bf16[1024,1024]{1,0:T(8,128)(2,1)}, bf16[1024,1024]{1,0:T(8,128)(2,1)S(1)}) fusion(bf16[2,1024,1024]{2,1,0:T(8,128)(2,1)} %all-gather.2.cloned.1.call-done), kind=kLoop, calls=%fused_computation | loop fusion | bytes 8388608 | tf_op jit(solution)/shard_map/squeeze | solution.py:121
  140.0 3.4 %all-to-all-start.3 = ((bf16[8,64,128]{2,1,0:T(8,128)(2,1)}), bf16[8,64,128]{2,1,0:T(8,128)(2,1)S(1)}, u32[]{:S(2)}, u32[]{:S(2)}) async-start(bf16[8,64,128]{2,1,0:T(8,128)(2,1)} %bitcast_bitcast_fusion.3), calls=%async_computation.3 | async-start | bytes 262144 | tf_op jit(solution)/shard_map/all_to_all | solution.py:32
  143.3 5.3 %convolution_convert_fusion = bf16[1024,1024]{1,0:T(8,128)(2,1)} fusion(bf16[1024,1024]{1,0:T(8,128)(2,1)} %get-tuple-element.37, bf16[1024,1024]{1,0:T(8,128)(2,1)S(1)} %get-tuple-element.35), kind=kOutput, calls=%fused_computation.23 | convolution fusion | flops 2148532224 | bytes 6291456 | tf_op jit(solution)/shard_map/dot_general | solution.py:12
  148.6 2.4 %all-to-all-done.3 = bf16[8,64,128]{2,1,0:T(8,128)(2,1)S(1)} async-done(((bf16[8,64,128]{2,1,0:T(8,128)(2,1)}), bf16[8,64,128]{2,1,0:T(8,128)(2,1)S(1)}, u32[]{:S(2)}, u32[]{:S(2)}) %all-to-all-start.3) | async-done | bytes 131104 | tf_op jit(solution)/shard_map/all_to_all | solution.py:32
  151.0 2.3 %collective-permute-start.17 = (bf16[8,64,128]{2,1,0:T(8,128)(2,1)S(1)}, bf16[8,64,128]{2,1,0:T(8,128)(2,1)S(1)}, u32[]{:S(2)}, u32[]{:S(2)}) collective-permute-start(bf16[8,64,128]{2,1,0:T(8,128)(2,1)S(1)} %all-to-all-done.3), channel_id=1, source_target_pairs={{0,8},{8,0},{1,9},{9,1},{2,10},{10,2},{3,11},{11,3},{4,12},{12,4},... | collective-permute-start | bytes 393224 | tf_op jit(solution)/shard_map/ppermute | solution.py:24
  155.0 1.4 collective-permute-start.18
  156.4 6.8 %collective-permute-done.18 = bf16[64,1024]{1,0:T(8,128)(2,1)S(1)} collective-permute-done((bf16[64,1024]{1,0:T(8,128)(2,1)S(1)}, bf16[64,1024]{1,0:T(8,128)(2,1)S(1)}, u32[]{:S(2)}, u32[]{:S(2)}) %collective-permute-start.18) | collective-permute-done | bytes 131104 | tf_op jit(solution)/shard_map/ppermute | solution.py:20
  163.8 11.0 %all_to_all.31 = bf16[8,64,128]{2,1,0:T(8,128)(2,1)S(1)} all-to-all(bf16[8,64,128]{2,1,0:T(8,128)(2,1)S(1)} %bitcast_bitcast_fusion.2), channel_id=1, replica_groups=mesh['y'=4,'x'=4,'core'=2,'z'=8] {'z'}, dimensions={0} | all-to-all | bytes 262144 | tf_op jit(solution)/shard_map/all_to_all | solution.py:32
  174.8 2.5 %collective-permute-start.19 = (bf16[8,64,128]{2,1,0:T(8,128)(2,1)S(1)}, bf16[8,64,128]{2,1,0:T(8,128)(2,1)S(1)}, u32[]{:S(2)}, u32[]{:S(2)}) collective-permute-start(bf16[8,64,128]{2,1,0:T(8,128)(2,1)S(1)} %all_to_all.31), channel_id=1, source_target_pairs={{0,8},{8,0},{1,9},{9,1},{2,10},{10,2},{3,11},{11,3},{4,12},{12,4},... | collective-permute-start | bytes 393224 | tf_op jit(solution)/shard_map/ppermute | solution.py:24
  179.5 2.1 collective-permute-start.22
  182.0 2.3 %fusion.60 = bf16[128,1024]{1,0:T(8,128)(2,1)S(1)} fusion(bf16[128,1024]{1,0:T(8,128)(2,1)S(1)} %fusion.103, bf16[1024,1024]{1,0:T(8,128)(2,1)} %collective-permute-done.1, pred[]{:T(512)S(6)} %eq.4, bf16[64,1024]{1,0:T(8,128)(2,1)S(1)} %collective-permute-done.23, bf16[64,1024]{1,0:T(8,128)(2,1)S(1)} %get-tuple-element.57), kind=kOutput, calls=%fused_computation.47 | convolution fusion | flops 269746176 | bytes 2883585 | tf_op jit(solution)/shard_map/dot_general | solution.py:12
  186.3 3.7 %all-to-all-start.5 = ((bf16[8,256,128]{2,1,0:T(8,128)(2,1)}), bf16[8,256,128]{2,1,0:T(8,128)(2,1)S(1)}, u32[]{:S(2)}, u32[]{:S(2)}) async-start(bf16[8,256,128]{2,1,0:T(8,128)(2,1)} %bitcast_bitcast_fusion), calls=%async_computation.5 | async-start | bytes 1048576 | tf_op jit(solution)/shard_map/all_to_all | solution.py:32
  190.1 8.5 %collective-permute-done.20 = bf16[64,1024]{1,0:T(8,128)(2,1)S(1)} collective-permute-done((bf16[64,1024]{1,0:T(8,128)(2,1)S(1)}, bf16[64,1024]{1,0:T(8,128)(2,1)S(1)}, u32[]{:S(2)}, u32[]{:S(2)}) %collective-permute-start.20) | collective-permute-done | bytes 131104 | tf_op jit(solution)/shard_map/ppermute | solution.py:20
  199.0 8.9 %all-to-all-done.5 = bf16[8,256,128]{2,1,0:T(8,128)(2,1)S(1)} async-done(((bf16[8,256,128]{2,1,0:T(8,128)(2,1)}), bf16[8,256,128]{2,1,0:T(8,128)(2,1)S(1)}, u32[]{:S(2)}, u32[]{:S(2)}) %all-to-all-start.5) | async-done | bytes 524320 | tf_op jit(solution)/shard_map/all_to_all | solution.py:32
  208.7 2.1 convolution_select_fusion
  210.7 2.1 fusion.61
  (107 shorter events, 24.5 us)
Async XLA Ops:
  6.5 8.0 %copy-start.7 = (bf16[2,1024,128]{2,1,0:T(8,128)(2,1)S(1)}, bf16[2,1024,128]{2,1,0:T(8,128)(2,1)}, u32[]{:S(2)}) copy-start(bf16[2,1024,128]{2,1,0:T(8,128)(2,1)} %param.2) | copy-start | bytes 1572868
  11.2 7.4 %copy-start.2 = (bf16[1024,1024]{1,0:T(8,128)(2,1)}, bf16[1024,1024]{1,0:T(8,128)(2,1)S(1)}, u32[]{:S(2)}) copy-start(bf16[1024,1024]{1,0:T(8,128)(2,1)S(1)} %fusion.24) | copy-start | bytes 6291460
  11.2 7.4 %collective-permute-start.1 = (bf16[1024,1024]{1,0:T(8,128)(2,1)S(1)}, bf16[1024,1024]{1,0:T(8,128)(2,1)}, u32[]{:S(2)}, u32[]{:S(2)}) collective-permute-start(bf16[1024,1024]{1,0:T(8,128)(2,1)S(1)} %fusion.24), channel_id=1, source_target_pairs={{0,8},{8,0},{1,9},{9,1},{2,10},{10,2},{3,11},{11,3},{4,12},{12,4},... | collective-permute-start | bytes 6291464 | tf_op jit(solution)/shard_map/ppermute | solution.py:24
  14.5 10.9 %collective-permute-start = (bf16[1024,128]{1,0:T(8,128)(2,1)S(1)}, bf16[1024,128]{1,0:T(8,128)(2,1)S(1)}, u32[]{:S(2)}, u32[]{:S(2)}) collective-permute-start(bf16[1024,128]{1,0:T(8,128)(2,1)S(1)} %slice_bitcast_fusion.4), channel_id=1, source_target_pairs={{8,0},{9,1},{10,2},{11,3},{12,4},{13,5},{14,6},{15,7},{24,16},{25,... | collective-permute-start | bytes 786440 | tf_op jit(solution)/shard_map/ppermute | solution.py:57
  23.2 2.2 %copy-start.3 = (bf16[1024,1024]{1,0:T(8,128)(2,1)S(1)}, bf16[1024,1024]{1,0:T(8,128)(2,1)}, u32[]{:S(2)}) copy-start(bf16[1024,1024]{1,0:T(8,128)(2,1)} %copy-done.2) | copy-start | bytes 6291460
  26.8 24.4 %all-to-all-start = ((bf16[8,256,128]{2,1,0:T(8,128)(2,1)}), bf16[8,256,128]{2,1,0:T(8,128)(2,1)S(1)}, u32[]{:S(2)}, u32[]{:S(2)}) async-start(bf16[8,256,128]{2,1,0:T(8,128)(2,1)} %bitcast_bitcast_fusion.1), calls=%async_computation | async-start | bytes 1048576 | tf_op jit(solution)/shard_map/all_to_all | solution.py:32
  33.3 101.5 %all-gather.2.cloned.1.call-start = ((), (), s32[]{:S(2)}) async-start(), calls=%async_computation.6 | async-start | bytes 4456448 | tf_op jit(solution)/shard_map/all_gather | solution.py:102
  33.3 6.5 %collective-permute-start.2 = (bf16[64,1024]{1,0:T(8,128)(2,1)S(1)}, bf16[64,1024]{1,0:T(8,128)(2,1)S(1)}, u32[]{:S(2)}, u32[]{:S(2)}) collective-permute-start(bf16[64,1024]{1,0:T(8,128)(2,1)S(1)} %constant_dynamic-slice_fusion.2), channel_id=1, source_target_pairs={{16,0},{32,16},{48,32},{64,48},{80,64},{96,80},{112,96},{128,112},... | collective-permute-start | bytes 393224 | tf_op jit(solution)/shard_map/ppermute | solution.py:20
  40.3 7.4 %collective-permute-start.3 = (bf16[64,1024]{1,0:T(8,128)(2,1)S(1)}, bf16[64,1024]{1,0:T(8,128)(2,1)S(1)}, u32[]{:S(2)}, u32[]{:S(2)}) collective-permute-start(bf16[64,1024]{1,0:T(8,128)(2,1)S(1)} %convolution_convert_fusion.7), channel_id=1, source_target_pairs={{16,0},{32,16},{48,32},{64,48},{80,64},{96,80},{112,96},{128,112},... | collective-permute-start | bytes 393224 | tf_op jit(solution)/shard_map/ppermute | solution.py:20
  42.7 30.0 %collective-permute-start.8 = (bf16[1024,512]{1,0:T(8,128)(2,1)}, bf16[1024,512]{1,0:T(8,128)(2,1)}, u32[]{:S(2)}, u32[]{:S(2)}) collective-permute-start(bf16[1024,512]{1,0:T(8,128)(2,1)} %constant_dynamic-slice_fusion), channel_id=1, source_target_pairs={{0,16},{16,32},{32,48},{48,64},{64,80},{80,96},{96,112},{112,128},... | collective-permute-start | bytes 3145736 | tf_op jit(solution)/shard_map/ppermute | solution.py:20
  51.2 10.3 %collective-permute-start.5 = (bf16[64,1024]{1,0:T(8,128)(2,1)S(1)}, bf16[64,1024]{1,0:T(8,128)(2,1)}, u32[]{:S(2)}, u32[]{:S(2)}) collective-permute-start(bf16[64,1024]{1,0:T(8,128)(2,1)S(1)} %convolution_convert_fusion.6), channel_id=1, source_target_pairs={{16,0},{32,16},{48,32},{64,48},{80,64},{96,80},{112,96},{128,112},... | collective-permute-start | bytes 393224 | tf_op jit(solution)/shard_map/ppermute | solution.py:20
  52.5 3.7 %copy-start.8 = (bf16[2,1024,128]{1,2,0:T(8,128)(2,1)S(1)}, bf16[2,1024,128]{1,2,0:T(8,128)(2,1)}, u32[]{:S(2)}) copy-start(bf16[2,1024,128]{1,2,0:T(8,128)(2,1)} %copy.22) | copy-start | bytes 1572868
  53.3 3.0 %copy-start.11 = (bf16[8,1,128,128]{3,2,1,0:T(8,128)(2,1)S(1)}, bf16[8,1,128,128]{3,2,1,0:T(8,128)(2,1)}, u32[]{:S(2)}) copy-start(bf16[8,1,128,128]{3,2,1,0:T(8,128)(2,1)} %get-tuple-element.46) | copy-start | bytes 786436
  56.2 2.2 %copy-start.4 = (bf16[1024,1024]{1,0:T(8,128)(2,1)S(1)}, bf16[1024,1024]{1,0:T(8,128)(2,1)}, u32[]{:S(2)}) copy-start(bf16[1024,1024]{1,0:T(8,128)(2,1)} %copy-done.2) | copy-start | bytes 6291460
  61.0 10.4 %collective-permute-start.4 = (f32[64,1024]{1,0:T(8,128)S(1)}, f32[64,1024]{1,0:T(8,128)S(1)}, u32[]{:S(2)}, u32[]{:S(2)}) collective-permute-start(f32[64,1024]{1,0:T(8,128)S(1)} %constant_dynamic-slice_fusion.1), channel_id=1, source_target_pairs={{0,8},{8,0},{1,9},{9,1},{2,10},{10,2},{3,11},{11,3},{4,12},{12,4},... | collective-permute-start | bytes 786440 | tf_op jit(solution)/shard_map/ppermute | solution.py:24
  63.0 10.0 %collective-permute-start.6 = (bf16[64,1024]{1,0:T(8,128)(2,1)S(1)}, bf16[64,1024]{1,0:T(8,128)(2,1)S(1)}, u32[]{:S(2)}, u32[]{:S(2)}) collective-permute-start(bf16[64,1024]{1,0:T(8,128)(2,1)S(1)} %convolution_convert_fusion.5), channel_id=1, source_target_pairs={{0,240},{16,0},{32,16},{48,32},{64,48},{80,64},{96,80},{112,96},{1... | collective-permute-start | bytes 393224 | tf_op jit(solution)/shard_map/ppermute | solution.py:20
  70.1 7.6 %collective-permute-start.7 = (bf16[64,1024]{1,0:T(8,128)(2,1)S(1)}, bf16[64,1024]{1,0:T(8,128)(2,1)S(1)}, u32[]{:S(2)}, u32[]{:S(2)}) collective-permute-start(bf16[64,1024]{1,0:T(8,128)(2,1)S(1)} %convolution_convert_fusion.5), channel_id=1, source_target_pairs={{64,240},{80,0},{96,16},{112,32},{128,48},{144,64},{160,80},{176,9... | collective-permute-start | bytes 393224 | tf_op jit(solution)/shard_map/ppermute | solution.py:20
  71.4 7.4 %copy-start.12 = (bf16[64,1024]{1,0:T(8,128)(2,1)}, bf16[64,1024]{1,0:T(8,128)(2,1)S(1)}, u32[]{:S(2)}) copy-start(bf16[64,1024]{1,0:T(8,128)(2,1)S(1)} %add_convert_fusion.3) | copy-start | bytes 393220
  71.4 6.7 %collective-permute-start.9 = (bf16[64,1024]{1,0:T(8,128)(2,1)S(1)}, bf16[64,1024]{1,0:T(8,128)(2,1)S(1)}, u32[]{:S(2)}, u32[]{:S(2)}) collective-permute-start(bf16[64,1024]{1,0:T(8,128)(2,1)S(1)} %add_convert_fusion.3), channel_id=1, source_target_pairs={{16,0},{32,16},{48,32},{64,48},{80,64},{96,80},{112,96},{128,112},... | collective-permute-start | bytes 393224 | tf_op jit(solution)/shard_map/ppermute | solution.py:20
  80.0 13.4 %all-to-all-start.1 = ((bf16[8,64,128]{2,1,0:T(8,128)(2,1)}), bf16[8,64,128]{2,1,0:T(8,128)(2,1)S(1)}, u32[]{:S(2)}, u32[]{:S(2)}) async-start(bf16[8,64,128]{2,1,0:T(8,128)(2,1)} %bitcast_bitcast_fusion.5), calls=%async_computation.1 | async-start | bytes 262144 | tf_op jit(solution)/shard_map/all_to_all | solution.py:32
  93.4 3.5 %collective-permute-start.10 = (bf16[8,64,128]{2,1,0:T(8,128)(2,1)S(1)}, bf16[8,64,128]{2,1,0:T(8,128)(2,1)S(1)}, u32[]{:S(2)}, u32[]{:S(2)}) collective-permute-start(bf16[8,64,128]{2,1,0:T(8,128)(2,1)S(1)} %all-to-all-done.1), channel_id=1, source_target_pairs={{0,8},{8,0},{1,9},{9,1},{2,10},{10,2},{3,11},{11,3},{4,12},{12,4},... | collective-permute-start | bytes 393224 | tf_op jit(solution)/shard_map/ppermute | solution.py:24
  95.9 14.1 %collective-permute-start.13 = (bf16[1024,512]{1,0:T(8,128)(2,1)S(1)}, bf16[1024,512]{1,0:T(8,128)(2,1)S(1)}, u32[]{:S(2)}, u32[]{:S(2)}) collective-permute-start(bf16[1024,512]{1,0:T(8,128)(2,1)S(1)} %convolution_convert_fusion.1), channel_id=1, source_target_pairs={{0,8},{8,0},{1,9},{9,1},{2,10},{10,2},{3,11},{11,3},{4,12},{12,4},... | collective-permute-start | bytes 3145736 | tf_op jit(solution)/shard_map/ppermute | solution.py:24
  98.5 0.8 collective-permute-start.11
  99.2 10.5 %collective-permute-start.12 = (bf16[64,1024]{1,0:T(8,128)(2,1)S(1)}, bf16[64,1024]{1,0:T(8,128)(2,1)S(1)}, u32[]{:S(2)}, u32[]{:S(2)}) collective-permute-start(bf16[64,1024]{1,0:T(8,128)(2,1)S(1)} %add_convert_fusion.2), channel_id=1, source_target_pairs={{0,16},{16,32},{32,48},{48,64},{64,80},{80,96},{96,112},{112,128},... | collective-permute-start | bytes 393224 | tf_op jit(solution)/shard_map/ppermute | solution.py:20
  121.7 3.0 %collective-permute-start.14 = (bf16[8,64,128]{2,1,0:T(8,128)(2,1)S(1)}, bf16[8,64,128]{2,1,0:T(8,128)(2,1)S(1)}, u32[]{:S(2)}, u32[]{:S(2)}) collective-permute-start(bf16[8,64,128]{2,1,0:T(8,128)(2,1)S(1)} %all_to_all.30), channel_id=1, source_target_pairs={{0,8},{8,0},{1,9},{9,1},{2,10},{10,2},{3,11},{11,3},{4,12},{12,4},... | collective-permute-start | bytes 393224 | tf_op jit(solution)/shard_map/ppermute | solution.py:24
  125.8 13.0 %collective-permute-start.15 = (bf16[64,1024]{1,0:T(8,128)(2,1)S(1)}, bf16[64,1024]{1,0:T(8,128)(2,1)S(1)}, u32[]{:S(2)}, u32[]{:S(2)}) collective-permute-start(bf16[64,1024]{1,0:T(8,128)(2,1)S(1)} %fusion.78), channel_id=1, source_target_pairs={{80,240},{96,0},{112,16},{128,32},{144,48},{160,64},{176,80},{192,... | collective-permute-start | bytes 393224 | tf_op jit(solution)/shard_map/ppermute | solution.py:20
  130.7 17.9 %collective-permute-start.16 = (bf16[64,1024]{1,0:T(8,128)(2,1)S(1)}, bf16[64,1024]{1,0:T(8,128)(2,1)S(1)}, u32[]{:S(2)}, u32[]{:S(2)}) collective-permute-start(bf16[64,1024]{1,0:T(8,128)(2,1)S(1)} %fusion.78), channel_id=1, source_target_pairs={{16,240},{32,0},{48,16},{64,32},{80,48},{96,64},{112,80},{128,96},... | collective-permute-start | bytes 393224 | tf_op jit(solution)/shard_map/ppermute | solution.py:20
  140.0 11.1 %all-to-all-start.3 = ((bf16[8,64,128]{2,1,0:T(8,128)(2,1)}), bf16[8,64,128]{2,1,0:T(8,128)(2,1)S(1)}, u32[]{:S(2)}, u32[]{:S(2)}) async-start(bf16[8,64,128]{2,1,0:T(8,128)(2,1)} %bitcast_bitcast_fusion.3), calls=%async_computation.3 | async-start | bytes 262144 | tf_op jit(solution)/shard_map/all_to_all | solution.py:32
  151.0 12.2 %copy-start = (bf16[1024,1024]{1,0:T(8,128)(2,1)S(1)}, bf16[1024,1024]{1,0:T(8,128)(2,1)}, u32[]{:S(2)}) copy-start(bf16[1024,1024]{1,0:T(8,128)(2,1)} %convolution_convert_fusion) | copy-start | bytes 6291460
  151.0 3.3 %collective-permute-start.17 = (bf16[8,64,128]{2,1,0:T(8,128)(2,1)S(1)}, bf16[8,64,128]{2,1,0:T(8,128)(2,1)S(1)}, u32[]{:S(2)}, u32[]{:S(2)}) collective-permute-start(bf16[8,64,128]{2,1,0:T(8,128)(2,1)S(1)} %all-to-all-done.3), channel_id=1, source_target_pairs={{0,8},{8,0},{1,9},{9,1},{2,10},{10,2},{3,11},{11,3},{4,12},{12,4},... | collective-permute-start | bytes 393224 | tf_op jit(solution)/shard_map/ppermute | solution.py:24
  155.0 23.4 %copy-start.1 = (bf16[1024,1024]{1,0:T(8,128)(2,1)S(1)}, bf16[1024,1024]{1,0:T(8,128)(2,1)}, u32[]{:S(2)}) copy-start(bf16[1024,1024]{1,0:T(8,128)(2,1)} %convolution_convert_fusion) | copy-start | bytes 6291460
  155.0 8.3 %collective-permute-start.18 = (bf16[64,1024]{1,0:T(8,128)(2,1)S(1)}, bf16[64,1024]{1,0:T(8,128)(2,1)S(1)}, u32[]{:S(2)}, u32[]{:S(2)}) collective-permute-start(bf16[64,1024]{1,0:T(8,128)(2,1)S(1)} %add_convert_fusion.1), channel_id=1, source_target_pairs={{112,240},{128,0},{144,16},{160,32},{176,48},{192,64},{208,80},{22... | collective-permute-start | bytes 393224 | tf_op jit(solution)/shard_map/ppermute | solution.py:20
  174.8 3.5 %collective-permute-start.19 = (bf16[8,64,128]{2,1,0:T(8,128)(2,1)S(1)}, bf16[8,64,128]{2,1,0:T(8,128)(2,1)S(1)}, u32[]{:S(2)}, u32[]{:S(2)}) collective-permute-start(bf16[8,64,128]{2,1,0:T(8,128)(2,1)S(1)} %all_to_all.31), channel_id=1, source_target_pairs={{0,8},{8,0},{1,9},{9,1},{2,10},{10,2},{3,11},{11,3},{4,12},{12,4},... | collective-permute-start | bytes 393224 | tf_op jit(solution)/shard_map/ppermute | solution.py:24
  177.3 4.3 %copy-start.5 = (bf16[1024,1024]{1,0:T(8,128)(2,1)S(1)}, bf16[1024,1024]{1,0:T(8,128)(2,1)}, u32[]{:S(2)}) copy-start(bf16[1024,1024]{1,0:T(8,128)(2,1)} %copy-done.2) | copy-start | bytes 6291460
  179.0 2.5 %collective-permute-start.23 = (bf16[64,1024]{1,0:T(8,128)(2,1)S(1)}, bf16[64,1024]{1,0:T(8,128)(2,1)S(1)}, u32[]{:S(2)}, u32[]{:S(2)}) collective-permute-start(bf16[64,1024]{1,0:T(8,128)(2,1)S(1)} %get-tuple-element.57), channel_id=1, source_target_pairs={{0,8},{8,0},{1,9},{9,1},{2,10},{10,2},{3,11},{11,3},{4,12},{12,4},... | collective-permute-start | bytes 393224 | tf_op jit(solution)/shard_map/ppermute | solution.py:24
  179.5 4.8 %collective-permute-start.22 = (bf16[128,1024]{1,0:T(8,128)(2,1)S(1)}, bf16[128,1024]{1,0:T(8,128)(2,1)S(1)}, u32[]{:S(2)}, u32[]{:S(2)}) collective-permute-start(bf16[128,1024]{1,0:T(8,128)(2,1)S(1)} %get-tuple-element.55), channel_id=1, source_target_pairs={{8,0},{9,1},{10,2},{11,3},{12,4},{13,5},{14,6},{15,7},{24,16},{25,... | collective-permute-start | bytes 786440 | tf_op jit(solution)/shard_map/ppermute | solution.py:134
  181.6 2.8 %copy-start.10 = (bf16[2,1024,1024]{2,1,0:T(8,128)(2,1)S(1)}, bf16[2,1024,1024]{2,1,0:T(8,128)(2,1)}, u32[]{:S(2)}) copy-start(bf16[2,1024,1024]{2,1,0:T(8,128)(2,1)} %param.3) | copy-start | bytes 12582916
  185.3 22.5 %copy-start.6 = (bf16[1024,1024]{1,0:T(8,128)(2,1)S(1)}, bf16[1024,1024]{1,0:T(8,128)(2,1)}, u32[]{:S(2)}) copy-start(bf16[1024,1024]{1,0:T(8,128)(2,1)} %copy-done.2) | copy-start | bytes 6291460
  186.3 21.6 %all-to-all-start.5 = ((bf16[8,256,128]{2,1,0:T(8,128)(2,1)}), bf16[8,256,128]{2,1,0:T(8,128)(2,1)S(1)}, u32[]{:S(2)}, u32[]{:S(2)}) async-start(bf16[8,256,128]{2,1,0:T(8,128)(2,1)} %bitcast_bitcast_fusion), calls=%async_computation.5 | async-start | bytes 1048576 | tf_op jit(solution)/shard_map/all_to_all | solution.py:32
  190.0 8.6 %collective-permute-start.20 = (bf16[64,1024]{1,0:T(8,128)(2,1)S(1)}, bf16[64,1024]{1,0:T(8,128)(2,1)S(1)}, u32[]{:S(2)}, u32[]{:S(2)}) collective-permute-start(bf16[64,1024]{1,0:T(8,128)(2,1)S(1)} %get-tuple-element.58), channel_id=1, source_target_pairs={{0,16},{16,32},{32,48},{48,64},{64,80},{80,96},{96,112},{112,128},... | collective-permute-start | bytes 393224 | tf_op jit(solution)/shard_map/ppermute | solution.py:20
  198.6 14.2 %collective-permute-start.21 = (bf16[64,1024]{1,0:T(8,128)(2,1)S(1)}, bf16[64,1024]{1,0:T(8,128)(2,1)}, u32[]{:S(2)}, u32[]{:S(2)}) collective-permute-start(bf16[64,1024]{1,0:T(8,128)(2,1)S(1)} %collective-permute-done.20), channel_id=1, source_target_pairs={{0,8},{8,0},{1,9},{9,1},{2,10},{10,2},{3,11},{11,3},{4,12},{12,4},... | collective-permute-start | bytes 393224 | tf_op jit(solution)/shard_map/ppermute | solution.py:24
  208.5 2.2 %copy-start.9 = (bf16[2,1024,128]{1,2,0:T(8,128)(2,1)S(1)}, bf16[2,1024,128]{1,2,0:T(8,128)(2,1)}, u32[]{:S(2)}) copy-start(bf16[2,1024,128]{1,2,0:T(8,128)(2,1)} %copy.22) | copy-start | bytes 1572868
Sparse Core Ops, SparseCore 0:
  79.0 45.0 all-gather.1

commit v3 on v2

v3 whole, which is shorter than its diff:
```python
import jax
import jax.numpy as jnp
from jax import lax
from jax.experimental import pallas as pl
from jax.experimental.pallas import tpu as pltpu
from jax.sharding import Mesh, PartitionSpec as P

BF16 = jnp.bfloat16
F32 = jnp.float32
CHIPS = ("y", "x")
VMEM = 60 * 2**20


def dot(left, right):
    return jnp.dot(left, right, preferred_element_type=F32)


def moved(block, pairs):
    return lax.ppermute(block, CHIPS, pairs)


def from_other_core(block):
    return lax.ppermute(block, "core", [(0, 1), (1, 0)])


def turned(rows):
    slabs = lax.axis_size("z")
    m, n = rows.shape
    rows = lax.optimization_barrier(rows)
    pieces = rows.reshape(m, slabs, n // slabs).swapaxes(0, 1)
    return lax.all_to_all(pieces, "z", 0, 0, tiled=True)


def fetch(source, target, sem, pieces=8):
    rows = target.shape[0] // pieces
    for i in range(pieces):
        part = pl.ds(i * rows, rows)
        pltpu.make_async_copy(source.at[part], target.at[part], sem).start()


def chip_close(core, got, first_p, coupling, own, other):
    _, order, width = first_p.shape
    slabs = order // width

    def kernel(core_ref, got_ref, p_ref, k_ref, own_ref, other_ref, part_ref, kept_ref,
               sent_ref, k, low, k_sem, low_sem):
        fetch(k_ref.at[0], k, k_sem)

        @pl.when(core_ref[0] == 0)
        def _():
            fetch(own_ref, low, low_sem)

        @pl.when(core_ref[0] == 1)
        def _():
            fetch(other_ref, low, low_sem)

        y_a = got_ref[:, 0].reshape(order, width).T
        y_b = got_ref[:, 1].reshape(order, width).T
        p = p_ref[0].T.astype(F32)
        pltpu.make_async_copy(k_ref.at[0], k, k_sem).wait()
        both = jnp.dot(
            jnp.concatenate([y_a, y_b], axis=0), k[...], preferred_element_type=F32
        )
        base = p + both[:width]
        part_ref[...] = base.astype(BF16)
        low_core = core_ref[0] == 0
        left = jnp.where(low_core, y_b.astype(F32), both[width:]).astype(BF16)
        pltpu.make_async_copy(own_ref, low, low_sem).wait()
        total = jnp.where(low_core, base, 0.0) + jnp.dot(
            left, low[...], preferred_element_type=F32
        )
        top, bottom = total[: width // 2], total[width // 2 :]
        kept_ref[...] = jnp.where(low_core, top, bottom)
        sent_ref[...] = jnp.where(low_core, bottom, top)

    whole = pl.BlockSpec(memory_space=pltpu.VMEM)
    hbm = pl.BlockSpec(memory_space=pl.ANY)
    return pl.pallas_call(
        kernel,
        in_specs=[pl.BlockSpec(memory_space=pltpu.SMEM), whole, whole, hbm, hbm, hbm],
        out_specs=[whole, whole, whole],
        out_shape=[
            jax.ShapeDtypeStruct((width, order), BF16),
            jax.ShapeDtypeStruct((width // 2, order), F32),
            jax.ShapeDtypeStruct((width // 2, order), F32),
        ],
        scratch_shapes=[
            pltpu.VMEM((order, order), BF16),
            pltpu.VMEM((order, order), BF16),
            pltpu.SemaphoreType.DMA,
            pltpu.SemaphoreType.DMA,
        ],
        cost_estimate=pl.CostEstimate(
            flops=width * order**2 // 8, bytes_accessed=order * order // 8, transcendentals=0
        ),
        compiler_params=pltpu.CompilerParams(vmem_limit_bytes=VMEM),
    )(core.reshape(1), got, first_p, coupling, own, other)


def last_close(core, got, start, part, precision_blocks, coupling, own, other):
    _, order, width = precision_blocks.shape

    def kernel(core_ref, got_ref, start_ref, part_ref, p_ref, k_ref, own_ref, other_ref, out_ref,
               k, high, k_sem, high_sem):
        low_core = core_ref[0] == 0

        @pl.when(low_core)
        def _():
            fetch(other_ref, high, high_sem)

        @pl.when(jnp.logical_not(low_core))
        def _():
            fetch(own_ref, high, high_sem)

        fetch(k_ref.at[1], k, k_sem)
        y_a = got_ref[:, 0].reshape(order, width).T
        y_b = got_ref[:, 1].reshape(order, width).T
        left = jnp.where(low_core, y_b.astype(F32), y_a.astype(F32)).astype(BF16)
        pltpu.make_async_copy(own_ref, high, high_sem).wait()
        w = jnp.dot(left, high[...], preferred_element_type=F32)
        q = jnp.where(low_core, y_a.astype(F32) + w, y_b.astype(F32)).astype(BF16)
        pltpu.make_async_copy(k_ref.at[1], k, k_sem).wait()
        second = jnp.dot(q, k[...], preferred_element_type=F32)
        out_ref[1] = (p_ref[0].astype(F32) + second.T).astype(BF16)
        first = jnp.where(low_core, start_ref[...].astype(F32), part_ref[...].astype(F32) + w)
        out_ref[0] = first.astype(BF16).T

    whole = pl.BlockSpec(memory_space=pltpu.VMEM)
    hbm = pl.BlockSpec(memory_space=pl.ANY)
    return pl.pallas_call(
        kernel,
        grid=(1,),
        in_specs=[
            pl.BlockSpec(memory_space=pltpu.SMEM),
            whole,
            whole,
            whole,
            pl.BlockSpec((1, order, width), lambda i: (1, 0, 0)),
            hbm,
            hbm,
            hbm,
        ],
        out_specs=pl.BlockSpec((2, order, width), lambda i: (0, 0, 0)),
        out_shape=jax.ShapeDtypeStruct((2, order, width), BF16),
        scratch_shapes=[
            pltpu.VMEM((order, order), BF16),
            pltpu.VMEM((order, order), BF16),
            pltpu.SemaphoreType.DMA,
            pltpu.SemaphoreType.DMA,
        ],
        cost_estimate=pl.CostEstimate(
            flops=4 * width * order**2, bytes_accessed=5 * order * order, transcendentals=0
        ),
        compiler_params=pltpu.CompilerParams(vmem_limit_bytes=VMEM),
    )(core.reshape(1), got, start, part, precision_blocks, coupling, own, other)


def shards(precision_blocks, coupling):
    core = lax.axis_index("core")
    slab = lax.axis_index("z")
    chip = lax.axis_index(CHIPS)
    chips = lax.axis_size(CHIPS)
    order, width = precision_blocks.shape[1:]
    half = width // 2

    def side(a, b):
        return jnp.where(core == 0, a, b)

    def half_rows(block, which):
        return lax.dynamic_slice_in_dim(block, which * half, half, 0)

    def both_halves(block):
        far = from_other_core(block)
        return side(jnp.concatenate([block, far], axis=0), jnp.concatenate([far, block], axis=0))

    def later(distance):
        return [(i + distance, i) for i in range(chips - distance)]

    def ahead_by(distance):
        return [((e + distance), (e - 1) % chips) for e in range(chips - distance)]

    p_high = lax.ppermute(precision_blocks[0], "core", [(1, 0)])
    own = dot(coupling[1], coupling[0]).astype(BF16)
    other = from_other_core(own)
    z_a = lax.dot_general(
        precision_blocks[1], coupling[0], (((0,), (0,)), ((), ())), preferred_element_type=F32
    ).astype(BF16)
    z_b = side(dot(p_high.T, own), dot(z_a, other)).astype(BF16)

    whole = dot(side(other, own), side(own, other)).astype(BF16)
    piece = lax.dynamic_slice_in_dim(whole, slab * width + core * half, half, 0)
    z_b, piece = lax.optimization_barrier((z_b, piece))
    got = turned(jnp.concatenate([z_a, z_b], axis=0))
    piece = dot(moved(piece, later(1)), whole).astype(BF16)
    got, piece = lax.optimization_barrier((got, piece))
    phi2 = lax.all_gather(piece, ("z", "core"), axis=0, tiled=True)
    hop = moved(piece, later(1))

    part, kept, sent = chip_close(
        core, got.reshape(8, 2, width, width), precision_blocks[:1], coupling, own, other
    )
    hop, kept = lax.optimization_barrier((hop, kept))
    piece = dot(hop, whole).astype(BF16)
    piece = dot(moved(piece, later(1)), whole).astype(BF16)
    pieces = [moved(piece, ahead_by(d)) for d in (0, 4, 8)]
    reduced = (kept + from_other_core(sent)).astype(BF16)

    def closed(base, got, times):
        far = from_other_core(got)
        full = jnp.stack([side(got, far), side(far, got)], axis=1).reshape(order, width)
        y = half_rows(full.T, core)
        return (base.astype(F32) + times(y)).astype(BF16)

    times = lambda x: dot(x, whole)
    x = moved(reduced, later(1))
    x, pieces = lax.optimization_barrier((x, pieces))
    gathered = lax.all_gather(jnp.stack(pieces), ("z", "core"), axis=1, tiled=True)
    reduced = closed(reduced, turned(times(x).astype(BF16)), times)
    times = lambda x: dot(x, phi2)
    x = moved(reduced, later(2))
    reduced = closed(reduced, turned(times(x).astype(BF16)), times)

    x1, x2, x3 = (moved(reduced, ahead_by(d)) for d in (4, 8, 12))
    base = moved(reduced, ahead_by(0))
    phis = lax.optimization_barrier((gathered[0], gathered[1], gathered[2]))
    z = dot(x3, phis[2]).astype(BF16)
    z = dot(jnp.concatenate([x2, z], axis=0), phis[1]).astype(BF16)
    z = dot(jnp.concatenate([x1, z], axis=0), phis[0]).astype(BF16)
    got, base = lax.optimization_barrier((turned(z), base))
    far = from_other_core(got)
    full = jnp.stack([side(got, far), side(far, got)], axis=1).reshape(8, 2, 3, half, width)
    y = [half_rows(full[:, :, j].reshape(order, width).T, core) for j in range(3)]
    total = y[2]
    for j in (2, 1):
        total = (dot(total, phis[j]) + y[j - 1].astype(F32)).astype(BF16)
    reduced = (base.astype(F32) + dot(total, phis[0])).astype(BF16)

    start = both_halves(moved(reduced, [(c, (c + 1) % chips) for c in range(chips)]))
    after = both_halves(jnp.where(chip == chips - 1, jnp.zeros_like(reduced), reduced))
    part_high = lax.ppermute(part, "core", [(1, 0)])
    second_k = coupling[1]
    through = side(dot(after, other), dot(after, own)).astype(BF16)
    v = dot(side(part_high, after), second_k).astype(BF16)
    w = dot(through, second_k).astype(BF16)
    got = turned(jnp.concatenate([side(v, through), side(w, v)], axis=0))
    return last_close(
        core,
        got.reshape(8, 2, width, width),
        start,
        part,
        precision_blocks,
        coupling,
        own,
        other,
    )


def solution(mesh):
    grid = Mesh(mesh.devices.reshape(4, 4, 2, 8), ("y", "x", "core", "z"))
    return jax.shard_map(
        shards,
        mesh=grid,
        in_specs=(P(("y", "x", "core"), None, "z"), P(("y", "x", "core"), None, None)),
        out_specs=P(("y", "x", "core"), None, "z"),
        check_vma=False,
    )
```

time: 223 us -> 215 us (0.964)
  matrix products: 44.6 us -> 31.4 us
  Pallas kernels: 0 us -> 10.4 us
  starting transfers between devices: 66.8 us -> 57.3 us
  waiting for transfers between devices: 59.2 us -> 66.7 us
  local copies, waits for them, and re-layouts: 12.5 us -> 9.64 us
    dot_general x30 -> x20, matrix products: 42.6 us -> 29.3 us  [dot(): return jnp.dot(left, right, preferred_element_type=F32)]
    pallas_call x0 -> x2, Pallas kernels: none -> 10.4 us  [the longest x1 5.2 us: last_close(): pl.pallas_call(kernel, grid=(1,), in_specs=[pl.BlockSpec(memory_space=plt...]
    all_gather x1 -> x2, waiting for transfers between devices: 0.01 us -> 5.89 us  [the longest x1 5.88 us: shards(): lax.all_gather(jnp.stack(pieces), ('z', 'core'), axis=1, tiled=True)]
    all_to_all x4 -> x3, waiting for transfers between devices: 19.9 us -> 24.9 us  [turned(): return lax.all_to_all(pieces, 'z', 0, 0, tiled=True)]
    all_to_all x4 -> x3, starting transfers between devices: 18.9 us -> 14 us  [turned(): return lax.all_to_all(pieces, 'z', 0, 0, tiled=True)]
    ppermute x13, waiting for transfers between devices: 35.3 us -> 31.4 us  [moved(): return lax.ppermute(block, CHIPS, pairs)]
    ppermute x13, starting transfers between devices: 29.8 us -> 26.8 us  [moved(): return lax.ppermute(block, CHIPS, pairs)]
    ppermute x9 -> x7, starting transfers between devices: 14.1 us -> 12.3 us  [from_other_core(): return lax.ppermute(block, 'core', [(0, 1), (1, 0)])]
  transfers between devices with their start and end apart: 29 -> 27, of which waited for: 15 -> 16; matrix products, arithmetic and copies ran while one was open for 21% -> 12% of each run, Pallas kernels for 0% -> 2%
where the time goes in v3:
time: 215 us; the launch traced here: 214 us
  waiting for transfers between devices  66.7 us (31%)
  starting transfers between devices  57.3 us (27%)
  matrix products  31.4 us (15%)
  blocking collectives  23 us (11%)
  between operations  14.1 us (7%)
  Pallas kernels  10.4 us (5%)
  local copies, waits for them, and re-layouts  9.64 us (4%)
    ppermute x13, waiting for transfers between devices, moved(): return lax.ppermute(block, CHIPS, pairs)  31.4 us
    dot_general x20, matrix products, dot(): return jnp.dot(left, right, preferred_element_type=F32)  29.3 us
    ppermute x13, starting transfers between devices, moved(): return lax.ppermute(block, CHIPS, pairs)  26.8 us
    all_to_all x3, waiting for transfers between devices, turned(): return lax.all_to_all(pieces, 'z', 0, 0, tiled=True)  24.9 us
    all_to_all x2, blocking collectives, turned(): return lax.all_to_all(pieces, 'z', 0, 0, tiled=True)  23 us
    all_to_all x3, starting transfers between devices, turned(): return lax.all_to_all(pieces, 'z', 0, 0, tiled=True)  14 us
    ppermute x7, starting transfers between devices, from_other_core(): return lax.ppermute(block, 'core', [(0, 1), (1, 0)])  12.3 us
    all_gather x1, waiting for transfers between devices, shards(): lax.all_gather(jnp.stack(pieces), ('z', 'core'), axis=1, tiled=True)  5.88 us
  transfers between devices with their start and end apart: 27, of which 16 were waited for; matrix products, arithmetic and copies ran while one was open for 12% of the time, Pallas kernels for 2%

profile of v3, /device:TPU:1, one launch (start us, length us, event | category | flops | bytes accessed | tf_op | source)
XLA Modules:
  0.0 214.4 jit_solution(6202029479388753113)
XLA Ops:
  6.5 4.6 %fusion.18.own_ref = bf16[1024,1024]{1,0:T(8,128)(2,1)S(1)} fusion(bf16[2,1024,1024]{2,1,0:T(8,128)(2,1)} %k_ref.3), kind=kOutput, calls=%fused_computation.17 | convolution fusion | flops 2148532224 | bytes 6291456 | tf_op jit(solution)/shard_map/dot_general | solution.py:15
  11.2 3.3 %collective-permute-start.1 = (bf16[1024,1024]{1,0:T(8,128)(2,1)S(1)}, bf16[1024,1024]{1,0:T(8,128)(2,1)}, u32[]{:S(2)}, u32[]{:S(2)}) collective-permute-start(bf16[1024,1024]{1,0:T(8,128)(2,1)S(1)} %fusion.18.own_ref), channel_id=1, source_target_pairs={{0,8},{8,0},{1,9},{9,1},{2,10},{10,2},{3,11},{11,3},{4,12},{12,4},... | collective-permute-start | bytes 6291464 | tf_op jit(solution)/shard_map/ppermute | solution.py:23
  15.2 2.1 collective-permute-start
  17.3 2.1 fusion.29
  19.4 4.6 %fusion.13 = bf16[1024,1024]{1,0:T(8,128)(2,1)S(1)} fusion(bf16[1024,1024]{1,0:T(8,128)(2,1)} %copy-done.4, bf16[1024,1024]{1,0:T(8,128)(2,1)} %collective-permute-done.1.other_ref, pred[]{:T(512)S(6)} %eq.4), kind=kOutput, calls=%fused_computation.16 | convolution fusion | flops 2150629376 | bytes 6291457 | tf_op jit(solution)/shard_map/dot_general | solution.py:15
  24.0 2.2 %fusion.74 = bf16[128,1024]{1,0:T(8,128)(2,1)S(1)} fusion(bf16[128,1024]{1,0:T(8,128)(2,1)S(1)} %fusion.29, bf16[1024,1024]{1,0:T(8,128)(2,1)} %collective-permute-done.1.other_ref), kind=kOutput, calls=%fused_computation.104 | convolution fusion | flops 268435456 | bytes 2621440 | tf_op jit(solution)/shard_map/dot_general | solution.py:15
  27.7 6.5 %all-to-all-start = ((bf16[8,256,128]{2,1,0:T(8,128)(2,1)}), bf16[8,256,128]{2,1,0:T(8,128)(2,1)S(1)}, u32[]{:S(2)}, u32[]{:S(2)}) async-start(bf16[8,256,128]{2,1,0:T(8,128)(2,1)} %bitcast_bitcast_fusion.1), calls=%async_computation | async-start | bytes 1048576 | tf_op jit(solution)/shard_map/all_to_all | solution.py:31
  34.2 1.3 collective-permute-start.2
  35.5 6.0 %collective-permute-done.2 = bf16[64,1024]{1,0:T(8,128)(2,1)S(1)} collective-permute-done((bf16[64,1024]{1,0:T(8,128)(2,1)S(1)}, bf16[64,1024]{1,0:T(8,128)(2,1)S(1)}, u32[]{:S(2)}, u32[]{:S(2)}) %collective-permute-start.2) | collective-permute-done | bytes 131104 | tf_op jit(solution)/shard_map/ppermute | solution.py:19
  42.6 9.6 %all-to-all-done = bf16[8,256,128]{2,1,0:T(8,128)(2,1)S(1)} async-done(((bf16[8,256,128]{2,1,0:T(8,128)(2,1)}), bf16[8,256,128]{2,1,0:T(8,128)(2,1)S(1)}, u32[]{:S(2)}, u32[]{:S(2)}) %all-to-all-start) | async-done | bytes 524320 | tf_op jit(solution)/shard_map/all_to_all | solution.py:31
  52.3 1.3 collective-permute-start.4
  53.6 5.2 %shard_map.28 = (bf16[128,1024]{1,0:T(8,128)(2,1)}, f32[64,1024]{1,0:T(8,128)}, f32[64,1024]{1,0:T(8,128)}) custom-call(s32[1]{0:T(128)} %bitcast.core_ref, bf16[8,2,128,128]{3,2,1,0:T(8,128)(2,1)} %bitcast.135, bf16[1,1024,128]{2,1,0:T(8,128)(2,1)} %get-tuple-element.51.p_ref, bf16[2,1024,1024]{2,1,0:T(8,128)(2,1)} %k_ref.3, bf16[1024,1024]{1,0:T(8,128)(2,1)} %copy-done.4, ...), custom_call_target="tpu_custom_call" | custom-call | flops 16777216 | bytes 131072 | tf_op jit(solution)/shard_map/pallas_call | solution.py:78
  59.6 1.3 collective-permute-start.7
  60.9 1.3 collective-permute-start.5
  62.2 3.9 %collective-permute-done.7 = bf16[64,1024]{1,0:T(8,128)(2,1)S(1)} collective-permute-done((bf16[64,1024]{1,0:T(8,128)(2,1)S(1)}, bf16[64,1024]{1,0:T(8,128)(2,1)S(1)}, u32[]{:S(2)}, u32[]{:S(2)}) %collective-permute-start.7) | collective-permute-done | bytes 131104 | tf_op jit(solution)/shard_map/ppermute | solution.py:19
  66.6 1.3 collective-permute-start.10
  67.9 8.0 %collective-permute-start.8 = (bf16[64,1024]{1,0:T(8,128)(2,1)S(1)}, bf16[64,1024]{1,0:T(8,128)(2,1)S(1)}, u32[]{:S(2)}, u32[]{:S(2)}) collective-permute-start(bf16[64,1024]{1,0:T(8,128)(2,1)S(1)} %convolution_convert_fusion.5), channel_id=1, source_target_pairs={{0,240},{16,0},{32,16},{48,32},{64,48},{80,64},{96,80},{112,96},{1... | collective-permute-start | bytes 393224 | tf_op jit(solution)/shard_map/ppermute | solution.py:19
  75.9 1.3 collective-permute-start.9
  77.2 1.3 collective-permute-start.6
  78.6 4.3 %collective-permute-done.9 = bf16[64,1024]{1,0:T(8,128)(2,1)S(1)} collective-permute-done((bf16[64,1024]{1,0:T(8,128)(2,1)S(1)}, bf16[64,1024]{1,0:T(8,128)(2,1)S(1)}, u32[]{:S(2)}, u32[]{:S(2)}) %collective-permute-start.9) | collective-permute-done | bytes 131104 | tf_op jit(solution)/shard_map/ppermute | solution.py:19
  84.7 10.4 %all_to_all.25 = bf16[8,64,128]{2,1,0:T(8,128)(2,1)S(1)} all-to-all(bf16[8,64,128]{2,1,0:T(8,128)(2,1)S(1)} %bitcast_bitcast_fusion.4), channel_id=1, replica_groups=mesh['y'=4,'x'=4,'core'=2,'z'=8] {'z'}, dimensions={0} | all-to-all | bytes 262144 | tf_op jit(solution)/shard_map/all_to_all | solution.py:31
  95.1 4.3 %collective-permute-start.11 = (bf16[8,64,128]{2,1,0:T(8,128)(2,1)S(1)}, bf16[8,64,128]{2,1,0:T(8,128)(2,1)S(1)}, u32[]{:S(2)}, u32[]{:S(2)}) collective-permute-start(bf16[8,64,128]{2,1,0:T(8,128)(2,1)S(1)} %all_to_all.25), channel_id=1, source_target_pairs={{0,8},{8,0},{1,9},{9,1},{2,10},{10,2},{3,11},{11,3},{4,12},{12,4},... | collective-permute-start | bytes 393224 | tf_op jit(solution)/shard_map/ppermute | solution.py:23
  99.4 1.2 collective-permute-done.11
  101.2 1.3 collective-permute-start.12
  102.5 6.8 %collective-permute-done.12 = bf16[64,1024]{1,0:T(8,128)(2,1)S(1)} collective-permute-done((bf16[64,1024]{1,0:T(8,128)(2,1)S(1)}, bf16[64,1024]{1,0:T(8,128)(2,1)S(1)}, u32[]{:S(2)}, u32[]{:S(2)}) %collective-permute-start.12) | collective-permute-done | bytes 131104 | tf_op jit(solution)/shard_map/ppermute | solution.py:19
  109.3 2.3 %convolution_convert_fusion.3 = bf16[64,1024]{1,0:T(8,128)(2,1)S(1)} fusion(bf16[64,1024]{1,0:T(8,128)(2,1)S(1)} %collective-permute-done.12, bf16[1024,1024]{1,0:T(8,128)(2,1)} %all-gather.3.cloned.1.call-done), kind=kOutput, calls=%fused_computation.41 | convolution fusion | flops 134283264 | bytes 2359296 | tf_op jit(solution)/shard_map/dot_general | solution.py:15
  111.6 12.6 %all_to_all.26 = bf16[8,64,128]{2,1,0:T(8,128)(2,1)S(1)} all-to-all(bf16[8,64,128]{2,1,0:T(8,128)(2,1)S(1)} %bitcast_bitcast_fusion.3), channel_id=1, replica_groups=mesh['y'=4,'x'=4,'core'=2,'z'=8] {'z'}, dimensions={0} | all-to-all | bytes 262144 | tf_op jit(solution)/shard_map/all_to_all | solution.py:31
  124.2 2.0 collective-permute-start.13
  127.9 1.3 collective-permute-start.16
  129.2 1.3 collective-permute-start.15
  130.5 1.3 collective-permute-start.14
  131.8 5.9 %all-gather.5.cloned.1.call-done = bf16[3,1024,1024]{2,1,0:T(8,128)(2,1)} async-done(((bf16[3,64,1024]{2,1,0:T(8,128)(2,1)}), bf16[3,1024,1024]{2,1,0:T(8,128)(2,1)}) %all-gather.5.cloned.1.call-update) | async-done | bytes 6291472 | tf_op jit(solution)/shard_map/all_gather | solution.py:217
  137.7 3.8 %slice_bitcast_fusion = (bf16[1024,1024]{1,0:T(8,128)(2,1)S(1)}, bf16[1024,1024]{1,0:T(8,128)(2,1)S(1)}, bf16[1024,1024]{1,0:T(8,128)(2,1)S(1)}) fusion(bf16[3,1024,1024]{2,1,0:T(8,128)(2,1)} %all-gather.5.cloned.1.call-done), kind=kLoop, calls=%fused_computation | loop fusion | bytes 12582912 | tf_op jit(solution)/shard_map/squeeze | solution.py:225
  145.0 4.1 %all-to-all-start.3 = ((bf16[8,192,128]{2,1,0:T(8,128)(2,1)}), bf16[8,192,128]{2,1,0:T(8,128)(2,1)S(1)}, u32[]{:S(2)}, u32[]{:S(2)}) async-start(bf16[8,192,128]{2,1,0:T(8,128)(2,1)} %bitcast_bitcast_fusion.2), calls=%async_computation.3 | async-start | bytes 786432 | tf_op jit(solution)/shard_map/all_to_all | solution.py:31
  149.0 4.7 %collective-permute-start.17 = (bf16[64,1024]{1,0:T(8,128)(2,1)S(1)}, bf16[64,1024]{1,0:T(8,128)(2,1)S(1)}, u32[]{:S(2)}, u32[]{:S(2)}) collective-permute-start(bf16[64,1024]{1,0:T(8,128)(2,1)S(1)} %fusion.43), channel_id=1, source_target_pairs={{0,240},{16,0},{32,16},{48,32},{64,48},{80,64},{96,80},{112,96},{1... | collective-permute-start | bytes 393224 | tf_op jit(solution)/shard_map/ppermute | solution.py:19
  153.7 2.3 %collective-permute-done.17 = bf16[64,1024]{1,0:T(8,128)(2,1)S(1)} collective-permute-done((bf16[64,1024]{1,0:T(8,128)(2,1)S(1)}, bf16[64,1024]{1,0:T(8,128)(2,1)S(1)}, u32[]{:S(2)}, u32[]{:S(2)}) %collective-permute-start.17) | collective-permute-done | bytes 131104 | tf_op jit(solution)/shard_map/ppermute | solution.py:19
  156.0 8.2 %all-to-all-done.3 = bf16[8,192,128]{2,1,0:T(8,128)(2,1)S(1)} async-done(((bf16[8,192,128]{2,1,0:T(8,128)(2,1)}), bf16[8,192,128]{2,1,0:T(8,128)(2,1)S(1)}, u32[]{:S(2)}, u32[]{:S(2)}) %all-to-all-start.3) | async-done | bytes 393248 | tf_op jit(solution)/shard_map/all_to_all | solution.py:31
  164.7 1.3 collective-permute-done.18
  166.7 2.2 %fusion.44 = bf16[64,1024]{1,0:T(8,128)(2,1)S(1)} fusion(bf16[1024,1024]{1,0:T(8,128)(2,1)} %copy-done, bf16[1024,64]{0,1:T(8,128)(2,1)S(1)} %copy.40, bf16[1024,128]{1,0:T(8,128)(2,1)S(1)} %bitcast.141, s32[]{:T(128)S(6)} %select_n.106), kind=kOutput, calls=%fused_computation.38 | convolution fusion | flops 134414336 | bytes 2621444 | tf_op jit(solution)/shard_map/dot_general | solution.py:15
  169.0 2.5 %fusion.46 = f32[64,1024]{1,0:T(8,128)S(1)} fusion(bf16[1024,1024]{1,0:T(8,128)(2,1)} %copy-done.3, bf16[64,1024]{1,0:T(8,128)(2,1)S(1)} %fusion.44, bf16[1024,1024]{1,0:T(8,128)(2,1)S(1)} %get-tuple-element.37, bf16[1024,64]{0,1:T(8,128)(2,1)S(1)} %copy.41), kind=kOutput, calls=%fused_computation.46 | convolution fusion | flops 268632064 | bytes 4718592 | tf_op jit(solution)/shard_map/dot_general | solution.py:15
  172.0 2.0 collective-permute-start.3
  174.1 2.2 %fusion.72 = bf16[128,1024]{1,0:T(8,128)(2,1)S(1)} fusion(bf16[1024,1024]{1,0:T(8,128)(2,1)} %copy-done.4, bf16[64,1024]{1,0:T(8,128)(2,1)S(1)} %collective-permute-done.19, bf16[64,1024]{1,0:T(8,128)(2,1)S(1)} %get-tuple-element.41, pred[]{:T(512)S(6)} %eq.4), kind=kOutput, calls=%fused_computation.102 | convolution fusion | flops 269615104 | bytes 2621441 | tf_op jit(solution)/shard_map/dot_general | solution.py:15
  176.3 2.1 fusion.39
  180.2 3.5 %all-to-all-start.4 = ((bf16[8,256,128]{2,1,0:T(8,128)(2,1)}), bf16[8,256,128]{2,1,0:T(8,128)(2,1)S(1)}, u32[]{:S(2)}, u32[]{:S(2)}) async-start(bf16[8,256,128]{2,1,0:T(8,128)(2,1)} %bitcast_bitcast_fusion), calls=%async_computation.4 | async-start | bytes 1048576 | tf_op jit(solution)/shard_map/all_to_all | solution.py:31
  183.7 1.3 collective-permute-start.20
  185.0 7.3 %collective-permute-done.20 = bf16[64,1024]{1,0:T(8,128)(2,1)S(1)} collective-permute-done((bf16[64,1024]{1,0:T(8,128)(2,1)S(1)}, bf16[64,1024]{1,0:T(8,128)(2,1)S(1)}, u32[]{:S(2)}, u32[]{:S(2)}) %collective-permute-start.20) | collective-permute-done | bytes 131104 | tf_op jit(solution)/shard_map/ppermute | solution.py:19
  194.4 7.1 %all-to-all-done.4 = bf16[8,256,128]{2,1,0:T(8,128)(2,1)S(1)} async-done(((bf16[8,256,128]{2,1,0:T(8,128)(2,1)}), bf16[8,256,128]{2,1,0:T(8,128)(2,1)S(1)}, u32[]{:S(2)}, u32[]{:S(2)}) %all-to-all-start.4) | async-done | bytes 524320 | tf_op jit(solution)/shard_map/all_to_all | solution.py:31
  202.3 5.2 %shard_map.29 = bf16[2,1024,128]{2,1,0:T(8,128)(2,1)} custom-call(s32[1]{0:T(128)} %bitcast.core_ref, bf16[8,2,128,128]{3,2,1,0:T(8,128)(2,1)} %bitcast.136, bf16[128,1024]{1,0:T(8,128)(2,1)} %maximum_select_fusion.1.start_ref, bf16[128,1024]{1,0:T(8,128)(2,1)} %get-tuple-element.26.part_ref, bf16[2,1024,128]{2,1,0:T(8,128)(2,1)} %p_ref.1, ...), custom_call_target="tpu_custom_call" | custom-call | flops 536870912 | bytes 5242880 | tf_op jit(solution)/shard_map/pallas_call | solution.py:130
  (84 shorter events, 18.7 us)
Async XLA Ops:
  6.5 8.0 %copy-start.8 = (bf16[2,1024,128]{2,1,0:T(8,128)(2,1)S(1)}, bf16[2,1024,128]{2,1,0:T(8,128)(2,1)}, u32[]{:S(2)}) copy-start(bf16[2,1024,128]{2,1,0:T(8,128)(2,1)} %p_ref.1) | copy-start | bytes 1572868
  11.2 8.3 %copy-start.4 = (bf16[1024,1024]{1,0:T(8,128)(2,1)}, bf16[1024,1024]{1,0:T(8,128)(2,1)S(1)}, u32[]{:S(2)}) copy-start(bf16[1024,1024]{1,0:T(8,128)(2,1)S(1)} %fusion.18.own_ref) | copy-start | bytes 6291460
  11.2 8.3 %collective-permute-start.1 = (bf16[1024,1024]{1,0:T(8,128)(2,1)S(1)}, bf16[1024,1024]{1,0:T(8,128)(2,1)}, u32[]{:S(2)}, u32[]{:S(2)}) collective-permute-start(bf16[1024,1024]{1,0:T(8,128)(2,1)S(1)} %fusion.18.own_ref), channel_id=1, source_target_pairs={{0,8},{8,0},{1,9},{9,1},{2,10},{10,2},{3,11},{11,3},{4,12},{12,4},... | collective-permute-start | bytes 6291464 | tf_op jit(solution)/shard_map/ppermute | solution.py:23
  15.2 11.0 %collective-permute-start = (bf16[1024,128]{1,0:T(8,128)(2,1)S(1)}, bf16[1024,128]{1,0:T(8,128)(2,1)S(1)}, u32[]{:S(2)}, u32[]{:S(2)}) collective-permute-start(bf16[1024,128]{1,0:T(8,128)(2,1)S(1)} %get-tuple-element.52), channel_id=1, source_target_pairs={{8,0},{9,1},{10,2},{11,3},{12,4},{13,5},{14,6},{15,7},{24,16},{25,... | collective-permute-start | bytes 786440 | tf_op jit(solution)/shard_map/ppermute | solution.py:182
  24.0 2.2 %copy-start.5 = (bf16[1024,1024]{1,0:T(8,128)(2,1)S(1)}, bf16[1024,1024]{1,0:T(8,128)(2,1)}, u32[]{:S(2)}) copy-start(bf16[1024,1024]{1,0:T(8,128)(2,1)} %copy-done.4) | copy-start | bytes 6291460
  27.7 24.5 %all-to-all-start = ((bf16[8,256,128]{2,1,0:T(8,128)(2,1)}), bf16[8,256,128]{2,1,0:T(8,128)(2,1)S(1)}, u32[]{:S(2)}, u32[]{:S(2)}) async-start(bf16[8,256,128]{2,1,0:T(8,128)(2,1)} %bitcast_bitcast_fusion.1), calls=%async_computation | async-start | bytes 1048576 | tf_op jit(solution)/shard_map/all_to_all | solution.py:31
  34.1 75.2 %all-gather.3.cloned.1.call-start = ((), (), s32[]{:S(2)}) async-start(), calls=%async_computation.5 | async-start | bytes 2228224 | tf_op jit(solution)/shard_map/all_gather | solution.py:196
  34.2 7.3 %collective-permute-start.2 = (bf16[64,1024]{1,0:T(8,128)(2,1)S(1)}, bf16[64,1024]{1,0:T(8,128)(2,1)S(1)}, u32[]{:S(2)}, u32[]{:S(2)}) collective-permute-start(bf16[64,1024]{1,0:T(8,128)(2,1)S(1)} %constant_dynamic-slice_fusion.2), channel_id=1, source_target_pairs={{16,0},{32,16},{48,32},{64,48},{80,64},{96,80},{112,96},{128,112},... | collective-permute-start | bytes 393224 | tf_op jit(solution)/shard_map/ppermute | solution.py:19
  52.2 1.4 copy-start.6
  52.3 85.4 %all-gather.5.cloned.1.call-start = ((), (), s32[]{:S(2)}) async-start(), calls=%async_computation.6 | async-start | bytes 6684672 | tf_op jit(solution)/shard_map/all_gather | solution.py:217
  52.3 6.8 %collective-permute-start.4 = (bf16[64,1024]{1,0:T(8,128)(2,1)}, bf16[64,1024]{1,0:T(8,128)(2,1)S(1)}, u32[]{:S(2)}, u32[]{:S(2)}) collective-permute-start(bf16[64,1024]{1,0:T(8,128)(2,1)} %convolution_convert_fusion.7), channel_id=1, source_target_pairs={{16,0},{32,16},{48,32},{64,48},{80,64},{96,80},{112,96},{128,112},... | collective-permute-start | bytes 393224 | tf_op jit(solution)/shard_map/ppermute | solution.py:19
  58.8 2.1 copy-start.11
  59.1 18.1 %copy-start.9 = (f32[64,1024]{1,0:T(8,128)S(1)}, f32[64,1024]{1,0:T(8,128)}, u32[]{:S(2)}) copy-start(f32[64,1024]{1,0:T(8,128)} %get-tuple-element.29) | copy-start | bytes 786436
  59.6 6.5 %collective-permute-start.7 = (bf16[64,1024]{1,0:T(8,128)(2,1)S(1)}, bf16[64,1024]{1,0:T(8,128)(2,1)S(1)}, u32[]{:S(2)}, u32[]{:S(2)}) collective-permute-start(bf16[64,1024]{1,0:T(8,128)(2,1)S(1)} %convolution_convert_fusion.6), channel_id=1, source_target_pairs={{16,0},{32,16},{48,32},{64,48},{80,64},{96,80},{112,96},{128,112},... | collective-permute-start | bytes 393224 | tf_op jit(solution)/shard_map/ppermute | solution.py:19
  60.9 16.3 %collective-permute-start.5 = (f32[64,1024]{1,0:T(8,128)S(1)}, f32[64,1024]{1,0:T(8,128)S(1)}, u32[]{:S(2)}, u32[]{:S(2)}) collective-permute-start(f32[64,1024]{1,0:T(8,128)S(1)} %copy-done.11), channel_id=1, source_target_pairs={{0,8},{8,0},{1,9},{9,1},{2,10},{10,2},{3,11},{11,3},{4,12},{12,4},... | collective-permute-start | bytes 786440 | tf_op jit(solution)/shard_map/ppermute | solution.py:23
  66.6 11.9 %collective-permute-start.10 = (bf16[64,1024]{1,0:T(8,128)(2,1)S(1)}, bf16[64,1024]{1,0:T(8,128)(2,1)S(1)}, u32[]{:S(2)}, u32[]{:S(2)}) collective-permute-start(bf16[64,1024]{1,0:T(8,128)(2,1)S(1)} %convolution_convert_fusion.5), channel_id=1, source_target_pairs={{128,240},{144,0},{160,16},{176,32},{192,48},{208,64},{224,80},{24... | collective-permute-start | bytes 393224 | tf_op jit(solution)/shard_map/ppermute | solution.py:19
  67.9 10.6 %collective-permute-start.8 = (bf16[64,1024]{1,0:T(8,128)(2,1)S(1)}, bf16[64,1024]{1,0:T(8,128)(2,1)S(1)}, u32[]{:S(2)}, u32[]{:S(2)}) collective-permute-start(bf16[64,1024]{1,0:T(8,128)(2,1)S(1)} %convolution_convert_fusion.5), channel_id=1, source_target_pairs={{0,240},{16,0},{32,16},{48,32},{64,48},{80,64},{96,80},{112,96},{1... | collective-permute-start | bytes 393224 | tf_op jit(solution)/shard_map/ppermute | solution.py:19
  75.9 7.0 %collective-permute-start.9 = (bf16[64,1024]{1,0:T(8,128)(2,1)S(1)}, bf16[64,1024]{1,0:T(8,128)(2,1)S(1)}, u32[]{:S(2)}, u32[]{:S(2)}) collective-permute-start(bf16[64,1024]{1,0:T(8,128)(2,1)S(1)} %convolution_convert_fusion.5), channel_id=1, source_target_pairs={{64,240},{80,0},{96,16},{112,32},{128,48},{144,64},{160,80},{176,9... | collective-permute-start | bytes 393224 | tf_op jit(solution)/shard_map/ppermute | solution.py:19
  77.2 6.1 %collective-permute-start.6 = (bf16[64,1024]{1,0:T(8,128)(2,1)S(1)}, bf16[64,1024]{1,0:T(8,128)(2,1)S(1)}, u32[]{:S(2)}, u32[]{:S(2)}) collective-permute-start(bf16[64,1024]{1,0:T(8,128)(2,1)S(1)} %add_convert_fusion.2), channel_id=1, source_target_pairs={{16,0},{32,16},{48,32},{64,48},{80,64},{96,80},{112,96},{128,112},... | collective-permute-start | bytes 393224 | tf_op jit(solution)/shard_map/ppermute | solution.py:19
  95.1 5.4 %collective-permute-start.11 = (bf16[8,64,128]{2,1,0:T(8,128)(2,1)S(1)}, bf16[8,64,128]{2,1,0:T(8,128)(2,1)S(1)}, u32[]{:S(2)}, u32[]{:S(2)}) collective-permute-start(bf16[8,64,128]{2,1,0:T(8,128)(2,1)S(1)} %all_to_all.25), channel_id=1, source_target_pairs={{0,8},{8,0},{1,9},{9,1},{2,10},{10,2},{3,11},{11,3},{4,12},{12,4},... | collective-permute-start | bytes 393224 | tf_op jit(solution)/shard_map/ppermute | solution.py:23
  101.2 8.1 %collective-permute-start.12 = (bf16[64,1024]{1,0:T(8,128)(2,1)S(1)}, bf16[64,1024]{1,0:T(8,128)(2,1)S(1)}, u32[]{:S(2)}, u32[]{:S(2)}) collective-permute-start(bf16[64,1024]{1,0:T(8,128)(2,1)S(1)} %add_convert_fusion.1), channel_id=1, source_target_pairs={{32,0},{48,16},{64,32},{80,48},{96,64},{112,80},{128,96},{144,112}... | collective-permute-start | bytes 393224 | tf_op jit(solution)/shard_map/ppermute | solution.py:19
  109.3 17.9 %copy-start.2 = (bf16[1024,1024]{1,0:T(8,128)(2,1)S(1)}, bf16[1024,1024]{1,0:T(8,128)(2,1)}, u32[]{:S(2)}) copy-start(bf16[1024,1024]{1,0:T(8,128)(2,1)} %all-gather.3.cloned.1.call-done) | copy-start | bytes 6291460
  124.2 3.0 %collective-permute-start.13 = (bf16[8,64,128]{2,1,0:T(8,128)(2,1)S(1)}, bf16[8,64,128]{2,1,0:T(8,128)(2,1)S(1)}, u32[]{:S(2)}, u32[]{:S(2)}) collective-permute-start(bf16[8,64,128]{2,1,0:T(8,128)(2,1)S(1)} %all_to_all.26), channel_id=1, source_target_pairs={{0,8},{8,0},{1,9},{9,1},{2,10},{10,2},{3,11},{11,3},{4,12},{12,4},... | collective-permute-start | bytes 393224 | tf_op jit(solution)/shard_map/ppermute | solution.py:23
  127.9 13.6 %collective-permute-start.16 = (bf16[64,1024]{1,0:T(8,128)(2,1)S(1)}, bf16[64,1024]{1,0:T(8,128)(2,1)S(1)}, u32[]{:S(2)}, u32[]{:S(2)}) collective-permute-start(bf16[64,1024]{1,0:T(8,128)(2,1)S(1)} %fusion.43), channel_id=1, source_target_pairs={{192,240},{208,0},{224,16},{240,32},{193,241},{209,1},{225,17},{24... | collective-permute-start | bytes 393224 | tf_op jit(solution)/shard_map/ppermute | solution.py:19
  129.2 12.8 %collective-permute-start.15 = (bf16[64,1024]{1,0:T(8,128)(2,1)S(1)}, bf16[64,1024]{1,0:T(8,128)(2,1)S(1)}, u32[]{:S(2)}, u32[]{:S(2)}) collective-permute-start(bf16[64,1024]{1,0:T(8,128)(2,1)S(1)} %fusion.43), channel_id=1, source_target_pairs={{128,240},{144,0},{160,16},{176,32},{192,48},{208,64},{224,80},{24... | collective-permute-start | bytes 393224 | tf_op jit(solution)/shard_map/ppermute | solution.py:19
  130.5 12.3 %collective-permute-start.14 = (bf16[64,1024]{1,0:T(8,128)(2,1)S(1)}, bf16[64,1024]{1,0:T(8,128)(2,1)S(1)}, u32[]{:S(2)}, u32[]{:S(2)}) collective-permute-start(bf16[64,1024]{1,0:T(8,128)(2,1)S(1)} %fusion.43), channel_id=1, source_target_pairs={{64,240},{80,0},{96,16},{112,32},{128,48},{144,64},{160,80},{176,9... | collective-permute-start | bytes 393224 | tf_op jit(solution)/shard_map/ppermute | solution.py:19
  141.5 1.4 copy-start
  141.5 2.1 copy-start.3
  145.0 19.2 %all-to-all-start.3 = ((bf16[8,192,128]{2,1,0:T(8,128)(2,1)}), bf16[8,192,128]{2,1,0:T(8,128)(2,1)S(1)}, u32[]{:S(2)}, u32[]{:S(2)}) async-start(bf16[8,192,128]{2,1,0:T(8,128)(2,1)} %bitcast_bitcast_fusion.2), calls=%async_computation.3 | async-start | bytes 786432 | tf_op jit(solution)/shard_map/all_to_all | solution.py:31
  149.0 7.0 %collective-permute-start.17 = (bf16[64,1024]{1,0:T(8,128)(2,1)S(1)}, bf16[64,1024]{1,0:T(8,128)(2,1)S(1)}, u32[]{:S(2)}, u32[]{:S(2)}) collective-permute-start(bf16[64,1024]{1,0:T(8,128)(2,1)S(1)} %fusion.43), channel_id=1, source_target_pairs={{0,240},{16,0},{32,16},{48,32},{64,48},{80,64},{96,80},{112,96},{1... | collective-permute-start | bytes 393224 | tf_op jit(solution)/shard_map/ppermute | solution.py:19
  164.2 1.8 collective-permute-start.18
  169.0 3.0 %copy-start.10 = (bf16[128,1024]{1,0:T(8,128)(2,1)S(1)}, bf16[128,1024]{1,0:T(8,128)(2,1)}, u32[]{:S(2)}) copy-start(bf16[128,1024]{1,0:T(8,128)(2,1)} %get-tuple-element.26.part_ref) | copy-start | bytes 786436
  171.5 2.5 %collective-permute-start.19 = (bf16[64,1024]{1,0:T(8,128)(2,1)S(1)}, bf16[64,1024]{1,0:T(8,128)(2,1)S(1)}, u32[]{:S(2)}, u32[]{:S(2)}) collective-permute-start(bf16[64,1024]{1,0:T(8,128)(2,1)S(1)} %get-tuple-element.41), channel_id=1, source_target_pairs={{0,8},{8,0},{1,9},{9,1},{2,10},{10,2},{3,11},{11,3},{4,12},{12,4},... | collective-permute-start | bytes 393224 | tf_op jit(solution)/shard_map/ppermute | solution.py:23
  172.0 6.3 %collective-permute-start.3 = (bf16[128,1024]{1,0:T(8,128)(2,1)S(1)}, bf16[128,1024]{1,0:T(8,128)(2,1)S(1)}, u32[]{:S(2)}, u32[]{:S(2)}) collective-permute-start(bf16[128,1024]{1,0:T(8,128)(2,1)S(1)} %copy-done.10), channel_id=1, source_target_pairs={{8,0},{9,1},{10,2},{11,3},{12,4},{13,5},{14,6},{15,7},{24,16},{25,... | collective-permute-start | bytes 786440 | tf_op jit(solution)/shard_map/ppermute | solution.py:240
  174.0 4.3 %copy-start.1 = (bf16[2,1024,1024]{2,1,0:T(8,128)(2,1)S(1)}, bf16[2,1024,1024]{2,1,0:T(8,128)(2,1)}, u32[]{:S(2)}) copy-start(bf16[2,1024,1024]{2,1,0:T(8,128)(2,1)} %k_ref.3) | copy-start | bytes 12582916
  180.2 21.3 %all-to-all-start.4 = ((bf16[8,256,128]{2,1,0:T(8,128)(2,1)}), bf16[8,256,128]{2,1,0:T(8,128)(2,1)S(1)}, u32[]{:S(2)}, u32[]{:S(2)}) async-start(bf16[8,256,128]{2,1,0:T(8,128)(2,1)} %bitcast_bitcast_fusion), calls=%async_computation.4 | async-start | bytes 1048576 | tf_op jit(solution)/shard_map/all_to_all | solution.py:31
  183.7 8.6 %collective-permute-start.20 = (bf16[64,1024]{1,0:T(8,128)(2,1)S(1)}, bf16[64,1024]{1,0:T(8,128)(2,1)S(1)}, u32[]{:S(2)}, u32[]{:S(2)}) collective-permute-start(bf16[64,1024]{1,0:T(8,128)(2,1)S(1)} %get-tuple-element.42), channel_id=1, source_target_pairs={{0,16},{16,32},{32,48},{48,64},{64,80},{80,96},{96,112},{112,128},... | collective-permute-start | bytes 393224 | tf_op jit(solution)/shard_map/ppermute | solution.py:19
  192.3 1.4 collective-permute-start.21
  201.5 0.8 copy-start.7
Sparse Core Ops, SparseCore 0:
  52.4 36.1 all-gather.2
  90.4 47.2 all-gather.4

commit v4 on v3

--- a/solution.py
+++ b/solution.py
@@ -187,10 +187,12 @@
     ).astype(BF16)
     z_b = side(dot(p_high.T, own), dot(z_a, other)).astype(BF16)
 
-    whole = dot(side(other, own), side(own, other)).astype(BF16)
+    pieces = jnp.concatenate([z_a, z_b], axis=0)
+    pieces = pieces.reshape(2 * width, order // width, width).swapaxes(0, 1)
+    pieces, other2 = lax.optimization_barrier((pieces, other))
+    got = lax.all_to_all(pieces, "z", 0, 0, tiled=True)
+    whole = dot(side(other2, own), side(own, other2)).astype(BF16)
     piece = lax.dynamic_slice_in_dim(whole, slab * width + core * half, half, 0)
-    z_b, piece = lax.optimization_barrier((z_b, piece))
-    got = turned(jnp.concatenate([z_a, z_b], axis=0))
     piece = dot(moved(piece, later(1)), whole).astype(BF16)
     got, piece = lax.optimization_barrier((got, piece))
     phi2 = lax.all_gather(piece, ("z", "core"), axis=0, tiled=True)
@@ -213,7 +215,8 @@
 
     times = lambda x: dot(x, whole)
     x = moved(reduced, later(1))
-    x, pieces = lax.optimization_barrier((x, pieces))
+    part_high = lax.ppermute(part, "core", [(1, 0)])
+    x, pieces, part_high = lax.optimization_barrier((x, pieces, part_high))
     gathered = lax.all_gather(jnp.stack(pieces), ("z", "core"), axis=1, tiled=True)
     reduced = closed(reduced, turned(times(x).astype(BF16)), times)
     times = lambda x: dot(x, phi2)
@@ -226,18 +229,17 @@
     z = dot(x3, phis[2]).astype(BF16)
     z = dot(jnp.concatenate([x2, z], axis=0), phis[1]).astype(BF16)
     z = dot(jnp.concatenate([x1, z], axis=0), phis[0]).astype(BF16)
-    got, base = lax.optimization_barrier((turned(z), base))
+    phi8 = dot(phis[1], phis[0]).astype(BF16)
+    phi12 = dot(phis[2], phi8).astype(BF16)
+    got, base, phi8, phi12 = lax.optimization_barrier((turned(z), base, phi8, phi12))
     far = from_other_core(got)
     full = jnp.stack([side(got, far), side(far, got)], axis=1).reshape(8, 2, 3, half, width)
     y = [half_rows(full[:, :, j].reshape(order, width).T, core) for j in range(3)]
-    total = y[2]
-    for j in (2, 1):
-        total = (dot(total, phis[j]) + y[j - 1].astype(F32)).astype(BF16)
-    reduced = (base.astype(F32) + dot(total, phis[0])).astype(BF16)
+    total = dot(y[0], phis[0]) + dot(y[1], phi8) + dot(y[2], phi12)
+    reduced = (base.astype(F32) + total).astype(BF16)
 
     start = both_halves(moved(reduced, [(c, (c + 1) % chips) for c in range(chips)]))
     after = both_halves(jnp.where(chip == chips - 1, jnp.zeros_like(reduced), reduced))
-    part_high = lax.ppermute(part, "core", [(1, 0)])
     second_k = coupling[1]
     through = side(dot(after, other), dot(after, own)).astype(BF16)
     v = dot(side(part_high, after), second_k).astype(BF16)

time: 215 us -> 209 us (0.972)
  waiting for transfers between devices: 66.7 us -> 57.6 us
  matrix products: 31.4 us -> 34.9 us
    all_to_all x3 -> x2, waiting for transfers between devices: 24.9 us -> 15.6 us  [turned(): return lax.all_to_all(pieces, 'z', 0, 0, tiled=True)]
    all_to_all x0 -> x1, starting transfers between devices: none -> 6.45 us  [shards(): got = lax.all_to_all(pieces, 'z', 0, 0, tiled=True)]
    all_to_all x3 -> x2, starting transfers between devices: 14 us -> 7.57 us  [turned(): return lax.all_to_all(pieces, 'z', 0, 0, tiled=True)]
    all_to_all x0 -> x1, waiting for transfers between devices: none -> 5.13 us  [shards(): got = lax.all_to_all(pieces, 'z', 0, 0, tiled=True)]
    ppermute x13, waiting for transfers between devices: 31.4 us -> 26.5 us  [moved(): return lax.ppermute(block, CHIPS, pairs)]
    dot_general x20 -> x23, matrix products: 29.3 us -> 32.8 us  [dot(): return jnp.dot(left, right, preferred_element_type=F32)]
    ppermute x13, starting transfers between devices: 26.8 us -> 24.2 us  [moved(): return lax.ppermute(block, CHIPS, pairs)]
  transfers between devices with their start and end apart: 27 -> 27, of which waited for: 16 -> 16; matrix products, arithmetic and copies ran while one was open for 12% -> 14% of each run, Pallas kernels for 2% -> 3%
where the time goes in v4:
time: 209 us; the launch traced here: 208 us
  waiting for transfers between devices  57.6 us (28%)
  starting transfers between devices  56.2 us (27%)
  matrix products  34.9 us (17%)
  blocking collectives  22.9 us (11%)
  between operations  14 us (7%)
  Pallas kernels  10.4 us (5%)
  local copies, waits for them, and re-layouts  9.36 us (4%)
  other arithmetic  2.72 us (1%)
    dot_general x23, matrix products, dot(): return jnp.dot(left, right, preferred_element_type=F32)  32.8 us
    ppermute x13, waiting for transfers between devices, moved(): return lax.ppermute(block, CHIPS, pairs)  26.5 us
    ppermute x13, starting transfers between devices, moved(): return lax.ppermute(block, CHIPS, pairs)  24.2 us
    all_to_all x2, blocking collectives, turned(): return lax.all_to_all(pieces, 'z', 0, 0, tiled=True)  22.9 us
    all_to_all x2, waiting for transfers between devices, turned(): return lax.all_to_all(pieces, 'z', 0, 0, tiled=True)  15.6 us
    ppermute x7, starting transfers between devices, from_other_core(): return lax.ppermute(block, 'core', [(0, 1), (1, 0)])  14 us
    all_to_all x2, starting transfers between devices, turned(): return lax.all_to_all(pieces, 'z', 0, 0, tiled=True)  7.57 us
    all_to_all x1, starting transfers between devices, shards(): got = lax.all_to_all(pieces, 'z', 0, 0, tiled=True)  6.45 us
  transfers between devices with their start and end apart: 27, of which 16 were waited for; matrix products, arithmetic and copies ran while one was open for 14% of the time, Pallas kernels for 3%

profile of v4, /device:TPU:1, one launch (start us, length us, event | category | flops | bytes accessed | tf_op | source)
XLA Modules:
  0.0 208.0 jit_solution(13342006236399641979)
XLA Ops:
  6.5 6.0 %fusion.18.own_ref = bf16[1024,1024]{1,0:T(8,128)(2,1)} fusion(bf16[2,1024,1024]{2,1,0:T(8,128)(2,1)} %k_ref.3), kind=kOutput, calls=%fused_computation.17 | convolution fusion | flops 2148532224 | bytes 6291456 | tf_op jit(solution)/shard_map/dot_general | solution.py:15
  12.5 3.2 %collective-permute-start.1 = (bf16[1024,1024]{1,0:T(8,128)(2,1)}, bf16[1024,1024]{1,0:T(8,128)(2,1)S(1)}, u32[]{:S(2)}, u32[]{:S(2)}) collective-permute-start(bf16[1024,1024]{1,0:T(8,128)(2,1)} %fusion.18.own_ref), channel_id=1, source_target_pairs={{0,8},{8,0},{1,9},{9,1},{2,10},{10,2},{3,11},{11,3},{4,12},{12,4},... | collective-permute-start | bytes 6291464 | tf_op jit(solution)/shard_map/ppermute | solution.py:23
  16.5 1.9 collective-permute-start
  18.4 2.1 fusion.29
  21.0 2.3 %fusion.38 = bf16[128,1024]{1,0:T(8,128)(2,1)S(1)} fusion(bf16[128,1024]{1,0:T(8,128)(2,1)S(1)} %fusion.76, bf16[1024,1024]{1,0:T(8,128)(2,1)} %fusion.18.own_ref, bf16[1024,128]{1,0:T(8,128)(2,1)S(1)} %collective-permute-done, pred[]{:T(512)S(6)} %eq.4), kind=kOutput, calls=%fused_computation.33 | convolution fusion | flops 268566528 | bytes 2883585 | tf_op jit(solution)/shard_map/dot_general | solution.py:15
  24.2 6.5 %all-to-all-start = ((bf16[8,256,128]{2,1,0:T(8,128)(2,1)}), bf16[8,256,128]{2,1,0:T(8,128)(2,1)S(1)}, u32[]{:S(2)}, u32[]{:S(2)}) async-start(bf16[8,256,128]{2,1,0:T(8,128)(2,1)} %bitcast_bitcast_fusion.1), calls=%async_computation | async-start | bytes 1048576 | tf_op jit(solution)/shard_map/all_to_all | solution.py:193
  30.7 4.6 %fusion.13 = bf16[1024,1024]{1,0:T(8,128)(2,1)S(1)} fusion(bf16[1024,1024]{1,0:T(8,128)(2,1)} %fusion.18.own_ref, bf16[1024,1024]{1,0:T(8,128)(2,1)} %copy-done, pred[]{:T(512)S(6)} %eq.4), kind=kOutput, calls=%fused_computation.16 | convolution fusion | flops 2150629376 | bytes 6291457 | tf_op jit(solution)/shard_map/dot_general | solution.py:15
  35.3 1.3 collective-permute-start.2
  36.6 5.8 %collective-permute-done.2 = bf16[64,1024]{1,0:T(8,128)(2,1)S(1)} collective-permute-done((bf16[64,1024]{1,0:T(8,128)(2,1)S(1)}, bf16[64,1024]{1,0:T(8,128)(2,1)S(1)}, u32[]{:S(2)}, u32[]{:S(2)}) %collective-permute-start.2) | collective-permute-done | bytes 131104 | tf_op jit(solution)/shard_map/ppermute | solution.py:19
  42.5 1.2 convolution_convert_fusion.9
  43.6 5.1 %all-to-all-done = bf16[8,256,128]{2,1,0:T(8,128)(2,1)S(1)} async-done(((bf16[8,256,128]{2,1,0:T(8,128)(2,1)}), bf16[8,256,128]{2,1,0:T(8,128)(2,1)S(1)}, u32[]{:S(2)}, u32[]{:S(2)}) %all-to-all-start) | async-done | bytes 524320 | tf_op jit(solution)/shard_map/all_to_all | solution.py:193
  48.8 1.3 collective-permute-start.3
  50.1 5.2 %shard_map.28 = (bf16[128,1024]{1,0:T(8,128)(2,1)}, f32[64,1024]{1,0:T(8,128)}, f32[64,1024]{1,0:T(8,128)}) custom-call(s32[1]{0:T(128)} %bitcast.core_ref, bf16[8,2,128,128]{3,2,1,0:T(8,128)(2,1)} %bitcast.131, bf16[1,1024,128]{2,1,0:T(8,128)(2,1)} %get-tuple-element.55.p_ref, bf16[2,1024,1024]{2,1,0:T(8,128)(2,1)} %k_ref.3, ...), custom_call_target="tpu_custom_call" | custom-call | flops 16777216 | bytes 131072 | tf_op jit(solution)/shard_map/pallas_call | solution.py:78
  56.1 1.3 collective-permute-start.6
  57.4 1.4 collective-permute-start.4
  58.7 1.9 collective-permute-start.10
  60.7 2.0 collective-permute-done.6
  63.2 1.3 collective-permute-start.9
  64.5 1.3 collective-permute-start.8
  65.8 8.4 %collective-permute-start.7 = (bf16[64,1024]{1,0:T(8,128)(2,1)S(1)}, bf16[64,1024]{1,0:T(8,128)(2,1)S(1)}, u32[]{:S(2)}, u32[]{:S(2)}) collective-permute-start(bf16[64,1024]{1,0:T(8,128)(2,1)S(1)} %convolution_convert_fusion.7), channel_id=1, source_target_pairs={{0,240},{16,0},{32,16},{48,32},{64,48},{80,64},{96,80},{112,96},{1... | collective-permute-start | bytes 393224 | tf_op jit(solution)/shard_map/ppermute | solution.py:19
  74.2 1.3 collective-permute-start.5
  76.1 4.2 %collective-permute-done.5 = bf16[64,1024]{1,0:T(8,128)(2,1)S(1)} collective-permute-done((bf16[64,1024]{1,0:T(8,128)(2,1)S(1)}, bf16[64,1024]{1,0:T(8,128)(2,1)S(1)}, u32[]{:S(2)}, u32[]{:S(2)}) %collective-permute-start.5) | collective-permute-done | bytes 131104 | tf_op jit(solution)/shard_map/ppermute | solution.py:19
  81.7 10.3 %all_to_all.25 = bf16[8,64,128]{2,1,0:T(8,128)(2,1)S(1)} all-to-all(bf16[8,64,128]{2,1,0:T(8,128)(2,1)S(1)} %bitcast_bitcast_fusion.4), channel_id=1, replica_groups=mesh['y'=4,'x'=4,'core'=2,'z'=8] {'z'}, dimensions={0} | all-to-all | bytes 262144 | tf_op jit(solution)/shard_map/all_to_all | solution.py:31
  92.0 5.3 %collective-permute-start.11 = (bf16[8,64,128]{2,1,0:T(8,128)(2,1)S(1)}, bf16[8,64,128]{2,1,0:T(8,128)(2,1)S(1)}, u32[]{:S(2)}, u32[]{:S(2)}) collective-permute-start(bf16[8,64,128]{2,1,0:T(8,128)(2,1)S(1)} %all_to_all.25), channel_id=1, source_target_pairs={{0,8},{8,0},{1,9},{9,1},{2,10},{10,2},{3,11},{11,3},{4,12},{12,4},... | collective-permute-start | bytes 393224 | tf_op jit(solution)/shard_map/ppermute | solution.py:23
  99.0 1.3 collective-permute-start.12
  100.3 6.8 %collective-permute-done.12 = bf16[64,1024]{1,0:T(8,128)(2,1)S(1)} collective-permute-done((bf16[64,1024]{1,0:T(8,128)(2,1)S(1)}, bf16[64,1024]{1,0:T(8,128)(2,1)S(1)}, u32[]{:S(2)}, u32[]{:S(2)}) %collective-permute-start.12) | collective-permute-done | bytes 131104 | tf_op jit(solution)/shard_map/ppermute | solution.py:19
  107.1 2.3 %convolution_convert_fusion.5 = bf16[64,1024]{1,0:T(8,128)(2,1)S(1)} fusion(bf16[64,1024]{1,0:T(8,128)(2,1)S(1)} %collective-permute-done.12, bf16[1024,1024]{1,0:T(8,128)(2,1)} %all-gather.3.cloned.1.call-done), kind=kOutput, calls=%fused_computation.41 | convolution fusion | flops 134283264 | bytes 2359296 | tf_op jit(solution)/shard_map/dot_general | solution.py:15
  109.4 12.5 %all_to_all.26 = bf16[8,64,128]{2,1,0:T(8,128)(2,1)S(1)} all-to-all(bf16[8,64,128]{2,1,0:T(8,128)(2,1)S(1)} %bitcast_bitcast_fusion.3), channel_id=1, replica_groups=mesh['y'=4,'x'=4,'core'=2,'z'=8] {'z'}, dimensions={0} | all-to-all | bytes 262144 | tf_op jit(solution)/shard_map/all_to_all | solution.py:31
  122.0 2.0 collective-permute-start.13
  125.7 1.6 collective-permute-start.17
  127.3 1.3 collective-permute-start.16
  128.6 1.3 collective-permute-start.15
  129.9 1.3 collective-permute-start.14
  131.2 5.0 %all-gather.5.cloned.1.call-done = bf16[3,1024,1024]{2,1,0:T(8,128)(2,1)} async-done(((bf16[3,64,1024]{2,1,0:T(8,128)(2,1)}), bf16[3,1024,1024]{2,1,0:T(8,128)(2,1)}) %all-gather.5.cloned.1.call-update) | async-done | bytes 6291472 | tf_op jit(solution)/shard_map/all_gather | solution.py:220
  136.2 3.8 %slice_bitcast_fusion = (bf16[1024,1024]{1,0:T(8,128)(2,1)S(1)}, bf16[1024,1024]{1,0:T(8,128)(2,1)S(1)}, bf16[1024,1024]{1,0:T(8,128)(2,1)S(1)}) fusion(bf16[3,1024,1024]{2,1,0:T(8,128)(2,1)} %all-gather.5.cloned.1.call-done), kind=kLoop, calls=%fused_computation | loop fusion | bytes 12582912 | tf_op jit(solution)/shard_map/squeeze | solution.py:228
  143.5 4.1 %all-to-all-start.3 = ((bf16[8,192,128]{2,1,0:T(8,128)(2,1)}), bf16[8,192,128]{2,1,0:T(8,128)(2,1)S(1)}, u32[]{:S(2)}, u32[]{:S(2)}) async-start(bf16[8,192,128]{2,1,0:T(8,128)(2,1)} %bitcast_bitcast_fusion.2), calls=%async_computation.3 | async-start | bytes 786432 | tf_op jit(solution)/shard_map/all_to_all | solution.py:31
  147.5 4.1 %convolution_convert_fusion.1 = bf16[1024,1024]{1,0:T(8,128)(2,1)S(1)} fusion(bf16[1024,1024]{1,0:T(8,128)(2,1)S(1)} %get-tuple-element.41, bf16[1024,1024]{1,0:T(8,128)(2,1)} %copy-done.4), kind=kOutput, calls=%fused_computation.19 | convolution fusion | flops 2148532224 | bytes 6291456 | tf_op jit(solution)/shard_map/dot_general | solution.py:15
  151.6 2.3 %convolution_convert_fusion = bf16[1024,1024]{1,0:T(8,128)(2,1)S(1)} fusion(bf16[1024,1024]{1,0:T(8,128)(2,1)S(1)} %copy-done.7, bf16[1024,1024]{1,0:T(8,128)(2,1)S(1)} %convolution_convert_fusion.1), kind=kOutput, calls=%fused_computation.18 | convolution fusion | flops 2148532224 | bytes 6291456 | tf_op jit(solution)/shard_map/dot_general | solution.py:15
  154.0 8.7 %all-to-all-done.3 = bf16[8,192,128]{2,1,0:T(8,128)(2,1)S(1)} async-done(((bf16[8,192,128]{2,1,0:T(8,128)(2,1)}), bf16[8,192,128]{2,1,0:T(8,128)(2,1)S(1)}, u32[]{:S(2)}, u32[]{:S(2)}) %all-to-all-start.3) | async-done | bytes 393248 | tf_op jit(solution)/shard_map/all_to_all | solution.py:31
  163.2 1.3 collective-permute-done.18
  168.0 1.0 collective-permute-done.19
  169.0 2.2 %fusion.74 = bf16[128,1024]{1,0:T(8,128)(2,1)S(1)} fusion(bf16[1024,1024]{1,0:T(8,128)(2,1)} %fusion.18.own_ref, bf16[64,1024]{1,0:T(8,128)(2,1)S(1)} %collective-permute-done.19, bf16[64,1024]{1,0:T(8,128)(2,1)S(1)} %get-tuple-element.61, pred[]{:T(512)S(6)} %eq.4), kind=kOutput, calls=%fused_computation.102 | convolution fusion | flops 269615104 | bytes 2621441 | tf_op jit(solution)/shard_map/dot_general | solution.py:15
  173.7 3.5 %all-to-all-start.4 = ((bf16[8,256,128]{2,1,0:T(8,128)(2,1)}), bf16[8,256,128]{2,1,0:T(8,128)(2,1)S(1)}, u32[]{:S(2)}, u32[]{:S(2)}) async-start(bf16[8,256,128]{2,1,0:T(8,128)(2,1)} %bitcast_bitcast_fusion), calls=%async_computation.4 | async-start | bytes 1048576 | tf_op jit(solution)/shard_map/all_to_all | solution.py:31
  177.2 1.3 collective-permute-start.20
  178.5 6.9 %collective-permute-done.20 = bf16[64,1024]{1,0:T(8,128)(2,1)S(1)} collective-permute-done((bf16[64,1024]{1,0:T(8,128)(2,1)S(1)}, bf16[64,1024]{1,0:T(8,128)(2,1)S(1)}, u32[]{:S(2)}, u32[]{:S(2)}) %collective-permute-start.20) | collective-permute-done | bytes 131104 | tf_op jit(solution)/shard_map/ppermute | solution.py:19
  185.4 1.2 collective-permute-start.21
  188.3 6.9 %all-to-all-done.4 = bf16[8,256,128]{2,1,0:T(8,128)(2,1)S(1)} async-done(((bf16[8,256,128]{2,1,0:T(8,128)(2,1)}), bf16[8,256,128]{2,1,0:T(8,128)(2,1)S(1)}, u32[]{:S(2)}, u32[]{:S(2)}) %all-to-all-start.4) | async-done | bytes 524320 | tf_op jit(solution)/shard_map/all_to_all | solution.py:31
  196.0 5.2 %shard_map.29 = bf16[2,1024,128]{2,1,0:T(8,128)(2,1)} custom-call(s32[1]{0:T(128)} %bitcast.core_ref, bf16[8,2,128,128]{3,2,1,0:T(8,128)(2,1)} %bitcast.132, bf16[128,1024]{1,0:T(8,128)(2,1)} %maximum_select_fusion.1.start_ref, bf16[128,1024]{1,0:T(8,128)(2,1)} %get-tuple-element.34.part_ref, bf16[2,1024,128]{2,1,0:T(8,128)(2,1)} %p_ref.1, ...), custom_call_target="tpu_custom_call" | custom-call | flops 536870912 | bytes 5242880 | tf_op jit(solution)/shard_map/pallas_call | solution.py:130
  (90 shorter events, 21.0 us)
Async XLA Ops:
  6.5 9.2 %copy-start.12 = (bf16[2,1024,128]{2,1,0:T(8,128)(2,1)S(1)}, bf16[2,1024,128]{2,1,0:T(8,128)(2,1)}, u32[]{:S(2)}) copy-start(bf16[2,1024,128]{2,1,0:T(8,128)(2,1)} %p_ref.1) | copy-start | bytes 1572868
  12.5 8.0 %collective-permute-start.1 = (bf16[1024,1024]{1,0:T(8,128)(2,1)}, bf16[1024,1024]{1,0:T(8,128)(2,1)S(1)}, u32[]{:S(2)}, u32[]{:S(2)}) collective-permute-start(bf16[1024,1024]{1,0:T(8,128)(2,1)} %fusion.18.own_ref), channel_id=1, source_target_pairs={{0,8},{8,0},{1,9},{9,1},{2,10},{10,2},{3,11},{11,3},{4,12},{12,4},... | collective-permute-start | bytes 6291464 | tf_op jit(solution)/shard_map/ppermute | solution.py:23
  16.5 4.5 %collective-permute-start = (bf16[1024,128]{1,0:T(8,128)(2,1)S(1)}, bf16[1024,128]{1,0:T(8,128)(2,1)S(1)}, u32[]{:S(2)}, u32[]{:S(2)}) collective-permute-start(bf16[1024,128]{1,0:T(8,128)(2,1)S(1)} %get-tuple-element.56), channel_id=1, source_target_pairs={{8,0},{9,1},{10,2},{11,3},{12,4},{13,5},{14,6},{15,7},{24,16},{25,... | collective-permute-start | bytes 786440 | tf_op jit(solution)/shard_map/ppermute | solution.py:182
  20.5 2.8 %copy-start = (bf16[1024,1024]{1,0:T(8,128)(2,1)}, bf16[1024,1024]{1,0:T(8,128)(2,1)S(1)}, u32[]{:S(2)}) copy-start(bf16[1024,1024]{1,0:T(8,128)(2,1)S(1)} %collective-permute-done.1.other_ref) | copy-start | bytes 6291460
  24.2 24.5 %all-to-all-start = ((bf16[8,256,128]{2,1,0:T(8,128)(2,1)}), bf16[8,256,128]{2,1,0:T(8,128)(2,1)S(1)}, u32[]{:S(2)}, u32[]{:S(2)}) async-start(bf16[8,256,128]{2,1,0:T(8,128)(2,1)} %bitcast_bitcast_fusion.1), calls=%async_computation | async-start | bytes 1048576 | tf_op jit(solution)/shard_map/all_to_all | solution.py:193
  30.7 76.4 %all-gather.3.cloned.1.call-start = ((), (), s32[]{:S(2)}) async-start(), calls=%async_computation.5 | async-start | bytes 2228224 | tf_op jit(solution)/shard_map/all_gather | solution.py:198
  35.3 7.1 %collective-permute-start.2 = (bf16[64,1024]{1,0:T(8,128)(2,1)S(1)}, bf16[64,1024]{1,0:T(8,128)(2,1)S(1)}, u32[]{:S(2)}, u32[]{:S(2)}) collective-permute-start(bf16[64,1024]{1,0:T(8,128)(2,1)S(1)} %constant_dynamic-slice_fusion), channel_id=1, source_target_pairs={{16,0},{32,16},{48,32},{64,48},{80,64},{96,80},{112,96},{128,112},... | collective-permute-start | bytes 393224 | tf_op jit(solution)/shard_map/ppermute | solution.py:19
  48.7 1.4 copy-start.8
  48.8 87.5 %all-gather.5.cloned.1.call-start = ((), (), s32[]{:S(2)}) async-start(), calls=%async_computation.6 | async-start | bytes 6684672 | tf_op jit(solution)/shard_map/all_gather | solution.py:220
  48.8 6.7 %collective-permute-start.3 = (bf16[64,1024]{1,0:T(8,128)(2,1)}, bf16[64,1024]{1,0:T(8,128)(2,1)S(1)}, u32[]{:S(2)}, u32[]{:S(2)}) collective-permute-start(bf16[64,1024]{1,0:T(8,128)(2,1)} %convolution_convert_fusion.9), channel_id=1, source_target_pairs={{16,0},{32,16},{48,32},{64,48},{80,64},{96,80},{112,96},{128,112},... | collective-permute-start | bytes 393224 | tf_op jit(solution)/shard_map/ppermute | solution.py:19
  55.3 2.0 copy-start.15
  55.3 3.4 %copy-start.14 = (bf16[128,1024]{1,0:T(8,128)(2,1)S(1)}, bf16[128,1024]{1,0:T(8,128)(2,1)}, u32[]{:S(2)}) copy-start(bf16[128,1024]{1,0:T(8,128)(2,1)} %get-tuple-element.34.part_ref) | copy-start | bytes 786436
  55.6 18.6 %copy-start.13 = (f32[64,1024]{1,0:T(8,128)S(1)}, f32[64,1024]{1,0:T(8,128)}, u32[]{:S(2)}) copy-start(f32[64,1024]{1,0:T(8,128)} %get-tuple-element.31) | copy-start | bytes 786436
  56.1 6.6 %collective-permute-start.6 = (bf16[64,1024]{1,0:T(8,128)(2,1)S(1)}, bf16[64,1024]{1,0:T(8,128)(2,1)S(1)}, u32[]{:S(2)}, u32[]{:S(2)}) collective-permute-start(bf16[64,1024]{1,0:T(8,128)(2,1)S(1)} %convolution_convert_fusion.8), channel_id=1, source_target_pairs={{16,0},{32,16},{48,32},{64,48},{80,64},{96,80},{112,96},{128,112},... | collective-permute-start | bytes 393224 | tf_op jit(solution)/shard_map/ppermute | solution.py:19
  57.4 16.8 %collective-permute-start.4 = (f32[64,1024]{1,0:T(8,128)S(1)}, f32[64,1024]{1,0:T(8,128)S(1)}, u32[]{:S(2)}, u32[]{:S(2)}) collective-permute-start(f32[64,1024]{1,0:T(8,128)S(1)} %copy-done.15), channel_id=1, source_target_pairs={{0,8},{8,0},{1,9},{9,1},{2,10},{10,2},{3,11},{11,3},{4,12},{12,4},... | collective-permute-start | bytes 786440 | tf_op jit(solution)/shard_map/ppermute | solution.py:23
  58.7 16.8 %collective-permute-start.10 = (bf16[128,1024]{1,0:T(8,128)(2,1)S(1)}, bf16[128,1024]{1,0:T(8,128)(2,1)S(1)}, u32[]{:S(2)}, u32[]{:S(2)}) collective-permute-start(bf16[128,1024]{1,0:T(8,128)(2,1)S(1)} %copy-done.14), channel_id=1, source_target_pairs={{8,0},{9,1},{10,2},{11,3},{12,4},{13,5},{14,6},{15,7},{24,16},{25,... | collective-permute-start | bytes 786440 | tf_op jit(solution)/shard_map/ppermute | solution.py:218
  63.2 12.4 %collective-permute-start.9 = (bf16[64,1024]{1,0:T(8,128)(2,1)S(1)}, bf16[64,1024]{1,0:T(8,128)(2,1)S(1)}, u32[]{:S(2)}, u32[]{:S(2)}) collective-permute-start(bf16[64,1024]{1,0:T(8,128)(2,1)S(1)} %convolution_convert_fusion.7), channel_id=1, source_target_pairs={{128,240},{144,0},{160,16},{176,32},{192,48},{208,64},{224,80},{24... | collective-permute-start | bytes 393224 | tf_op jit(solution)/shard_map/ppermute | solution.py:19
  64.5 11.1 %collective-permute-start.8 = (bf16[64,1024]{1,0:T(8,128)(2,1)S(1)}, bf16[64,1024]{1,0:T(8,128)(2,1)S(1)}, u32[]{:S(2)}, u32[]{:S(2)}) collective-permute-start(bf16[64,1024]{1,0:T(8,128)(2,1)S(1)} %convolution_convert_fusion.7), channel_id=1, source_target_pairs={{64,240},{80,0},{96,16},{112,32},{128,48},{144,64},{160,80},{176,9... | collective-permute-start | bytes 393224 | tf_op jit(solution)/shard_map/ppermute | solution.py:19
  65.8 10.4 %collective-permute-start.7 = (bf16[64,1024]{1,0:T(8,128)(2,1)S(1)}, bf16[64,1024]{1,0:T(8,128)(2,1)S(1)}, u32[]{:S(2)}, u32[]{:S(2)}) collective-permute-start(bf16[64,1024]{1,0:T(8,128)(2,1)S(1)} %convolution_convert_fusion.7), channel_id=1, source_target_pairs={{0,240},{16,0},{32,16},{48,32},{64,48},{80,64},{96,80},{112,96},{1... | collective-permute-start | bytes 393224 | tf_op jit(solution)/shard_map/ppermute | solution.py:19
  74.2 6.1 %collective-permute-start.5 = (bf16[64,1024]{1,0:T(8,128)(2,1)S(1)}, bf16[64,1024]{1,0:T(8,128)(2,1)S(1)}, u32[]{:S(2)}, u32[]{:S(2)}) collective-permute-start(bf16[64,1024]{1,0:T(8,128)(2,1)S(1)} %add_convert_fusion.2), channel_id=1, source_target_pairs={{16,0},{32,16},{48,32},{64,48},{80,64},{96,80},{112,96},{128,112},... | collective-permute-start | bytes 393224 | tf_op jit(solution)/shard_map/ppermute | solution.py:19
  92.0 6.3 %collective-permute-start.11 = (bf16[8,64,128]{2,1,0:T(8,128)(2,1)S(1)}, bf16[8,64,128]{2,1,0:T(8,128)(2,1)S(1)}, u32[]{:S(2)}, u32[]{:S(2)}) collective-permute-start(bf16[8,64,128]{2,1,0:T(8,128)(2,1)S(1)} %all_to_all.25), channel_id=1, source_target_pairs={{0,8},{8,0},{1,9},{9,1},{2,10},{10,2},{3,11},{11,3},{4,12},{12,4},... | collective-permute-start | bytes 393224 | tf_op jit(solution)/shard_map/ppermute | solution.py:23
  99.0 8.1 %collective-permute-start.12 = (bf16[64,1024]{1,0:T(8,128)(2,1)S(1)}, bf16[64,1024]{1,0:T(8,128)(2,1)S(1)}, u32[]{:S(2)}, u32[]{:S(2)}) collective-permute-start(bf16[64,1024]{1,0:T(8,128)(2,1)S(1)} %add_convert_fusion.1), channel_id=1, source_target_pairs={{32,0},{48,16},{64,32},{80,48},{96,64},{112,80},{128,96},{144,112}... | collective-permute-start | bytes 393224 | tf_op jit(solution)/shard_map/ppermute | solution.py:19
  107.1 17.9 %copy-start.3 = (bf16[1024,1024]{1,0:T(8,128)(2,1)S(1)}, bf16[1024,1024]{1,0:T(8,128)(2,1)}, u32[]{:S(2)}) copy-start(bf16[1024,1024]{1,0:T(8,128)(2,1)} %all-gather.3.cloned.1.call-done) | copy-start | bytes 6291460
  122.0 3.0 %collective-permute-start.13 = (bf16[8,64,128]{2,1,0:T(8,128)(2,1)S(1)}, bf16[8,64,128]{2,1,0:T(8,128)(2,1)S(1)}, u32[]{:S(2)}, u32[]{:S(2)}) collective-permute-start(bf16[8,64,128]{2,1,0:T(8,128)(2,1)S(1)} %all_to_all.26), channel_id=1, source_target_pairs={{0,8},{8,0},{1,9},{9,1},{2,10},{10,2},{3,11},{11,3},{4,12},{12,4},... | collective-permute-start | bytes 393224 | tf_op jit(solution)/shard_map/ppermute | solution.py:23
  125.7 28.3 %collective-permute-start.17 = (bf16[64,1024]{1,0:T(8,128)(2,1)S(1)}, bf16[64,1024]{1,0:T(8,128)(2,1)S(1)}, u32[]{:S(2)}, u32[]{:S(2)}) collective-permute-start(bf16[64,1024]{1,0:T(8,128)(2,1)S(1)} %fusion.43), channel_id=1, source_target_pairs={{0,240},{16,0},{32,16},{48,32},{64,48},{80,64},{96,80},{112,96},{1... | collective-permute-start | bytes 393224 | tf_op jit(solution)/shard_map/ppermute | solution.py:19
  127.3 12.7 %collective-permute-start.16 = (bf16[64,1024]{1,0:T(8,128)(2,1)S(1)}, bf16[64,1024]{1,0:T(8,128)(2,1)S(1)}, u32[]{:S(2)}, u32[]{:S(2)}) collective-permute-start(bf16[64,1024]{1,0:T(8,128)(2,1)S(1)} %fusion.43), channel_id=1, source_target_pairs={{192,240},{208,0},{224,16},{240,32},{193,241},{209,1},{225,17},{24... | collective-permute-start | bytes 393224 | tf_op jit(solution)/shard_map/ppermute | solution.py:19
  128.6 11.9 %collective-permute-start.15 = (bf16[64,1024]{1,0:T(8,128)(2,1)S(1)}, bf16[64,1024]{1,0:T(8,128)(2,1)S(1)}, u32[]{:S(2)}, u32[]{:S(2)}) collective-permute-start(bf16[64,1024]{1,0:T(8,128)(2,1)S(1)} %fusion.43), channel_id=1, source_target_pairs={{128,240},{144,0},{160,16},{176,32},{192,48},{208,64},{224,80},{24... | collective-permute-start | bytes 393224 | tf_op jit(solution)/shard_map/ppermute | solution.py:19
  129.9 11.5 %collective-permute-start.14 = (bf16[64,1024]{1,0:T(8,128)(2,1)S(1)}, bf16[64,1024]{1,0:T(8,128)(2,1)S(1)}, u32[]{:S(2)}, u32[]{:S(2)}) collective-permute-start(bf16[64,1024]{1,0:T(8,128)(2,1)S(1)} %fusion.43), channel_id=1, source_target_pairs={{64,240},{80,0},{96,16},{112,32},{128,48},{144,64},{160,80},{176,9... | collective-permute-start | bytes 393224 | tf_op jit(solution)/shard_map/ppermute | solution.py:19
  140.0 1.4 copy-start.6
  140.0 2.0 copy-start.4
  143.5 19.2 %all-to-all-start.3 = ((bf16[8,192,128]{2,1,0:T(8,128)(2,1)}), bf16[8,192,128]{2,1,0:T(8,128)(2,1)S(1)}, u32[]{:S(2)}, u32[]{:S(2)}) async-start(bf16[8,192,128]{2,1,0:T(8,128)(2,1)} %bitcast_bitcast_fusion.2), calls=%async_computation.3 | async-start | bytes 786432 | tf_op jit(solution)/shard_map/all_to_all | solution.py:31
  147.5 4.1 %copy-start.7 = (bf16[1024,1024]{1,0:T(8,128)(2,1)S(1)}, bf16[1024,1024]{1,0:T(8,128)(2,1)}, u32[]{:S(2)}) copy-start(bf16[1024,1024]{1,0:T(8,128)(2,1)} %copy-done.6) | copy-start | bytes 6291460
  151.6 2.4 %copy-start.9 = (bf16[1024,1024]{1,0:T(8,128)(2,1)}, bf16[1024,1024]{1,0:T(8,128)(2,1)S(1)}, u32[]{:S(2)}) copy-start(bf16[1024,1024]{1,0:T(8,128)(2,1)S(1)} %convolution_convert_fusion.1) | copy-start | bytes 6291460
  162.7 1.8 collective-permute-start.18
  163.2 1.6 copy-start.5
  164.7 1.6 copy-start.10
  167.6 3.6 %copy-start.1 = (bf16[1024,1024]{1,0:T(8,128)(2,1)S(1)}, bf16[1024,1024]{1,0:T(8,128)(2,1)}, u32[]{:S(2)}) copy-start(bf16[1024,1024]{1,0:T(8,128)(2,1)} %copy-done) | copy-start | bytes 6291460
  167.6 1.4 collective-permute-start.19
  169.0 2.9 %copy-start.2 = (bf16[2,1024,1024]{2,1,0:T(8,128)(2,1)S(1)}, bf16[2,1024,1024]{2,1,0:T(8,128)(2,1)}, u32[]{:S(2)}) copy-start(bf16[2,1024,1024]{2,1,0:T(8,128)(2,1)} %k_ref.3) | copy-start | bytes 12582916
  173.7 21.4 %all-to-all-start.4 = ((bf16[8,256,128]{2,1,0:T(8,128)(2,1)}), bf16[8,256,128]{2,1,0:T(8,128)(2,1)S(1)}, u32[]{:S(2)}, u32[]{:S(2)}) async-start(bf16[8,256,128]{2,1,0:T(8,128)(2,1)} %bitcast_bitcast_fusion), calls=%async_computation.4 | async-start | bytes 1048576 | tf_op jit(solution)/shard_map/all_to_all | solution.py:31
  177.2 8.1 %collective-permute-start.20 = (bf16[64,1024]{1,0:T(8,128)(2,1)S(1)}, bf16[64,1024]{1,0:T(8,128)(2,1)S(1)}, u32[]{:S(2)}, u32[]{:S(2)}) collective-permute-start(bf16[64,1024]{1,0:T(8,128)(2,1)S(1)} %get-tuple-element.62), channel_id=1, source_target_pairs={{0,16},{16,32},{32,48},{48,64},{64,80},{80,96},{96,112},{112,128},... | collective-permute-start | bytes 393224 | tf_op jit(solution)/shard_map/ppermute | solution.py:19
  185.4 2.2 %collective-permute-start.21 = (bf16[64,1024]{1,0:T(8,128)(2,1)S(1)}, bf16[64,1024]{1,0:T(8,128)(2,1)S(1)}, u32[]{:S(2)}, u32[]{:S(2)}) collective-permute-start(bf16[64,1024]{1,0:T(8,128)(2,1)S(1)} %collective-permute-done.20), channel_id=1, source_target_pairs={{0,8},{8,0},{1,9},{9,1},{2,10},{10,2},{3,11},{11,3},{4,12},{12,4},... | collective-permute-start | bytes 393224 | tf_op jit(solution)/shard_map/ppermute | solution.py:23
  195.2 0.8 copy-start.11
Sparse Core Ops, SparseCore 0:
  48.9 38.1 all-gather.2
  88.9 47.2 all-gather.4

commit v5 on v4

--- a/solution.py
+++ b/solution.py
@@ -235,7 +235,8 @@
     far = from_other_core(got)
     full = jnp.stack([side(got, far), side(far, got)], axis=1).reshape(8, 2, 3, half, width)
     y = [half_rows(full[:, :, j].reshape(order, width).T, core) for j in range(3)]
-    total = dot(y[0], phis[0]) + dot(y[1], phi8) + dot(y[2], phi12)
+    total = dot(y[2], phi12) + dot(y[1], phi8)
+    total = lax.optimization_barrier(total) + dot(y[0], phis[0])
     reduced = (base.astype(F32) + total).astype(BF16)
 
     start = both_halves(moved(reduced, [(c, (c + 1) % chips) for c in range(chips)]))

time: 209 us -> 209 us (level)
  no operation moved by 1% of the time
where the time goes in v5:
time: 209 us; the launch traced here: 208 us
  waiting for transfers between devices  57.6 us (28%)
  starting transfers between devices  56.2 us (27%)
  matrix products  34.9 us (17%)
  blocking collectives  22.9 us (11%)
  between operations  14 us (7%)
  Pallas kernels  10.4 us (5%)
  local copies, waits for them, and re-layouts  9.42 us (5%)
  other arithmetic  2.76 us (1%)
    dot_general x23, matrix products, dot(): return jnp.dot(left, right, preferred_element_type=F32)  32.8 us
    ppermute x13, waiting for transfers between devices, moved(): return lax.ppermute(block, CHIPS, pairs)  26.5 us
    ppermute x13, starting transfers between devices, moved(): return lax.ppermute(block, CHIPS, pairs)  24.2 us
    all_to_all x2, blocking collectives, turned(): return lax.all_to_all(pieces, 'z', 0, 0, tiled=True)  22.9 us
    all_to_all x2, waiting for transfers between devices, turned(): return lax.all_to_all(pieces, 'z', 0, 0, tiled=True)  15.6 us
    ppermute x7, starting transfers between devices, from_other_core(): return lax.ppermute(block, 'core', [(0, 1), (1, 0)])  14 us
    all_to_all x2, starting transfers between devices, turned(): return lax.all_to_all(pieces, 'z', 0, 0, tiled=True)  7.57 us
    all_to_all x1, starting transfers between devices, shards(): got = lax.all_to_all(pieces, 'z', 0, 0, tiled=True)  6.45 us
  transfers between devices with their start and end apart: 27, of which 16 were waited for; matrix products, arithmetic and copies ran while one was open for 14% of the time, Pallas kernels for 3%

profile of v5, /device:TPU:1, one launch (start us, length us, event | category | flops | bytes accessed | tf_op | source)
XLA Modules:
  0.0 208.1 jit_solution(392515999490453950)
XLA Ops:
  6.5 6.0 %fusion.18.own_ref = bf16[1024,1024]{1,0:T(8,128)(2,1)} fusion(bf16[2,1024,1024]{2,1,0:T(8,128)(2,1)} %k_ref.3), kind=kOutput, calls=%fused_computation.17 | convolution fusion | flops 2148532224 | bytes 6291456 | tf_op jit(solution)/shard_map/dot_general | solution.py:15
  12.5 3.2 %collective-permute-start.1 = (bf16[1024,1024]{1,0:T(8,128)(2,1)}, bf16[1024,1024]{1,0:T(8,128)(2,1)S(1)}, u32[]{:S(2)}, u32[]{:S(2)}) collective-permute-start(bf16[1024,1024]{1,0:T(8,128)(2,1)} %fusion.18.own_ref), channel_id=1, source_target_pairs={{0,8},{8,0},{1,9},{9,1},{2,10},{10,2},{3,11},{11,3},{4,12},{12,4},... | collective-permute-start | bytes 6291464 | tf_op jit(solution)/shard_map/ppermute | solution.py:23
  16.5 1.9 collective-permute-start
  18.4 2.1 fusion.29
  21.0 2.3 %fusion.38 = bf16[128,1024]{1,0:T(8,128)(2,1)S(1)} fusion(bf16[128,1024]{1,0:T(8,128)(2,1)S(1)} %fusion.74, bf16[1024,1024]{1,0:T(8,128)(2,1)} %fusion.18.own_ref, bf16[1024,128]{1,0:T(8,128)(2,1)S(1)} %collective-permute-done, pred[]{:T(512)S(6)} %eq.4), kind=kOutput, calls=%fused_computation.33 | convolution fusion | flops 268566528 | bytes 2883585 | tf_op jit(solution)/shard_map/dot_general | solution.py:15
  24.2 6.5 %all-to-all-start = ((bf16[8,256,128]{2,1,0:T(8,128)(2,1)}), bf16[8,256,128]{2,1,0:T(8,128)(2,1)S(1)}, u32[]{:S(2)}, u32[]{:S(2)}) async-start(bf16[8,256,128]{2,1,0:T(8,128)(2,1)} %bitcast_bitcast_fusion.1), calls=%async_computation | async-start | bytes 1048576 | tf_op jit(solution)/shard_map/all_to_all | solution.py:193
  30.7 4.6 %fusion.13 = bf16[1024,1024]{1,0:T(8,128)(2,1)S(1)} fusion(bf16[1024,1024]{1,0:T(8,128)(2,1)} %fusion.18.own_ref, bf16[1024,1024]{1,0:T(8,128)(2,1)} %copy-done, pred[]{:T(512)S(6)} %eq.4), kind=kOutput, calls=%fused_computation.16 | convolution fusion | flops 2150629376 | bytes 6291457 | tf_op jit(solution)/shard_map/dot_general | solution.py:15
  35.3 1.3 collective-permute-start.2
  36.6 5.8 %collective-permute-done.2 = bf16[64,1024]{1,0:T(8,128)(2,1)S(1)} collective-permute-done((bf16[64,1024]{1,0:T(8,128)(2,1)S(1)}, bf16[64,1024]{1,0:T(8,128)(2,1)S(1)}, u32[]{:S(2)}, u32[]{:S(2)}) %collective-permute-start.2) | collective-permute-done | bytes 131104 | tf_op jit(solution)/shard_map/ppermute | solution.py:19
  42.5 1.2 convolution_convert_fusion.9
  43.6 5.1 %all-to-all-done = bf16[8,256,128]{2,1,0:T(8,128)(2,1)S(1)} async-done(((bf16[8,256,128]{2,1,0:T(8,128)(2,1)}), bf16[8,256,128]{2,1,0:T(8,128)(2,1)S(1)}, u32[]{:S(2)}, u32[]{:S(2)}) %all-to-all-start) | async-done | bytes 524320 | tf_op jit(solution)/shard_map/all_to_all | solution.py:193
  48.8 1.3 collective-permute-start.3
  50.1 5.2 %shard_map.28 = (bf16[128,1024]{1,0:T(8,128)(2,1)}, f32[64,1024]{1,0:T(8,128)}, f32[64,1024]{1,0:T(8,128)}) custom-call(s32[1]{0:T(128)} %bitcast.core_ref, bf16[8,2,128,128]{3,2,1,0:T(8,128)(2,1)} %bitcast.131, bf16[1,1024,128]{2,1,0:T(8,128)(2,1)} %get-tuple-element.57.p_ref, bf16[2,1024,1024]{2,1,0:T(8,128)(2,1)} %k_ref.3, ...), custom_call_target="tpu_custom_call" | custom-call | flops 16777216 | bytes 131072 | tf_op jit(solution)/shard_map/pallas_call | solution.py:78
  56.1 1.3 collective-permute-start.6
  57.4 1.4 collective-permute-start.4
  58.7 1.9 collective-permute-start.10
  60.7 2.0 collective-permute-done.6
  63.2 1.3 collective-permute-start.9
  64.5 1.3 collective-permute-start.8
  65.8 8.4 %collective-permute-start.7 = (bf16[64,1024]{1,0:T(8,128)(2,1)S(1)}, bf16[64,1024]{1,0:T(8,128)(2,1)S(1)}, u32[]{:S(2)}, u32[]{:S(2)}) collective-permute-start(bf16[64,1024]{1,0:T(8,128)(2,1)S(1)} %convolution_convert_fusion.7), channel_id=1, source_target_pairs={{0,240},{16,0},{32,16},{48,32},{64,48},{80,64},{96,80},{112,96},{1... | collective-permute-start | bytes 393224 | tf_op jit(solution)/shard_map/ppermute | solution.py:19
  74.2 1.3 collective-permute-start.5
  76.1 4.2 %collective-permute-done.5 = bf16[64,1024]{1,0:T(8,128)(2,1)S(1)} collective-permute-done((bf16[64,1024]{1,0:T(8,128)(2,1)S(1)}, bf16[64,1024]{1,0:T(8,128)(2,1)S(1)}, u32[]{:S(2)}, u32[]{:S(2)}) %collective-permute-start.5) | collective-permute-done | bytes 131104 | tf_op jit(solution)/shard_map/ppermute | solution.py:19
  81.7 10.3 %all_to_all.25 = bf16[8,64,128]{2,1,0:T(8,128)(2,1)S(1)} all-to-all(bf16[8,64,128]{2,1,0:T(8,128)(2,1)S(1)} %bitcast_bitcast_fusion.4), channel_id=1, replica_groups=mesh['y'=4,'x'=4,'core'=2,'z'=8] {'z'}, dimensions={0} | all-to-all | bytes 262144 | tf_op jit(solution)/shard_map/all_to_all | solution.py:31
  92.0 5.3 %collective-permute-start.11 = (bf16[8,64,128]{2,1,0:T(8,128)(2,1)S(1)}, bf16[8,64,128]{2,1,0:T(8,128)(2,1)S(1)}, u32[]{:S(2)}, u32[]{:S(2)}) collective-permute-start(bf16[8,64,128]{2,1,0:T(8,128)(2,1)S(1)} %all_to_all.25), channel_id=1, source_target_pairs={{0,8},{8,0},{1,9},{9,1},{2,10},{10,2},{3,11},{11,3},{4,12},{12,4},... | collective-permute-start | bytes 393224 | tf_op jit(solution)/shard_map/ppermute | solution.py:23
  97.3 1.0 collective-permute-done.11
  99.0 1.3 collective-permute-start.12
  100.3 6.8 %collective-permute-done.12 = bf16[64,1024]{1,0:T(8,128)(2,1)S(1)} collective-permute-done((bf16[64,1024]{1,0:T(8,128)(2,1)S(1)}, bf16[64,1024]{1,0:T(8,128)(2,1)S(1)}, u32[]{:S(2)}, u32[]{:S(2)}) %collective-permute-start.12) | collective-permute-done | bytes 131104 | tf_op jit(solution)/shard_map/ppermute | solution.py:19
  107.1 2.3 %convolution_convert_fusion.5 = bf16[64,1024]{1,0:T(8,128)(2,1)S(1)} fusion(bf16[64,1024]{1,0:T(8,128)(2,1)S(1)} %collective-permute-done.12, bf16[1024,1024]{1,0:T(8,128)(2,1)} %all-gather.3.cloned.1.call-done), kind=kOutput, calls=%fused_computation.41 | convolution fusion | flops 134283264 | bytes 2359296 | tf_op jit(solution)/shard_map/dot_general | solution.py:15
  109.4 12.5 %all_to_all.26 = bf16[8,64,128]{2,1,0:T(8,128)(2,1)S(1)} all-to-all(bf16[8,64,128]{2,1,0:T(8,128)(2,1)S(1)} %bitcast_bitcast_fusion.3), channel_id=1, replica_groups=mesh['y'=4,'x'=4,'core'=2,'z'=8] {'z'}, dimensions={0} | all-to-all | bytes 262144 | tf_op jit(solution)/shard_map/all_to_all | solution.py:31
  122.0 2.0 collective-permute-start.13
  125.7 1.6 collective-permute-start.17
  127.3 1.3 collective-permute-start.16
  128.6 1.3 collective-permute-start.15
  129.9 1.3 collective-permute-start.14
  131.2 5.0 %all-gather.5.cloned.1.call-done = bf16[3,1024,1024]{2,1,0:T(8,128)(2,1)} async-done(((bf16[3,64,1024]{2,1,0:T(8,128)(2,1)}), bf16[3,1024,1024]{2,1,0:T(8,128)(2,1)}) %all-gather.5.cloned.1.call-update) | async-done | bytes 6291472 | tf_op jit(solution)/shard_map/all_gather | solution.py:220
  136.2 3.8 %slice_bitcast_fusion = (bf16[1024,1024]{1,0:T(8,128)(2,1)S(1)}, bf16[1024,1024]{1,0:T(8,128)(2,1)S(1)}, bf16[1024,1024]{1,0:T(8,128)(2,1)S(1)}) fusion(bf16[3,1024,1024]{2,1,0:T(8,128)(2,1)} %all-gather.5.cloned.1.call-done), kind=kLoop, calls=%fused_computation | loop fusion | bytes 12582912 | tf_op jit(solution)/shard_map/squeeze | solution.py:228
  143.5 4.1 %all-to-all-start.3 = ((bf16[8,192,128]{2,1,0:T(8,128)(2,1)}), bf16[8,192,128]{2,1,0:T(8,128)(2,1)S(1)}, u32[]{:S(2)}, u32[]{:S(2)}) async-start(bf16[8,192,128]{2,1,0:T(8,128)(2,1)} %bitcast_bitcast_fusion.2), calls=%async_computation.3 | async-start | bytes 786432 | tf_op jit(solution)/shard_map/all_to_all | solution.py:31
  147.5 4.1 %convolution_convert_fusion.1 = bf16[1024,1024]{1,0:T(8,128)(2,1)S(1)} fusion(bf16[1024,1024]{1,0:T(8,128)(2,1)S(1)} %get-tuple-element.41, bf16[1024,1024]{1,0:T(8,128)(2,1)} %copy-done.4), kind=kOutput, calls=%fused_computation.19 | convolution fusion | flops 2148532224 | bytes 6291456 | tf_op jit(solution)/shard_map/dot_general | solution.py:15
  151.6 2.3 %convolution_convert_fusion = bf16[1024,1024]{1,0:T(8,128)(2,1)S(1)} fusion(bf16[1024,1024]{1,0:T(8,128)(2,1)S(1)} %copy-done.7, bf16[1024,1024]{1,0:T(8,128)(2,1)S(1)} %convolution_convert_fusion.1), kind=kOutput, calls=%fused_computation.18 | convolution fusion | flops 2148532224 | bytes 6291456 | tf_op jit(solution)/shard_map/dot_general | solution.py:15
  154.0 8.7 %all-to-all-done.3 = bf16[8,192,128]{2,1,0:T(8,128)(2,1)S(1)} async-done(((bf16[8,192,128]{2,1,0:T(8,128)(2,1)}), bf16[8,192,128]{2,1,0:T(8,128)(2,1)S(1)}, u32[]{:S(2)}, u32[]{:S(2)}) %all-to-all-start.3) | async-done | bytes 393248 | tf_op jit(solution)/shard_map/all_to_all | solution.py:31
  163.2 1.3 collective-permute-done.18
  169.1 2.2 %fusion.72 = bf16[128,1024]{1,0:T(8,128)(2,1)S(1)} fusion(bf16[1024,1024]{1,0:T(8,128)(2,1)} %fusion.18.own_ref, bf16[64,1024]{1,0:T(8,128)(2,1)S(1)} %collective-permute-done.19, bf16[64,1024]{1,0:T(8,128)(2,1)S(1)} %get-tuple-element.47, pred[]{:T(512)S(6)} %eq.4), kind=kOutput, calls=%fused_computation.102 | convolution fusion | flops 269615104 | bytes 2621441 | tf_op jit(solution)/shard_map/dot_general | solution.py:15
  173.8 3.5 %all-to-all-start.4 = ((bf16[8,256,128]{2,1,0:T(8,128)(2,1)}), bf16[8,256,128]{2,1,0:T(8,128)(2,1)S(1)}, u32[]{:S(2)}, u32[]{:S(2)}) async-start(bf16[8,256,128]{2,1,0:T(8,128)(2,1)} %bitcast_bitcast_fusion), calls=%async_computation.4 | async-start | bytes 1048576 | tf_op jit(solution)/shard_map/all_to_all | solution.py:31
  177.3 1.3 collective-permute-start.20
  178.6 6.9 %collective-permute-done.20 = bf16[64,1024]{1,0:T(8,128)(2,1)S(1)} collective-permute-done((bf16[64,1024]{1,0:T(8,128)(2,1)S(1)}, bf16[64,1024]{1,0:T(8,128)(2,1)S(1)}, u32[]{:S(2)}, u32[]{:S(2)}) %collective-permute-start.20) | collective-permute-done | bytes 131104 | tf_op jit(solution)/shard_map/ppermute | solution.py:19
  185.4 1.2 collective-permute-start.21
  188.4 6.9 %all-to-all-done.4 = bf16[8,256,128]{2,1,0:T(8,128)(2,1)S(1)} async-done(((bf16[8,256,128]{2,1,0:T(8,128)(2,1)}), bf16[8,256,128]{2,1,0:T(8,128)(2,1)S(1)}, u32[]{:S(2)}, u32[]{:S(2)}) %all-to-all-start.4) | async-done | bytes 524320 | tf_op jit(solution)/shard_map/all_to_all | solution.py:31
  196.1 5.2 %shard_map.29 = bf16[2,1024,128]{2,1,0:T(8,128)(2,1)} custom-call(s32[1]{0:T(128)} %bitcast.core_ref, bf16[8,2,128,128]{3,2,1,0:T(8,128)(2,1)} %bitcast.132, bf16[128,1024]{1,0:T(8,128)(2,1)} %maximum_select_fusion.1.start_ref, bf16[128,1024]{1,0:T(8,128)(2,1)} %get-tuple-element.34.part_ref, bf16[2,1024,128]{2,1,0:T(8,128)(2,1)} %p_ref.1, ...), custom_call_target="tpu_custom_call" | custom-call | flops 536870912 | bytes 5242880 | tf_op jit(solution)/shard_map/pallas_call | solution.py:130
  (91 shorter events, 21.1 us)
Async XLA Ops:
  6.5 9.2 %copy-start.12 = (bf16[2,1024,128]{2,1,0:T(8,128)(2,1)S(1)}, bf16[2,1024,128]{2,1,0:T(8,128)(2,1)}, u32[]{:S(2)}) copy-start(bf16[2,1024,128]{2,1,0:T(8,128)(2,1)} %p_ref.1) | copy-start | bytes 1572868
  12.5 8.0 %collective-permute-start.1 = (bf16[1024,1024]{1,0:T(8,128)(2,1)}, bf16[1024,1024]{1,0:T(8,128)(2,1)S(1)}, u32[]{:S(2)}, u32[]{:S(2)}) collective-permute-start(bf16[1024,1024]{1,0:T(8,128)(2,1)} %fusion.18.own_ref), channel_id=1, source_target_pairs={{0,8},{8,0},{1,9},{9,1},{2,10},{10,2},{3,11},{11,3},{4,12},{12,4},... | collective-permute-start | bytes 6291464 | tf_op jit(solution)/shard_map/ppermute | solution.py:23
  16.5 4.5 %collective-permute-start = (bf16[1024,128]{1,0:T(8,128)(2,1)S(1)}, bf16[1024,128]{1,0:T(8,128)(2,1)S(1)}, u32[]{:S(2)}, u32[]{:S(2)}) collective-permute-start(bf16[1024,128]{1,0:T(8,128)(2,1)S(1)} %get-tuple-element.58), channel_id=1, source_target_pairs={{8,0},{9,1},{10,2},{11,3},{12,4},{13,5},{14,6},{15,7},{24,16},{25,... | collective-permute-start | bytes 786440 | tf_op jit(solution)/shard_map/ppermute | solution.py:182
  20.5 2.8 %copy-start = (bf16[1024,1024]{1,0:T(8,128)(2,1)}, bf16[1024,1024]{1,0:T(8,128)(2,1)S(1)}, u32[]{:S(2)}) copy-start(bf16[1024,1024]{1,0:T(8,128)(2,1)S(1)} %collective-permute-done.1.other_ref) | copy-start | bytes 6291460
  24.2 24.5 %all-to-all-start = ((bf16[8,256,128]{2,1,0:T(8,128)(2,1)}), bf16[8,256,128]{2,1,0:T(8,128)(2,1)S(1)}, u32[]{:S(2)}, u32[]{:S(2)}) async-start(bf16[8,256,128]{2,1,0:T(8,128)(2,1)} %bitcast_bitcast_fusion.1), calls=%async_computation | async-start | bytes 1048576 | tf_op jit(solution)/shard_map/all_to_all | solution.py:193
  30.7 76.4 %all-gather.3.cloned.1.call-start = ((), (), s32[]{:S(2)}) async-start(), calls=%async_computation.5 | async-start | bytes 2228224 | tf_op jit(solution)/shard_map/all_gather | solution.py:198
  35.3 7.1 %collective-permute-start.2 = (bf16[64,1024]{1,0:T(8,128)(2,1)S(1)}, bf16[64,1024]{1,0:T(8,128)(2,1)S(1)}, u32[]{:S(2)}, u32[]{:S(2)}) collective-permute-start(bf16[64,1024]{1,0:T(8,128)(2,1)S(1)} %constant_dynamic-slice_fusion), channel_id=1, source_target_pairs={{16,0},{32,16},{48,32},{64,48},{80,64},{96,80},{112,96},{128,112},... | collective-permute-start | bytes 393224 | tf_op jit(solution)/shard_map/ppermute | solution.py:19
  48.7 1.4 copy-start.8
  48.8 87.5 %all-gather.5.cloned.1.call-start = ((), (), s32[]{:S(2)}) async-start(), calls=%async_computation.6 | async-start | bytes 6684672 | tf_op jit(solution)/shard_map/all_gather | solution.py:220
  48.8 6.7 %collective-permute-start.3 = (bf16[64,1024]{1,0:T(8,128)(2,1)}, bf16[64,1024]{1,0:T(8,128)(2,1)S(1)}, u32[]{:S(2)}, u32[]{:S(2)}) collective-permute-start(bf16[64,1024]{1,0:T(8,128)(2,1)} %convolution_convert_fusion.9), channel_id=1, source_target_pairs={{16,0},{32,16},{48,32},{64,48},{80,64},{96,80},{112,96},{128,112},... | collective-permute-start | bytes 393224 | tf_op jit(solution)/shard_map/ppermute | solution.py:19
  55.3 2.0 copy-start.15
  55.3 3.4 %copy-start.14 = (bf16[128,1024]{1,0:T(8,128)(2,1)S(1)}, bf16[128,1024]{1,0:T(8,128)(2,1)}, u32[]{:S(2)}) copy-start(bf16[128,1024]{1,0:T(8,128)(2,1)} %get-tuple-element.34.part_ref) | copy-start | bytes 786436
  55.6 18.6 %copy-start.13 = (f32[64,1024]{1,0:T(8,128)S(1)}, f32[64,1024]{1,0:T(8,128)}, u32[]{:S(2)}) copy-start(f32[64,1024]{1,0:T(8,128)} %get-tuple-element.31) | copy-start | bytes 786436
  56.1 6.6 %collective-permute-start.6 = (bf16[64,1024]{1,0:T(8,128)(2,1)S(1)}, bf16[64,1024]{1,0:T(8,128)(2,1)S(1)}, u32[]{:S(2)}, u32[]{:S(2)}) collective-permute-start(bf16[64,1024]{1,0:T(8,128)(2,1)S(1)} %convolution_convert_fusion.8), channel_id=1, source_target_pairs={{16,0},{32,16},{48,32},{64,48},{80,64},{96,80},{112,96},{128,112},... | collective-permute-start | bytes 393224 | tf_op jit(solution)/shard_map/ppermute | solution.py:19
  57.4 16.8 %collective-permute-start.4 = (f32[64,1024]{1,0:T(8,128)S(1)}, f32[64,1024]{1,0:T(8,128)S(1)}, u32[]{:S(2)}, u32[]{:S(2)}) collective-permute-start(f32[64,1024]{1,0:T(8,128)S(1)} %copy-done.15), channel_id=1, source_target_pairs={{0,8},{8,0},{1,9},{9,1},{2,10},{10,2},{3,11},{11,3},{4,12},{12,4},... | collective-permute-start | bytes 786440 | tf_op jit(solution)/shard_map/ppermute | solution.py:23
  58.7 16.8 %collective-permute-start.10 = (bf16[128,1024]{1,0:T(8,128)(2,1)S(1)}, bf16[128,1024]{1,0:T(8,128)(2,1)S(1)}, u32[]{:S(2)}, u32[]{:S(2)}) collective-permute-start(bf16[128,1024]{1,0:T(8,128)(2,1)S(1)} %copy-done.14), channel_id=1, source_target_pairs={{8,0},{9,1},{10,2},{11,3},{12,4},{13,5},{14,6},{15,7},{24,16},{25,... | collective-permute-start | bytes 786440 | tf_op jit(solution)/shard_map/ppermute | solution.py:218
  63.2 12.4 %collective-permute-start.9 = (bf16[64,1024]{1,0:T(8,128)(2,1)S(1)}, bf16[64,1024]{1,0:T(8,128)(2,1)S(1)}, u32[]{:S(2)}, u32[]{:S(2)}) collective-permute-start(bf16[64,1024]{1,0:T(8,128)(2,1)S(1)} %convolution_convert_fusion.7), channel_id=1, source_target_pairs={{128,240},{144,0},{160,16},{176,32},{192,48},{208,64},{224,80},{24... | collective-permute-start | bytes 393224 | tf_op jit(solution)/shard_map/ppermute | solution.py:19
  64.5 11.1 %collective-permute-start.8 = (bf16[64,1024]{1,0:T(8,128)(2,1)S(1)}, bf16[64,1024]{1,0:T(8,128)(2,1)S(1)}, u32[]{:S(2)}, u32[]{:S(2)}) collective-permute-start(bf16[64,1024]{1,0:T(8,128)(2,1)S(1)} %convolution_convert_fusion.7), channel_id=1, source_target_pairs={{64,240},{80,0},{96,16},{112,32},{128,48},{144,64},{160,80},{176,9... | collective-permute-start | bytes 393224 | tf_op jit(solution)/shard_map/ppermute | solution.py:19
  65.8 10.4 %collective-permute-start.7 = (bf16[64,1024]{1,0:T(8,128)(2,1)S(1)}, bf16[64,1024]{1,0:T(8,128)(2,1)S(1)}, u32[]{:S(2)}, u32[]{:S(2)}) collective-permute-start(bf16[64,1024]{1,0:T(8,128)(2,1)S(1)} %convolution_convert_fusion.7), channel_id=1, source_target_pairs={{0,240},{16,0},{32,16},{48,32},{64,48},{80,64},{96,80},{112,96},{1... | collective-permute-start | bytes 393224 | tf_op jit(solution)/shard_map/ppermute | solution.py:19
  74.2 6.1 %collective-permute-start.5 = (bf16[64,1024]{1,0:T(8,128)(2,1)S(1)}, bf16[64,1024]{1,0:T(8,128)(2,1)S(1)}, u32[]{:S(2)}, u32[]{:S(2)}) collective-permute-start(bf16[64,1024]{1,0:T(8,128)(2,1)S(1)} %add_convert_fusion.2), channel_id=1, source_target_pairs={{16,0},{32,16},{48,32},{64,48},{80,64},{96,80},{112,96},{128,112},... | collective-permute-start | bytes 393224 | tf_op jit(solution)/shard_map/ppermute | solution.py:19
  92.0 6.3 %collective-permute-start.11 = (bf16[8,64,128]{2,1,0:T(8,128)(2,1)S(1)}, bf16[8,64,128]{2,1,0:T(8,128)(2,1)S(1)}, u32[]{:S(2)}, u32[]{:S(2)}) collective-permute-start(bf16[8,64,128]{2,1,0:T(8,128)(2,1)S(1)} %all_to_all.25), channel_id=1, source_target_pairs={{0,8},{8,0},{1,9},{9,1},{2,10},{10,2},{3,11},{11,3},{4,12},{12,4},... | collective-permute-start | bytes 393224 | tf_op jit(solution)/shard_map/ppermute | solution.py:23
  99.0 8.1 %collective-permute-start.12 = (bf16[64,1024]{1,0:T(8,128)(2,1)S(1)}, bf16[64,1024]{1,0:T(8,128)(2,1)S(1)}, u32[]{:S(2)}, u32[]{:S(2)}) collective-permute-start(bf16[64,1024]{1,0:T(8,128)(2,1)S(1)} %add_convert_fusion.1), channel_id=1, source_target_pairs={{32,0},{48,16},{64,32},{80,48},{96,64},{112,80},{128,96},{144,112}... | collective-permute-start | bytes 393224 | tf_op jit(solution)/shard_map/ppermute | solution.py:19
  107.1 17.9 %copy-start.3 = (bf16[1024,1024]{1,0:T(8,128)(2,1)S(1)}, bf16[1024,1024]{1,0:T(8,128)(2,1)}, u32[]{:S(2)}) copy-start(bf16[1024,1024]{1,0:T(8,128)(2,1)} %all-gather.3.cloned.1.call-done) | copy-start | bytes 6291460
  122.0 3.0 %collective-permute-start.13 = (bf16[8,64,128]{2,1,0:T(8,128)(2,1)S(1)}, bf16[8,64,128]{2,1,0:T(8,128)(2,1)S(1)}, u32[]{:S(2)}, u32[]{:S(2)}) collective-permute-start(bf16[8,64,128]{2,1,0:T(8,128)(2,1)S(1)} %all_to_all.26), channel_id=1, source_target_pairs={{0,8},{8,0},{1,9},{9,1},{2,10},{10,2},{3,11},{11,3},{4,12},{12,4},... | collective-permute-start | bytes 393224 | tf_op jit(solution)/shard_map/ppermute | solution.py:23
  125.7 28.3 %collective-permute-start.17 = (bf16[64,1024]{1,0:T(8,128)(2,1)S(1)}, bf16[64,1024]{1,0:T(8,128)(2,1)S(1)}, u32[]{:S(2)}, u32[]{:S(2)}) collective-permute-start(bf16[64,1024]{1,0:T(8,128)(2,1)S(1)} %fusion.43), channel_id=1, source_target_pairs={{0,240},{16,0},{32,16},{48,32},{64,48},{80,64},{96,80},{112,96},{1... | collective-permute-start | bytes 393224 | tf_op jit(solution)/shard_map/ppermute | solution.py:19
  127.3 12.7 %collective-permute-start.16 = (bf16[64,1024]{1,0:T(8,128)(2,1)S(1)}, bf16[64,1024]{1,0:T(8,128)(2,1)S(1)}, u32[]{:S(2)}, u32[]{:S(2)}) collective-permute-start(bf16[64,1024]{1,0:T(8,128)(2,1)S(1)} %fusion.43), channel_id=1, source_target_pairs={{192,240},{208,0},{224,16},{240,32},{193,241},{209,1},{225,17},{24... | collective-permute-start | bytes 393224 | tf_op jit(solution)/shard_map/ppermute | solution.py:19
  128.6 11.9 %collective-permute-start.15 = (bf16[64,1024]{1,0:T(8,128)(2,1)S(1)}, bf16[64,1024]{1,0:T(8,128)(2,1)S(1)}, u32[]{:S(2)}, u32[]{:S(2)}) collective-permute-start(bf16[64,1024]{1,0:T(8,128)(2,1)S(1)} %fusion.43), channel_id=1, source_target_pairs={{128,240},{144,0},{160,16},{176,32},{192,48},{208,64},{224,80},{24... | collective-permute-start | bytes 393224 | tf_op jit(solution)/shard_map/ppermute | solution.py:19
  129.9 11.5 %collective-permute-start.14 = (bf16[64,1024]{1,0:T(8,128)(2,1)S(1)}, bf16[64,1024]{1,0:T(8,128)(2,1)S(1)}, u32[]{:S(2)}, u32[]{:S(2)}) collective-permute-start(bf16[64,1024]{1,0:T(8,128)(2,1)S(1)} %fusion.43), channel_id=1, source_target_pairs={{64,240},{80,0},{96,16},{112,32},{128,48},{144,64},{160,80},{176,9... | collective-permute-start | bytes 393224 | tf_op jit(solution)/shard_map/ppermute | solution.py:19
  140.0 1.4 copy-start.6
  140.0 2.0 copy-start.4
  143.5 19.2 %all-to-all-start.3 = ((bf16[8,192,128]{2,1,0:T(8,128)(2,1)}), bf16[8,192,128]{2,1,0:T(8,128)(2,1)S(1)}, u32[]{:S(2)}, u32[]{:S(2)}) async-start(bf16[8,192,128]{2,1,0:T(8,128)(2,1)} %bitcast_bitcast_fusion.2), calls=%async_computation.3 | async-start | bytes 786432 | tf_op jit(solution)/shard_map/all_to_all | solution.py:31
  147.5 4.1 %copy-start.7 = (bf16[1024,1024]{1,0:T(8,128)(2,1)S(1)}, bf16[1024,1024]{1,0:T(8,128)(2,1)}, u32[]{:S(2)}) copy-start(bf16[1024,1024]{1,0:T(8,128)(2,1)} %copy-done.6) | copy-start | bytes 6291460
  151.6 2.4 %copy-start.9 = (bf16[1024,1024]{1,0:T(8,128)(2,1)}, bf16[1024,1024]{1,0:T(8,128)(2,1)S(1)}, u32[]{:S(2)}) copy-start(bf16[1024,1024]{1,0:T(8,128)(2,1)S(1)} %convolution_convert_fusion.1) | copy-start | bytes 6291460
  162.7 1.8 collective-permute-start.18
  163.2 1.6 copy-start.10
  165.4 1.6 copy-start.5
  167.6 3.7 %copy-start.1 = (bf16[1024,1024]{1,0:T(8,128)(2,1)S(1)}, bf16[1024,1024]{1,0:T(8,128)(2,1)}, u32[]{:S(2)}) copy-start(bf16[1024,1024]{1,0:T(8,128)(2,1)} %copy-done) | copy-start | bytes 6291460
  167.7 1.4 collective-permute-start.19
  169.1 2.8 %copy-start.2 = (bf16[2,1024,1024]{2,1,0:T(8,128)(2,1)S(1)}, bf16[2,1024,1024]{2,1,0:T(8,128)(2,1)}, u32[]{:S(2)}) copy-start(bf16[2,1024,1024]{2,1,0:T(8,128)(2,1)} %k_ref.3) | copy-start | bytes 12582916
  173.8 21.4 %all-to-all-start.4 = ((bf16[8,256,128]{2,1,0:T(8,128)(2,1)}), bf16[8,256,128]{2,1,0:T(8,128)(2,1)S(1)}, u32[]{:S(2)}, u32[]{:S(2)}) async-start(bf16[8,256,128]{2,1,0:T(8,128)(2,1)} %bitcast_bitcast_fusion), calls=%async_computation.4 | async-start | bytes 1048576 | tf_op jit(solution)/shard_map/all_to_all | solution.py:31
  177.3 8.1 %collective-permute-start.20 = (bf16[64,1024]{1,0:T(8,128)(2,1)S(1)}, bf16[64,1024]{1,0:T(8,128)(2,1)S(1)}, u32[]{:S(2)}, u32[]{:S(2)}) collective-permute-start(bf16[64,1024]{1,0:T(8,128)(2,1)S(1)} %get-tuple-element.48), channel_id=1, source_target_pairs={{0,16},{16,32},{32,48},{48,64},{64,80},{80,96},{96,112},{112,128},... | collective-permute-start | bytes 393224 | tf_op jit(solution)/shard_map/ppermute | solution.py:19
  185.4 2.2 %collective-permute-start.21 = (bf16[64,1024]{1,0:T(8,128)(2,1)S(1)}, bf16[64,1024]{1,0:T(8,128)(2,1)S(1)}, u32[]{:S(2)}, u32[]{:S(2)}) collective-permute-start(bf16[64,1024]{1,0:T(8,128)(2,1)S(1)} %collective-permute-done.20), channel_id=1, source_target_pairs={{0,8},{8,0},{1,9},{9,1},{2,10},{10,2},{3,11},{11,3},{4,12},{12,4},... | collective-permute-start | bytes 393224 | tf_op jit(solution)/shard_map/ppermute | solution.py:23
  195.3 0.8 copy-start.11
Sparse Core Ops, SparseCore 0:
  48.9 38.1 all-gather.2
  88.9 47.2 all-gather.4
